TPU v7x, 32 devices: a whole 2x2x4 slice. The times are simulated.
32 devices in a mesh: dp: 8 (over y, x, core), head: 4 (over z).
Axes of the slice: x: 2, y: 2, z: 4, core: 2. Of those that a mesh axis runs over, the one named last changes fastest.
Arguments:
- block_input: bfloat16 [2, 4096, 2048], P(None, 'dp', 'head'), may hold values from -6 to 6
- cotangent: bfloat16 [2, 4096, 2048], P(None, 'dp'), may hold values from -6 to 6
- seq_count: int32 [2, 8], P(None, 'dp'), may hold values from 1 to 2, as said below
- attn_gain: bfloat16 [2048], P('head'), may hold values from 0.5 to 1.5
- w_query: bfloat16 [2048, 2048], P(None, 'head'), may hold values from -0.125 to 0.125
- w_key: bfloat16 [2048, 2048], P(None, 'head'), may hold values from -0.125 to 0.125
- w_value: bfloat16 [2048, 2048], P(None, 'head'), may hold values from -0.125 to 0.125
- w_gate: bfloat16 [2048, 2048], P(None, 'head'), may hold values from -0.125 to 0.125
- w_alpha: bfloat16 [2048, 16], P(None, 'head'), may hold values from -0.125 to 0.125
- w_beta: bfloat16 [2048, 16], P(None, 'head'), may hold values from -0.125 to 0.125
- conv_weight: float32 [3, 4, 2048], P(None, None, 'head'), may hold values from -3 to 3
- decay_base: float32 [16], P('head'), may hold values from 0 to 2.5
- decay_bias: float32 [16], P('head'), may hold values from -5 to -2
- norm_gain: float32 [128], replicated, may hold values from 0.5 to 1.5
- w_out: bfloat16 [2048, 2048], P('head'), may hold values from -0.125 to 0.125
- mlp_gain: bfloat16 [2048], P('head'), may hold values from 0.5 to 1.5
- w_mlp_gate: bfloat16 [2048, 5632], P(None, 'head'), may hold values from -0.125 to 0.125
- w_mlp_up: bfloat16 [2048, 5632], P(None, 'head'), may hold values from -0.125 to 0.125
- w_down: bfloat16 [5632, 2048], P('head'), may hold values from -0.078125 to 0.078125
Outputs:
- output: bfloat16 [2, 4096, 2048], P(None, 'dp', 'head')
- grad_input: float32 [2, 4096, 2048], P(None, 'dp', 'head')
- grad_attn_gain: float32 [2048], P('head')
- grad_w_query: float32 [2048, 2048], P('dp', 'head')
- grad_w_key: float32 [2048, 2048], P('dp', 'head')
- grad_w_value: float32 [2048, 2048], P('dp', 'head')
- grad_w_gate: float32 [2048, 2048], P('dp', 'head')
- grad_w_alpha: float32 [2048, 16], P('dp', 'head')
- grad_w_beta: float32 [2048, 16], P('dp', 'head')
- grad_conv_weight: float32 [3, 4, 2048], P(None, None, 'head')
- grad_decay_base: float32 [16], P('head')
- grad_decay_bias: float32 [16], P('head')
- grad_norm_gain: float32 [128], replicated
- grad_w_out: float32 [2048, 2048], P('head', 'dp')
- grad_mlp_gain: float32 [2048], P('head')
- grad_w_mlp_gate: float32 [2048, 5632], P('dp', 'head')
- grad_w_mlp_up: float32 [2048, 5632], P('dp', 'head')
- grad_w_down: float32 [5632, 2048], P('head', 'dp')
Inputs may be any that keep to these rules, and one draw needn't show every extreme that they name: seq_count[m, g] counts the sequences that fill the first slots of data group g in micro-batch m; the rows of the other slots are ignored. In every micro-batch some group has 2.
All inputs are finite; a program needn't handle non-finite values.
Results may differ from a plain program's by a relative error of at most 0.014.
Values may be sent and summed in bfloat16 or wider, within the bound.
No kernel may reach another device: no remote copies, remote signals or barrier semaphores. Data moves between devices by JAX's collectives and lax.ppermute only.
A program may use at most 320 MiB of HBM per device.

v0:
```python
import jax
import jax.numpy as jnp
from jax import lax
from jax.sharding import PartitionSpec as P

SPAN = 64
SEQ = 256
SLOTS = 2


epsilon = 1e-06
highest_precision = lax.Precision.HIGHEST


def matmul(former, latter):
    return jnp.dot(former, latter, preferred_element_type=jnp.float32)


def matmul_rows(former, latter):
    return lax.dot_general(
        former, latter, (((0,), (0,)), ((), ())), preferred_element_type=jnp.float32
    )


def matmul_back(former, latter):
    return lax.dot_general(
        former, latter, (((1,), (1,)), ((), ())), preferred_element_type=jnp.float32
    )


def own_columns(values, own_start, shard_width):
    return lax.dynamic_slice_in_dim(values, own_start, shard_width, axis=values.ndim - 1)


def short_conv(values, weights):
    tap_count = weights.shape[0]
    length = values.shape[0]
    padded = jnp.pad(values, ((tap_count - 1, 0), (0, 0)))
    summed = jnp.zeros_like(values)
    for offset in range(tap_count):
        summed = summed + padded[offset : offset + length] * weights[offset]
    return jax.nn.silu(summed)


def unit_rows(values, factor):
    return values * lax.rsqrt(jnp.sum(values * values, -1, keepdims=True) + epsilon) * factor


def triangular(system, target):
    return jax.scipy.linalg.solve_triangular(system, target, lower=True, unit_diagonal=True)


def spanned_delta(queries, key_rows, value_rows, decay_log, strength):
    length, head_count, head_width = queries.shape
    blocks = length // SPAN

    def to_blocks(values):
        return jnp.swapaxes(values.reshape((blocks, SPAN, head_count) + values.shape[2:]), 1, 2)

    positions = jnp.arange(SPAN)
    strict_lower = positions[:, None] > positions[None, :]
    within = positions[:, None] >= positions[None, :]
    identity = jnp.eye(SPAN, dtype=jnp.float32)

    def block_step(memory_state, block_inputs):
        query_block_rows, key_block_rows, block_value, block_decay, block_strength = block_inputs
        cumulative = jnp.cumsum(block_decay, axis=-1)
        spread = cumulative[:, :, None] - cumulative[:, None, :]
        falloff = jnp.where(within, jnp.exp(jnp.where(within, spread, 0.0)), 0.0)
        similar = jnp.einsum(
            "hck,hdk->hcd", key_block_rows, key_block_rows, precision=highest_precision
        )
        system = identity + jnp.where(
            strict_lower, block_strength[:, :, None] * falloff * similar, 0.0
        )
        start_decay = jnp.exp(cumulative)
        carried_state = jnp.einsum(
            "fgr,frp->fgp", key_block_rows, memory_state, precision=highest_precision
        )
        target = block_strength[:, :, None] * (
            block_value - start_decay[:, :, None] * carried_state
        )
        state_updates = jax.vmap(triangular)(system, target)
        scores = jnp.einsum(
            "hck,hdk->hcd", query_block_rows, key_block_rows, precision=highest_precision
        )
        outputs = start_decay[:, :, None] * jnp.einsum(
            "fgr,frp->fgp", query_block_rows, memory_state, precision=highest_precision
        )
        outputs = outputs + jnp.einsum(
            "hcd,hdv->hcv", falloff * scores, state_updates, precision=highest_precision
        )
        trailing_decay = jnp.exp(cumulative[:, -1:] - cumulative)
        memory_state = jnp.exp(cumulative[:, -1])[:, None, None] * memory_state + jnp.einsum(
            "qgo,qgs->qos",
            key_block_rows,
            trailing_decay[:, :, None] * state_updates,
            precision=highest_precision,
        )
        return (memory_state, outputs)

    memory_state = jnp.zeros((head_count, head_width, head_width), jnp.float32)
    block_inputs = (
        to_blocks(queries),
        to_blocks(key_rows),
        to_blocks(value_rows),
        to_blocks(decay_log),
        to_blocks(strength),
    )
    memory_state, outputs = lax.scan(block_step, memory_state, block_inputs)
    return jnp.swapaxes(outputs, 1, 2).reshape(length, head_count, head_width)


def mixer_slot(
    query_pre,
    key_pre,
    value_pre,
    gate_pre,
    alpha_pre,
    beta_pre,
    conv_weight,
    decay_base,
    decay_bias,
    norm_gain,
):
    length, head_count = alpha_pre.shape
    head_width = query_pre.shape[1] // head_count
    shaped = (length, head_count, head_width)
    queries = unit_rows(short_conv(query_pre, conv_weight[0]).reshape(shaped), head_width ** (-0.5))
    key_rows = unit_rows(short_conv(key_pre, conv_weight[1]).reshape(shaped), 1.0)
    value_rows = short_conv(value_pre, conv_weight[2]).reshape(shaped)
    decay_log = -jnp.exp(decay_base) * jax.nn.softplus(alpha_pre + decay_bias)
    strength = jax.nn.sigmoid(beta_pre)
    delta_out = spanned_delta(queries, key_rows, value_rows, decay_log, strength)
    normed = (
        delta_out
        * lax.rsqrt(jnp.mean(delta_out * delta_out, -1, keepdims=True) + epsilon)
        * norm_gain
    )
    return (normed * jax.nn.silu(gate_pre.reshape(shaped))).reshape(length, head_count * head_width)


def mixer_rows(
    query_pre,
    key_pre,
    value_pre,
    gate_pre,
    alpha_pre,
    beta_pre,
    conv_weight,
    decay_base,
    decay_bias,
    norm_gain,
):

    def slotted(values):
        return values.reshape((SLOTS, values.shape[0] // SLOTS) + values.shape[1:])

    result = jax.vmap(mixer_slot, in_axes=(0, 0, 0, 0, 0, 0, None, None, None, None))(
        slotted(query_pre),
        slotted(key_pre),
        slotted(value_pre),
        slotted(gate_pre),
        slotted(alpha_pre),
        slotted(beta_pre),
        conv_weight,
        decay_base,
        decay_bias,
        norm_gain,
    )
    return result.reshape(query_pre.shape[0], result.shape[-1])


def body(
    block_input,
    cotangent,
    seq_count,
    attn_gain,
    w_query,
    w_key,
    w_value,
    w_gate,
    w_alpha,
    w_beta,
    conv_weight,
    decay_base,
    decay_bias,
    norm_gain,
    w_out,
    mlp_gain,
    w_mlp_gate,
    w_mlp_up,
    w_down,
):
    micro_count, row_count, shard_width = block_input.shape
    own_start = lax.axis_index("head") * shard_width
    gathered, attn_full, mlp_full = (
        lax.all_gather(block_input, "head", axis=2, tiled=True),
        lax.all_gather(attn_gain, "head", axis=0, tiled=True),
        lax.all_gather(mlp_gain, "head", axis=0, tiled=True),
    )
    attn_scale = attn_full.astype(jnp.float32)
    mlp_scale = mlp_full.astype(jnp.float32)
    feature_count = gathered.shape[2]
    attn_own = own_columns(attn_scale, own_start, shard_width)
    in_weights = (w_query, w_key, w_value, w_gate, w_alpha, w_beta)
    small_params = (conv_weight, decay_base, decay_bias, norm_gain)

    def micro_step(carry, slices):
        (
            in_grads,
            out_grad,
            mlp_gate_grad,
            mlp_up_grad,
            down_grad,
            small_grads,
            attn_gain_grad,
            mlp_gain_grad,
        ) = carry
        gathered_now, cotangent_now, live_count = slices
        live_rows = (jnp.arange(row_count) // SEQ < live_count)[:, None]
        inputs = jnp.where(live_rows, gathered_now.astype(jnp.float32), 0.0)
        inputs_own = own_columns(inputs, own_start, shard_width)
        scale_in = lax.rsqrt(jnp.mean(inputs * inputs, -1, keepdims=True) + epsilon)
        normed = (inputs * scale_in * attn_scale).astype(jnp.bfloat16)
        pre_acts = tuple((matmul(normed, weight) for weight in in_weights))
        mixed_float, mixer_pullback = jax.vjp(mixer_rows, *pre_acts + small_params)
        mixed = mixed_float.astype(jnp.bfloat16)
        partial_attn = matmul(mixed, w_out)
        hidden = inputs + lax.psum(partial_attn, "head")
        scale_mid = lax.rsqrt(jnp.mean(hidden * hidden, -1, keepdims=True) + epsilon)
        normed_mid = (hidden * scale_mid * mlp_scale).astype(jnp.bfloat16)
        hidden_own = own_columns(hidden, own_start, shard_width)
        gate_act = matmul(normed_mid, w_mlp_gate)
        up_act = matmul(normed_mid, w_mlp_up)
        sigmoid_gate = jax.nn.sigmoid(gate_act)
        silu_gate = gate_act * sigmoid_gate
        product = (silu_gate * up_act).astype(jnp.bfloat16)
        output_own = hidden_own + lax.psum_scatter(
            matmul(product, w_down).astype(jnp.bfloat16), "head", scatter_dimension=1, tiled=True
        ).astype(jnp.float32)
        grad_output = jnp.where(live_rows, cotangent_now, jnp.zeros((), jnp.bfloat16))
        grad_output_float = grad_output.astype(jnp.float32)
        down_grad = down_grad + matmul_rows(product, grad_output)
        grad_product = matmul_back(grad_output, w_down)
        grad_gate = (
            grad_product * up_act * sigmoid_gate * (1.0 + gate_act * (1.0 - sigmoid_gate))
        ).astype(jnp.bfloat16)
        grad_up = (grad_product * silu_gate).astype(jnp.bfloat16)
        mlp_gate_grad = mlp_gate_grad + matmul_rows(normed_mid, grad_gate)
        mlp_up_grad = mlp_up_grad + matmul_rows(normed_mid, grad_up)
        partial_mid = matmul_back(grad_gate, w_mlp_gate) + matmul_back(grad_up, w_mlp_up)
        grad_mid = lax.psum(partial_mid, "head")
        dot_mid = jnp.sum(grad_mid * mlp_scale * hidden, -1, keepdims=True)
        grad_hidden = (
            grad_output_float
            + scale_mid * mlp_scale * grad_mid
            - hidden * scale_mid**3 * dot_mid / feature_count
        )
        mlp_gain_grad = mlp_gain_grad + own_columns(
            jnp.sum(grad_mid * hidden * scale_mid, 0), own_start, shard_width
        )
        grad_hidden_own = own_columns(grad_hidden, own_start, shard_width)
        grad_hidden_low = grad_hidden.astype(jnp.bfloat16)
        out_grad = out_grad + matmul_rows(mixed, grad_hidden_low)
        grad_mixed = matmul_back(grad_hidden_low, w_out)
        pulled = mixer_pullback(grad_mixed)
        grad_pre = tuple((pulled[index].astype(jnp.bfloat16) for index in range(6)))
        partial_in = jnp.zeros(inputs.shape, jnp.float32)
        new_in_grads = []
        for index in range(6):
            new_in_grads.append(in_grads[index] + matmul_rows(normed, grad_pre[index]))
            partial_in = partial_in + matmul_back(grad_pre[index], in_weights[index])
        grad_in_own = lax.psum_scatter(
            partial_in.astype(jnp.bfloat16), "head", scatter_dimension=1, tiled=True
        ).astype(jnp.float32)
        dot_in, norm_gain_step = lax.psum(
            (jnp.sum(grad_in_own * attn_own * inputs_own, -1, keepdims=True), pulled[9]), "head"
        )
        grad_input_own = (
            grad_hidden_own
            + scale_in * attn_own * grad_in_own
            - inputs_own * scale_in**3 * dot_in / feature_count
        )
        attn_gain_grad = attn_gain_grad + jnp.sum(grad_in_own * inputs_own * scale_in, 0)
        small_grads = (
            small_grads[0] + pulled[6],
            small_grads[1] + pulled[7],
            small_grads[2] + pulled[8],
            small_grads[3] + norm_gain_step,
        )
        carry = (
            tuple(new_in_grads),
            out_grad,
            mlp_gate_grad,
            mlp_up_grad,
            down_grad,
            small_grads,
            attn_gain_grad,
            mlp_gain_grad,
        )
        return (carry, (output_own.astype(jnp.bfloat16), grad_input_own))

    start = (
        tuple((jnp.zeros(weight.shape, jnp.float32) for weight in in_weights)),
        jnp.zeros(w_out.shape, jnp.float32),
        jnp.zeros(w_mlp_gate.shape, jnp.float32),
        jnp.zeros(w_mlp_up.shape, jnp.float32),
        jnp.zeros(w_down.shape, jnp.float32),
        tuple((jnp.zeros(param.shape, jnp.float32) for param in small_params)),
        jnp.zeros((shard_width,), jnp.float32),
        jnp.zeros((shard_width,), jnp.float32),
    )
    final, (results, input_grads) = lax.scan(
        micro_step, start, (gathered, cotangent, seq_count[:, 0])
    )
    (
        in_grads,
        out_grad,
        mlp_gate_grad,
        mlp_up_grad,
        down_grad,
        small_grads,
        attn_gain_grad,
        mlp_gain_grad,
    ) = final
    summed = (
        lax.psum_scatter(
            in_grads[0].astype(jnp.bfloat16), "dp", scatter_dimension=0, tiled=True
        ).astype(jnp.float32),
        lax.psum_scatter(
            in_grads[1].astype(jnp.bfloat16), "dp", scatter_dimension=0, tiled=True
        ).astype(jnp.float32),
        lax.psum_scatter(
            in_grads[2].astype(jnp.bfloat16), "dp", scatter_dimension=0, tiled=True
        ).astype(jnp.float32),
        lax.psum_scatter(
            in_grads[3].astype(jnp.bfloat16), "dp", scatter_dimension=0, tiled=True
        ).astype(jnp.float32),
        lax.psum_scatter(
            in_grads[4].astype(jnp.bfloat16), "dp", scatter_dimension=0, tiled=True
        ).astype(jnp.float32),
        lax.psum_scatter(
            in_grads[5].astype(jnp.bfloat16), "dp", scatter_dimension=0, tiled=True
        ).astype(jnp.float32),
        lax.psum_scatter(
            out_grad.astype(jnp.bfloat16), "dp", scatter_dimension=1, tiled=True
        ).astype(jnp.float32),
        lax.psum_scatter(
            mlp_gate_grad.astype(jnp.bfloat16), "dp", scatter_dimension=0, tiled=True
        ).astype(jnp.float32),
        lax.psum_scatter(
            mlp_up_grad.astype(jnp.bfloat16), "dp", scatter_dimension=0, tiled=True
        ).astype(jnp.float32),
        lax.psum_scatter(
            down_grad.astype(jnp.bfloat16), "dp", scatter_dimension=1, tiled=True
        ).astype(jnp.float32),
    )
    small_summed = lax.psum(
        (
            attn_gain_grad,
            small_grads[0],
            small_grads[1],
            small_grads[2],
            small_grads[3],
            mlp_gain_grad,
        ),
        "dp",
    )
    return (
        results,
        input_grads,
        small_summed[0],
        summed[0],
        summed[1],
        summed[2],
        summed[3],
        summed[4],
        summed[5],
        small_summed[1],
        small_summed[2],
        small_summed[3],
        small_summed[4],
        summed[6],
        small_summed[5],
        summed[7],
        summed[8],
        summed[9],
    )


def solution(mesh):
    return jax.shard_map(
        body,
        mesh=mesh,
        in_specs=(
            P(None, "dp", "head"),
            P(None, "dp", None),
            P(None, "dp"),
            P("head"),
            P(None, "head"),
            P(None, "head"),
            P(None, "head"),
            P(None, "head"),
            P(None, "head"),
            P(None, "head"),
            P(None, None, "head"),
            P("head"),
            P("head"),
            P(),
            P("head", None),
            P("head"),
            P(None, "head"),
            P(None, "head"),
            P("head", None),
        ),
        out_specs=(
            P(None, "dp", "head"),
            P(None, "dp", "head"),
            P("head"),
            P("dp", "head"),
            P("dp", "head"),
            P("dp", "head"),
            P("dp", "head"),
            P("dp", "head"),
            P("dp", "head"),
            P(None, None, "head"),
            P("head"),
            P("head"),
            P(),
            P("head", "dp"),
            P("head"),
            P("dp", "head"),
            P("dp", "head"),
            P("head", "dp"),
        ),
        check_vma=False,
    )
```

profile of v0, /device:TPU:0, one launch (start us, length us, event | category | flops | bytes accessed | tf_op | source)
XLA Modules:
  0.0 2848.6 jit_solution(801475719771899789)
XLA Ops:
  9.5 13.5 all-gather.1
  23.1 12.3 all-gather
  41.8 51.5 %all-gather.4.cloned.1.call-done = bf16[2,512,2048]{2,1,0:T(8,128)(2,1)} async-done(((bf16[2,512,512]{2,1,0:T(8,128)(2,1)}), bf16[2,512,2048]{2,1,0:T(8,128)(2,1)}) %all-gather.4.cloned.1.call-update) | async-done | bytes 4194320 | tf_op jit(solution)/shard_map/all_gather | solution.py:198
  93.3 2260.7 %while.215 = (s32[]{:T(128)}, f32[2048,512]{1,0:T(8,128)}, f32[2048,512]{1,0:T(8,128)}, f32[2048,512]{1,0:T(8,128)}, f32[2048,512]{1,0:T(8,128)}, /*index=5*/f32...) while((s32[]{:T(128)}, f32[2048,512]{1,0:T(8,128)}, ...), condition=%wide.region_49.50_spmd.clone, body=%wide.region_0.49_spmd.clone.sunk | while | flops 44420390912 | bytes 1137291136 | solution.py:314
  156.8 224.8 %while.216 = (s32[]{:T(128)}, f32[2,4,128,128]{3,2,1,0:T(8,128)S(1)}, f32[4,2,4,64,128]{4,3,2,1,0:T(8,128)}, f32[4,2,4,64,64]{4,3,2,1,0:T(8,128)}, f32[4,2,4,64,...) while((s32[]{:T(128)}, ...), condition=%wide.region_6.6_spmd.clone.clone, body=%wide.region_4.5_spmd.clone.clone.sunk | while | flops 505566272 | bytes 11923100 | solution.py:110
  162.2 39.3 %custom-call.92 = f32[2,4,1,64,64]{3,4,2,1,0:T(8,128)S(1)} custom-call(f32[2,4,1,64,64]{4,3,2,1,0:T(8,128)S(1)} %add_bitcast_fusion.11), custom_call_target="InvertDiagBlocksLowerTriangular" | custom-call | tf_op jit(solution)/shard_map/while/body/eval_jaxpr/jvp(vmap())/while/body/eval_jaxpr/vmap(jit(_solve_triangular))/triangular_solve | solution.py:50
  218.1 39.3 %custom-call.92 = f32[2,4,1,64,64]{3,4,2,1,0:T(8,128)S(1)} custom-call(f32[2,4,1,64,64]{4,3,2,1,0:T(8,128)S(1)} %add_bitcast_fusion.11), custom_call_target="InvertDiagBlocksLowerTriangular" | custom-call | tf_op jit(solution)/shard_map/while/body/eval_jaxpr/jvp(vmap())/while/body/eval_jaxpr/vmap(jit(_solve_triangular))/triangular_solve | solution.py:50
  274.2 39.3 %custom-call.92 = f32[2,4,1,64,64]{3,4,2,1,0:T(8,128)S(1)} custom-call(f32[2,4,1,64,64]{4,3,2,1,0:T(8,128)S(1)} %add_bitcast_fusion.11), custom_call_target="InvertDiagBlocksLowerTriangular" | custom-call | tf_op jit(solution)/shard_map/while/body/eval_jaxpr/jvp(vmap())/while/body/eval_jaxpr/vmap(jit(_solve_triangular))/triangular_solve | solution.py:50
  330.2 39.3 %custom-call.92 = f32[2,4,1,64,64]{3,4,2,1,0:T(8,128)S(1)} custom-call(f32[2,4,1,64,64]{4,3,2,1,0:T(8,128)S(1)} %add_bitcast_fusion.11), custom_call_target="InvertDiagBlocksLowerTriangular" | custom-call | tf_op jit(solution)/shard_map/while/body/eval_jaxpr/jvp(vmap())/while/body/eval_jaxpr/vmap(jit(_solve_triangular))/triangular_solve | solution.py:50
  399.9 9.2 fusion.529
  409.1 142.1 %all-reduce.39.cloned.1.call-done = f32[512,2048]{1,0:T(8,128)} async-done(((f32[512,2048]{1,0:T(8,128)}), f32[512,2048]{1,0:T(8,128)}) %all-reduce.39.cloned.1.call-update) | async-done | bytes 4194320 | tf_op jit(solution)/shard_map/while/body/eval_jaxpr/psum | solution.py:230
  555.4 8.2 fusion.528
  585.1 9.2 select_add_fusion.30
  606.9 124.0 %all-reduce.41.cloned.1.call-done = f32[512,2048]{1,0:T(8,128)} async-done(((f32[512,2048]{1,0:T(8,128)}), f32[512,2048]{1,0:T(8,128)}) %all-reduce.41.cloned.1.call-update) | async-done | bytes 4194320 | tf_op jit(solution)/shard_map/while/body/eval_jaxpr/psum | solution.py:253
  756.5 352.7 %while.217 = (s32[]{:T(128)}, f32[2,4,128,128]{3,2,1,0:T(8,128)S(1)}, f32[4,2,4,64,128]{4,3,2,1,0:T(8,128)}, f32[4,2,4,64,128]{4,3,2,1,0:T(8,128)}, f32[4,2,4,64...) while((s32[]{:T(128)}, ...), condition=%wide.region_24.24_spmd.clone.clone, body=%wide.region_13.23_spmd.clone.clone.sunk | while | flops 1035385408 | bytes 20528352 | solution.py:110
  764.9 40.0 %custom-call.93 = f32[2,4,1,64,64]{3,4,2,1,0:T(8,128)} custom-call(f32[2,4,1,64,64]{4,3,2,1,0:T(8,128)S(1)} %add_bitcast_fusion.12), custom_call_target="InvertDiagBlocksLowerTriangular" | custom-call | tf_op jit(solution)/shard_map/while/body/eval_jaxpr/transpose(jvp(vmap()))/while/body/eval_jaxpr/vmap(jit(_solve_triangular))/triangular_solve | solution.py:50
  853.0 40.0 %custom-call.93 = f32[2,4,1,64,64]{3,4,2,1,0:T(8,128)} custom-call(f32[2,4,1,64,64]{4,3,2,1,0:T(8,128)S(1)} %add_bitcast_fusion.12), custom_call_target="InvertDiagBlocksLowerTriangular" | custom-call | tf_op jit(solution)/shard_map/while/body/eval_jaxpr/transpose(jvp(vmap()))/while/body/eval_jaxpr/vmap(jit(_solve_triangular))/triangular_solve | solution.py:50
  941.1 40.0 %custom-call.93 = f32[2,4,1,64,64]{3,4,2,1,0:T(8,128)} custom-call(f32[2,4,1,64,64]{4,3,2,1,0:T(8,128)S(1)} %add_bitcast_fusion.12), custom_call_target="InvertDiagBlocksLowerTriangular" | custom-call | tf_op jit(solution)/shard_map/while/body/eval_jaxpr/transpose(jvp(vmap()))/while/body/eval_jaxpr/vmap(jit(_solve_triangular))/triangular_solve | solution.py:50
  1029.2 40.0 %custom-call.93 = f32[2,4,1,64,64]{3,4,2,1,0:T(8,128)} custom-call(f32[2,4,1,64,64]{4,3,2,1,0:T(8,128)S(1)} %add_bitcast_fusion.12), custom_call_target="InvertDiagBlocksLowerTriangular" | custom-call | tf_op jit(solution)/shard_map/while/body/eval_jaxpr/transpose(jvp(vmap()))/while/body/eval_jaxpr/vmap(jit(_solve_triangular))/triangular_solve | solution.py:50
  1184.7 21.6 reduce-scatter.37.cloned.1.call-done
  1208.2 9.8 all-reduce.35
  1285.1 224.6 %while.216 = (s32[]{:T(128)}, f32[2,4,128,128]{3,2,1,0:T(8,128)S(1)}, f32[4,2,4,64,128]{4,3,2,1,0:T(8,128)}, f32[4,2,4,64,64]{4,3,2,1,0:T(8,128)}, f32[4,2,4,64,...) while((s32[]{:T(128)}, ...), condition=%wide.region_6.6_spmd.clone.clone, body=%wide.region_4.5_spmd.clone.clone.sunk | while | flops 505566272 | bytes 11923100 | solution.py:110
  1290.4 39.3 %custom-call.92 = f32[2,4,1,64,64]{3,4,2,1,0:T(8,128)S(1)} custom-call(f32[2,4,1,64,64]{4,3,2,1,0:T(8,128)S(1)} %add_bitcast_fusion.11), custom_call_target="InvertDiagBlocksLowerTriangular" | custom-call | tf_op jit(solution)/shard_map/while/body/eval_jaxpr/jvp(vmap())/while/body/eval_jaxpr/vmap(jit(_solve_triangular))/triangular_solve | solution.py:50
  1346.3 39.3 %custom-call.92 = f32[2,4,1,64,64]{3,4,2,1,0:T(8,128)S(1)} custom-call(f32[2,4,1,64,64]{4,3,2,1,0:T(8,128)S(1)} %add_bitcast_fusion.11), custom_call_target="InvertDiagBlocksLowerTriangular" | custom-call | tf_op jit(solution)/shard_map/while/body/eval_jaxpr/jvp(vmap())/while/body/eval_jaxpr/vmap(jit(_solve_triangular))/triangular_solve | solution.py:50
  1402.4 39.3 %custom-call.92 = f32[2,4,1,64,64]{3,4,2,1,0:T(8,128)S(1)} custom-call(f32[2,4,1,64,64]{4,3,2,1,0:T(8,128)S(1)} %add_bitcast_fusion.11), custom_call_target="InvertDiagBlocksLowerTriangular" | custom-call | tf_op jit(solution)/shard_map/while/body/eval_jaxpr/jvp(vmap())/while/body/eval_jaxpr/vmap(jit(_solve_triangular))/triangular_solve | solution.py:50
  1458.4 39.3 %custom-call.92 = f32[2,4,1,64,64]{3,4,2,1,0:T(8,128)S(1)} custom-call(f32[2,4,1,64,64]{4,3,2,1,0:T(8,128)S(1)} %add_bitcast_fusion.11), custom_call_target="InvertDiagBlocksLowerTriangular" | custom-call | tf_op jit(solution)/shard_map/while/body/eval_jaxpr/jvp(vmap())/while/body/eval_jaxpr/vmap(jit(_solve_triangular))/triangular_solve | solution.py:50
  1528.1 9.2 fusion.529
  1537.3 141.9 %all-reduce.39.cloned.1.call-done = f32[512,2048]{1,0:T(8,128)} async-done(((f32[512,2048]{1,0:T(8,128)}), f32[512,2048]{1,0:T(8,128)}) %all-reduce.39.cloned.1.call-update) | async-done | bytes 4194320 | tf_op jit(solution)/shard_map/while/body/eval_jaxpr/psum | solution.py:230
  1713.1 12.5 select_add_fusion.30
  1725.7 9.0 select_add_fusion.29
  1734.6 8.9 select_add_fusion.28
  1743.6 115.4 %all-reduce.41.cloned.1.call-done = f32[512,2048]{1,0:T(8,128)} async-done(((f32[512,2048]{1,0:T(8,128)}), f32[512,2048]{1,0:T(8,128)}) %all-reduce.41.cloned.1.call-update) | async-done | bytes 4194320 | tf_op jit(solution)/shard_map/while/body/eval_jaxpr/psum | solution.py:253
  1884.4 352.7 %while.217 = (s32[]{:T(128)}, f32[2,4,128,128]{3,2,1,0:T(8,128)S(1)}, f32[4,2,4,64,128]{4,3,2,1,0:T(8,128)}, f32[4,2,4,64,128]{4,3,2,1,0:T(8,128)}, f32[4,2,4,64...) while((s32[]{:T(128)}, ...), condition=%wide.region_24.24_spmd.clone.clone, body=%wide.region_13.23_spmd.clone.clone.sunk | while | flops 1035385408 | bytes 20528352 | solution.py:110
  1892.9 40.0 %custom-call.93 = f32[2,4,1,64,64]{3,4,2,1,0:T(8,128)} custom-call(f32[2,4,1,64,64]{4,3,2,1,0:T(8,128)S(1)} %add_bitcast_fusion.12), custom_call_target="InvertDiagBlocksLowerTriangular" | custom-call | tf_op jit(solution)/shard_map/while/body/eval_jaxpr/transpose(jvp(vmap()))/while/body/eval_jaxpr/vmap(jit(_solve_triangular))/triangular_solve | solution.py:50
  1981.0 40.0 %custom-call.93 = f32[2,4,1,64,64]{3,4,2,1,0:T(8,128)} custom-call(f32[2,4,1,64,64]{4,3,2,1,0:T(8,128)S(1)} %add_bitcast_fusion.12), custom_call_target="InvertDiagBlocksLowerTriangular" | custom-call | tf_op jit(solution)/shard_map/while/body/eval_jaxpr/transpose(jvp(vmap()))/while/body/eval_jaxpr/vmap(jit(_solve_triangular))/triangular_solve | solution.py:50
  2069.0 40.0 %custom-call.93 = f32[2,4,1,64,64]{3,4,2,1,0:T(8,128)} custom-call(f32[2,4,1,64,64]{4,3,2,1,0:T(8,128)S(1)} %add_bitcast_fusion.12), custom_call_target="InvertDiagBlocksLowerTriangular" | custom-call | tf_op jit(solution)/shard_map/while/body/eval_jaxpr/transpose(jvp(vmap()))/while/body/eval_jaxpr/vmap(jit(_solve_triangular))/triangular_solve | solution.py:50
  2157.1 40.0 %custom-call.93 = f32[2,4,1,64,64]{3,4,2,1,0:T(8,128)} custom-call(f32[2,4,1,64,64]{4,3,2,1,0:T(8,128)S(1)} %add_bitcast_fusion.12), custom_call_target="InvertDiagBlocksLowerTriangular" | custom-call | tf_op jit(solution)/shard_map/while/body/eval_jaxpr/transpose(jvp(vmap()))/while/body/eval_jaxpr/vmap(jit(_solve_triangular))/triangular_solve | solution.py:50
  2315.0 19.4 reduce-scatter.37.cloned.1.call-done
  2336.2 9.8 all-reduce.35
  2400.5 23.1 all-reduce.33
  2430.2 42.8 %reduce-scatter.17.cloned.1.call-done = bf16[256,512]{1,0:T(8,128)(2,1)} async-done(((bf16[2048,512]{1,0:T(8,128)(2,1)}), bf16[256,512]{1,0:T(8,128)(2,1)}) %reduce-scatter.17.cloned.1.call-update) | async-done | bytes 262160 | tf_op jit(solution)/shard_map/reduce_scatter | solution.py:328
  2474.9 43.1 %reduce-scatter.19.cloned.1.call-done = bf16[256,512]{1,0:T(8,128)(2,1)} async-done(((bf16[2048,512]{1,0:T(8,128)(2,1)}), bf16[256,512]{1,0:T(8,128)(2,1)}) %reduce-scatter.19.cloned.1.call-update) | async-done | bytes 262160 | tf_op jit(solution)/shard_map/reduce_scatter | solution.py:331
  2519.7 42.6 %reduce-scatter.21.cloned.1.call-done = bf16[256,512]{1,0:T(8,128)(2,1)} async-done(((bf16[2048,512]{1,0:T(8,128)(2,1)}), bf16[256,512]{1,0:T(8,128)(2,1)}) %reduce-scatter.21.cloned.1.call-update) | async-done | bytes 262160 | tf_op jit(solution)/shard_map/reduce_scatter | solution.py:334
  2564.1 42.9 %reduce-scatter.23.cloned.1.call-done = bf16[256,512]{1,0:T(8,128)(2,1)} async-done(((bf16[2048,512]{1,0:T(8,128)(2,1)}), bf16[256,512]{1,0:T(8,128)(2,1)}) %reduce-scatter.23.cloned.1.call-update) | async-done | bytes 262160 | tf_op jit(solution)/shard_map/reduce_scatter | solution.py:337
  2608.8 42.6 %reduce-scatter.25.cloned.1.call-done = bf16[512,256]{1,0:T(8,128)(2,1)} async-done(((bf16[512,2048]{1,0:T(8,128)(2,1)}), bf16[512,256]{1,0:T(8,128)(2,1)}) %reduce-scatter.25.cloned.1.call-update) | async-done | bytes 262160 | tf_op jit(solution)/shard_map/reduce_scatter | solution.py:346
  2653.2 61.0 %reduce-scatter.27.cloned.1.call-done = bf16[256,1408]{1,0:T(8,128)(2,1)} async-done(((bf16[2048,1408]{1,0:T(8,128)(2,1)}), bf16[256,1408]{1,0:T(8,128)(2,1)}) %reduce-scatter.27.cloned.1.call-update) | async-done | bytes 720912 | tf_op jit(solution)/shard_map/reduce_scatter | solution.py:349
  2716.5 60.1 %reduce-scatter.29.cloned.1.call-done = bf16[256,1408]{1,0:T(8,128)(2,1)} async-done(((bf16[2048,1408]{1,0:T(8,128)(2,1)}), bf16[256,1408]{1,0:T(8,128)(2,1)}) %reduce-scatter.29.cloned.1.call-update) | async-done | bytes 720912 | tf_op jit(solution)/shard_map/reduce_scatter | solution.py:352
  2778.9 60.6 %reduce-scatter.31.cloned.1.call-done = bf16[1408,256]{1,0:T(8,128)(2,1)} async-done(((bf16[1408,2048]{1,0:T(8,128)(2,1)}), bf16[1408,256]{1,0:T(8,128)(2,1)}) %reduce-scatter.31.cloned.1.call-update) | async-done | bytes 720912 | tf_op jit(solution)/shard_map/reduce_scatter | solution.py:355
  (1490 shorter events, 1042.1 us)
Async XLA Ops:
  7.2 86.1 %copy-start.81 = (f32[3,4,512]{2,1,0:T(4,128)S(1)}, f32[3,4,512]{2,1,0:T(4,128)}, u32[]{:S(2)}) copy-start(f32[3,4,512]{2,1,0:T(4,128)} %param.35) | copy-start | bytes 73732
  7.2 86.1 %copy-start.70 = (bf16[2048,4]{0,1:T(4,128)(2,1)S(1)}, bf16[2048,4]{0,1:T(4,128)(2,1)}, u32[]{:S(2)}) copy-start(bf16[2048,4]{0,1:T(4,128)(2,1)} %param.34) | copy-start | bytes 49156
  7.2 86.1 %copy-start.67 = (bf16[2048,4]{0,1:T(4,128)(2,1)S(1)}, bf16[2048,4]{0,1:T(4,128)(2,1)}, u32[]{:S(2)}) copy-start(bf16[2048,4]{0,1:T(4,128)(2,1)} %param.33) | copy-start | bytes 49156
  7.2 86.0 %all-gather.4.cloned.1.call-start = ((), (), s32[]{:S(2)}) async-start(), calls=%async_computation.12 | async-start | bytes 5242880 | tf_op jit(solution)/shard_map/all_gather | solution.py:198
  93.3 37.2 %copy-start.121 = (f32[1,1,4]{2,1,0:T(1,128)}, f32[1,1,4]{2,1,0:T(1,128)S(1)}, u32[]{:S(2)}) copy-start(f32[1,1,4]{2,1,0:T(1,128)S(1)} %get-tuple-element.5169) | copy-start | bytes 52 | tf_op jit(solution)/shard_map/while
  93.3 642.9 %copy-start.57 = (f32[2048]{0:T(1024)}, f32[2048]{0:T(1024)S(1)}, u32[]{:S(2)}) copy-start(f32[2048]{0:T(1024)S(1)} %get-tuple-element.5176) | copy-start | bytes 24580 | tf_op jit(solution)/shard_map/while
  93.3 457.9 %all-reduce.39.cloned.1.call-start = ((), (), s32[]{:S(2)}) async-start(), calls=%async_computation.23 | async-start | bytes 8388608 | tf_op jit(solution)/shard_map/while/body/eval_jaxpr/psum | solution.py:230
  96.8 42.5 %copy-start.83 = (f32[1,1,512]{2,1,0:T(1,128)}, f32[1,1,512]{2,1,0:T(1,128)S(1)}, u32[]{:S(2)}) copy-start(f32[1,1,512]{2,1,0:T(1,128)S(1)} %get-tuple-element.4637) | copy-start | bytes 6148 | tf_op jit(solution)/shard_map/while
  96.8 42.5 %copy-start.85 = (f32[1,1,512]{2,1,0:T(1,128)}, f32[1,1,512]{2,1,0:T(1,128)S(1)}, u32[]{:S(2)}) copy-start(f32[1,1,512]{2,1,0:T(1,128)S(1)} %get-tuple-element.4634) | copy-start | bytes 6148 | tf_op jit(solution)/shard_map/while
  96.9 42.5 %copy-start.87 = (f32[1,1,512]{2,1,0:T(1,128)}, f32[1,1,512]{2,1,0:T(1,128)S(1)}, u32[]{:S(2)}) copy-start(f32[1,1,512]{2,1,0:T(1,128)S(1)} %get-tuple-element.4635) | copy-start | bytes 6148 | tf_op jit(solution)/shard_map/while
  96.9 42.5 %copy-start.89 = (f32[1,1,512]{2,1,0:T(1,128)}, f32[1,1,512]{2,1,0:T(1,128)S(1)}, u32[]{:S(2)}) copy-start(f32[1,1,512]{2,1,0:T(1,128)S(1)} %get-tuple-element.4636) | copy-start | bytes 6148 | tf_op jit(solution)/shard_map/while
  104.4 282.0 %copy-start.72 = (f32[512]{0:T(512)}, f32[512]{0:T(512)S(1)}, u32[]{:S(2)}) copy-start(f32[512]{0:T(512)S(1)} %get-tuple-element.4619) | copy-start | bytes 6148 | tf_op jit(solution)/shard_map/while
  156.8 228.3 %copy-start.111 = (s32[1,2,2,128]{3,1,2,0:T(2,128)S(1)}, s32[1,2,2,128]{3,1,2,0:T(2,128)}, u32[]{:S(2)}) copy-start(s32[1,2,2,128]{3,1,2,0:T(2,128)} %copy.346) | copy-start | bytes 6148 | tf_op jit(solution)/shard_map/while
  397.5 333.4 %all-reduce.41.cloned.1.call-start = ((), (), s32[]{:S(2)}) async-start(), calls=%async_computation.24 | async-start | bytes 8388608 | tf_op jit(solution)/shard_map/while/body/eval_jaxpr/psum | solution.py:253
  576.8 587.7 %reduce-scatter.39.cloned.1.call-start = ((), (), s32[]{:S(2)}) async-start(), calls=%async_computation.26 | async-start | bytes 2621440 | tf_op jit(solution)/shard_map/while/body/eval_jaxpr/reduce_scatter | solution.py:239
  606.9 599.5 %reduce-scatter.37.cloned.1.call-start = ((), (), s32[]{:S(2)}) async-start(), calls=%async_computation.25 | async-start | bytes 2621440 | tf_op jit(solution)/shard_map/while/body/eval_jaxpr/reduce_scatter | solution.py:274
  1181.3 36.7 %copy-start.116 = (f32[512]{0:T(512)S(1)}, f32[512]{0:T(512)}, u32[]{:S(2)}) copy-start(f32[512]{0:T(512)} %get-tuple-element.5106) | copy-start | bytes 6148 | tf_op jit(solution)/shard_map/while
  1181.3 36.8 %copy-start.110 = (f32[512]{0:T(512)S(1)}, f32[512]{0:T(512)}, u32[]{:S(2)}) copy-start(f32[512]{0:T(512)} %get-tuple-element.4724) | copy-start | bytes 6148 | tf_op jit(solution)/shard_map/while
  1181.3 36.8 %copy-start.133 = (f32[2,512,512]{2,1,0:T(8,128)S(1)}, f32[2,512,512]{2,1,0:T(8,128)}, u32[]{:S(2)}) copy-start(f32[2,512,512]{2,1,0:T(8,128)} %get-tuple-element.5109) | copy-start | bytes 6291460 | tf_op jit(solution)/shard_map/while
  1184.7 36.8 %copy-start.58 = (f32[2048]{0:T(1024)S(1)}, f32[2048]{0:T(1024)}, u32[]{:S(2)}) copy-start(f32[2048]{0:T(1024)} %copy-done.57) | copy-start | bytes 24580 | tf_op jit(solution)/shard_map/while
  1184.7 36.8 %copy-start.82 = (f32[3,4,512]{2,1,0:T(4,128)S(1)}, f32[3,4,512]{2,1,0:T(4,128)}, u32[]{:S(2)}) copy-start(f32[3,4,512]{2,1,0:T(4,128)} %get-tuple-element.5407) | copy-start | bytes 73732 | tf_op jit(solution)/shard_map/while
  1184.7 36.8 %copy-start.122 = (f32[1,1,4]{2,1,0:T(1,128)S(1)}, f32[1,1,4]{2,1,0:T(1,128)}, u32[]{:S(2)}) copy-start(f32[1,1,4]{2,1,0:T(1,128)} %copy-done.121) | copy-start | bytes 52 | tf_op jit(solution)/shard_map/while
  1221.7 37.2 %copy-start.121 = (f32[1,1,4]{2,1,0:T(1,128)}, f32[1,1,4]{2,1,0:T(1,128)S(1)}, u32[]{:S(2)}) copy-start(f32[1,1,4]{2,1,0:T(1,128)S(1)} %get-tuple-element.5169) | copy-start | bytes 52 | tf_op jit(solution)/shard_map/while
  1221.7 642.5 %copy-start.57 = (f32[2048]{0:T(1024)}, f32[2048]{0:T(1024)S(1)}, u32[]{:S(2)}) copy-start(f32[2048]{0:T(1024)S(1)} %get-tuple-element.5176) | copy-start | bytes 24580 | tf_op jit(solution)/shard_map/while
  1221.7 457.5 %all-reduce.39.cloned.1.call-start = ((), (), s32[]{:S(2)}) async-start(), calls=%async_computation.23 | async-start | bytes 8388608 | tf_op jit(solution)/shard_map/while/body/eval_jaxpr/psum | solution.py:230
  1225.2 42.5 %copy-start.83 = (f32[1,1,512]{2,1,0:T(1,128)}, f32[1,1,512]{2,1,0:T(1,128)S(1)}, u32[]{:S(2)}) copy-start(f32[1,1,512]{2,1,0:T(1,128)S(1)} %get-tuple-element.4637) | copy-start | bytes 6148 | tf_op jit(solution)/shard_map/while
  1225.2 42.5 %copy-start.85 = (f32[1,1,512]{2,1,0:T(1,128)}, f32[1,1,512]{2,1,0:T(1,128)S(1)}, u32[]{:S(2)}) copy-start(f32[1,1,512]{2,1,0:T(1,128)S(1)} %get-tuple-element.4634) | copy-start | bytes 6148 | tf_op jit(solution)/shard_map/while
  1225.2 42.5 %copy-start.87 = (f32[1,1,512]{2,1,0:T(1,128)}, f32[1,1,512]{2,1,0:T(1,128)S(1)}, u32[]{:S(2)}) copy-start(f32[1,1,512]{2,1,0:T(1,128)S(1)} %get-tuple-element.4635) | copy-start | bytes 6148 | tf_op jit(solution)/shard_map/while
  1225.2 42.5 %copy-start.89 = (f32[1,1,512]{2,1,0:T(1,128)}, f32[1,1,512]{2,1,0:T(1,128)S(1)}, u32[]{:S(2)}) copy-start(f32[1,1,512]{2,1,0:T(1,128)S(1)} %get-tuple-element.4636) | copy-start | bytes 6148 | tf_op jit(solution)/shard_map/while
  1232.8 281.8 %copy-start.72 = (f32[512]{0:T(512)}, f32[512]{0:T(512)S(1)}, u32[]{:S(2)}) copy-start(f32[512]{0:T(512)S(1)} %get-tuple-element.4619) | copy-start | bytes 6148 | tf_op jit(solution)/shard_map/while
  1285.1 228.1 %copy-start.111 = (s32[1,2,2,128]{3,1,2,0:T(2,128)S(1)}, s32[1,2,2,128]{3,1,2,0:T(2,128)}, u32[]{:S(2)}) copy-start(s32[1,2,2,128]{3,1,2,0:T(2,128)} %copy.346) | copy-start | bytes 6148 | tf_op jit(solution)/shard_map/while
  1525.7 333.2 %all-reduce.41.cloned.1.call-start = ((), (), s32[]{:S(2)}) async-start(), calls=%async_computation.24 | async-start | bytes 8388608 | tf_op jit(solution)/shard_map/while/body/eval_jaxpr/psum | solution.py:253
  1704.8 587.7 %reduce-scatter.39.cloned.1.call-start = ((), (), s32[]{:S(2)}) async-start(), calls=%async_computation.26 | async-start | bytes 2621440 | tf_op jit(solution)/shard_map/while/body/eval_jaxpr/reduce_scatter | solution.py:239
  1743.5 590.9 %reduce-scatter.37.cloned.1.call-start = ((), (), s32[]{:S(2)}) async-start(), calls=%async_computation.25 | async-start | bytes 2621440 | tf_op jit(solution)/shard_map/while/body/eval_jaxpr/reduce_scatter | solution.py:274
  2309.3 36.7 %copy-start.123 = (f32[128]{0:T(128)S(1)}, f32[128]{0:T(128)}, u32[]{:S(2)}) copy-start(f32[128]{0:T(128)} %get-tuple-element.5105) | copy-start | bytes 1540 | tf_op jit(solution)/shard_map/while
  2309.3 36.7 %copy-start.116 = (f32[512]{0:T(512)S(1)}, f32[512]{0:T(512)}, u32[]{:S(2)}) copy-start(f32[512]{0:T(512)} %get-tuple-element.5106) | copy-start | bytes 6148 | tf_op jit(solution)/shard_map/while
  2309.3 36.8 %copy-start.110 = (f32[512]{0:T(512)S(1)}, f32[512]{0:T(512)}, u32[]{:S(2)}) copy-start(f32[512]{0:T(512)} %get-tuple-element.4724) | copy-start | bytes 6148 | tf_op jit(solution)/shard_map/while
  2309.3 36.8 %copy-start.133 = (f32[2,512,512]{2,1,0:T(8,128)S(1)}, f32[2,512,512]{2,1,0:T(8,128)}, u32[]{:S(2)}) copy-start(f32[2,512,512]{2,1,0:T(8,128)} %get-tuple-element.5109) | copy-start | bytes 6291460 | tf_op jit(solution)/shard_map/while
  2354.0 69.6 %reduce-scatter.35.cloned.1.call-start = ((), (), s32[]{:S(2)}) async-start(), calls=%async_computation.22 | async-start | bytes 589824
  2355.9 72.8 %reduce-scatter.33.cloned.1.call-start = ((), (), s32[]{:S(2)}) async-start(), calls=%async_computation.21 | async-start | bytes 589824
  2357.8 115.3 %reduce-scatter.17.cloned.1.call-start = ((), (), s32[]{:S(2)}) async-start(), calls=%async_computation.13 | async-start | bytes 2359296 | tf_op jit(solution)/shard_map/reduce_scatter | solution.py:328
  2361.6 156.3 %reduce-scatter.19.cloned.1.call-start = ((), (), s32[]{:S(2)}) async-start(), calls=%async_computation.14 | async-start | bytes 2359296 | tf_op jit(solution)/shard_map/reduce_scatter | solution.py:331
  2365.5 196.8 %reduce-scatter.21.cloned.1.call-start = ((), (), s32[]{:S(2)}) async-start(), calls=%async_computation.15 | async-start | bytes 2359296 | tf_op jit(solution)/shard_map/reduce_scatter | solution.py:334
  2369.5 237.6 %reduce-scatter.23.cloned.1.call-start = ((), (), s32[]{:S(2)}) async-start(), calls=%async_computation.16 | async-start | bytes 2359296 | tf_op jit(solution)/shard_map/reduce_scatter | solution.py:337
  2373.3 278.1 %reduce-scatter.25.cloned.1.call-start = ((), (), s32[]{:S(2)}) async-start(), calls=%async_computation.17 | async-start | bytes 2359296 | tf_op jit(solution)/shard_map/reduce_scatter | solution.py:346
  2377.2 337.0 %reduce-scatter.27.cloned.1.call-start = ((), (), s32[]{:S(2)}) async-start(), calls=%async_computation.18 | async-start | bytes 6488064 | tf_op jit(solution)/shard_map/reduce_scatter | solution.py:349
  2384.6 392.0 %reduce-scatter.29.cloned.1.call-start = ((), (), s32[]{:S(2)}) async-start(), calls=%async_computation.19 | async-start | bytes 6488064 | tf_op jit(solution)/shard_map/reduce_scatter | solution.py:352
  2392.0 447.4 %reduce-scatter.31.cloned.1.call-start = ((), (), s32[]{:S(2)}) async-start(), calls=%async_computation.20 | async-start | bytes 6488064 | tf_op jit(solution)/shard_map/reduce_scatter | solution.py:355
  (249 other events, 1642.3 us)
Sparse Core Ops, SparseCore 0:
  9.6 83.5 all-gather.3
  397.7 153.4 all-reduce.38
  576.9 153.9 all-reduce.40
  733.1 42.9 reduce-scatter.38
  1163.6 42.7 reduce-scatter.36
  1525.8 153.3 all-reduce.38
  1704.9 153.9 all-reduce.40
  1861.2 42.8 reduce-scatter.38
  2291.5 42.8 reduce-scatter.36
  2358.2 32.3 reduce-scatter.34
  2394.5 34.1 reduce-scatter.32
  2431.8 41.1 reduce-scatter.16
  2476.7 41.1 reduce-scatter.18
  2521.1 41.1 reduce-scatter.20
  2565.8 41.2 reduce-scatter.22
  2610.2 41.2 reduce-scatter.24
  2655.1 59.0 reduce-scatter.26
  2717.5 59.0 reduce-scatter.28
  2780.4 59.0 reduce-scatter.30
where the time goes:
time: 2860 us; the launch traced here: 2850 us
  waiting for transfers between devices  1020 us (36%)
  other arithmetic  937 us (33%)
  matrix products  552 us (19%)
  local copies, waits for them, and re-layouts  248 us (9%)
  blocking collectives  68.5 us (2%)
    another operation x72, other arithmetic, triangular(): jax.scipy.linalg.solve_triangular(system, target, lower=True, unit_diagon...  651 us
    psum x2, waiting for transfers between devices, micro_step(): hidden = inputs + lax.psum(partial_attn, 'head')  284 us
    psum x2, waiting for transfers between devices, micro_step(): grad_mid = lax.psum(partial_mid, 'head')  239 us
    dot_general x20, matrix products, matmul(): return jnp.dot(former, latter, preferred_element_type=jnp.float32)  85.1 us
    dot_general x20, matrix products, matmul_rows(): lax.dot_general(former, latter, (((0,), (0,)), ((), ())), preferred_eleme...  78.1 us
    reduce_scatter x1, waiting for transfers between devices, body(): lax.psum_scatter(mlp_gate_grad.astype(jnp.bfloat16), 'dp', scatter_dimens...  61 us
    reduce_scatter x1, waiting for transfers between devices, body(): lax.psum_scatter(down_grad.astype(jnp.bfloat16), 'dp', scatter_dimension=...  60.6 us
    reduce_scatter x1, waiting for transfers between devices, body(): lax.psum_scatter(mlp_up_grad.astype(jnp.bfloat16), 'dp', scatter_dimensio...  60.1 us
  transfers between devices with their start and end apart: 19, of which 16 were waited for; matrix products, arithmetic and copies ran while one was open for 37% of the time, Pallas kernels for 0%

commit v1 on v0

v1 whole, which is shorter than its diff:
```python
import functools
import jax
import jax.numpy as jnp
from jax import lax
from jax.experimental import pallas as pl
from jax.experimental.pallas import tpu as pltpu
from jax.sharding import PartitionSpec as P

SEQ = 256
CH = 128
TAPS = 4
epsilon = 1e-06
f32 = jnp.float32
bf16 = jnp.bfloat16


def halves(x):
    high = x.astype(bf16)
    return high, (x - high.astype(f32)).astype(bf16)


def left(x):
    return jnp.concatenate(halves(x), axis=1)


def right(x):
    row = jnp.concatenate(halves(x), axis=1)
    return jnp.concatenate([row, row], axis=0)


def right_t(x):
    high, low = halves(x)
    return jnp.concatenate(
        [jnp.concatenate([high, high], axis=1), jnp.concatenate([low, low], axis=1)], axis=0
    )


def fold(r):
    return r[:, :CH] + r[:, CH:]


def mm(l, r):
    return fold(jnp.dot(l, r, preferred_element_type=f32))


def mm_t(l, r):
    return fold(lax.dot_general(l, r, (((1,), (1,)), ((), ())), preferred_element_type=f32))


def grids():
    row = lax.broadcasted_iota(jnp.int32, (CH, CH), 0)
    col = lax.broadcasted_iota(jnp.int32, (CH, CH), 1)
    return row, col


def sum_matrix(row, col):
    lower = (row >= col).astype(bf16)
    zero = jnp.zeros((CH, CH), bf16)
    return jnp.concatenate(
        [
            jnp.concatenate([lower, jnp.full((CH, CH), -1, bf16)], axis=1),
            jnp.concatenate([lower, zero], axis=1),
            jnp.concatenate([(row < col).astype(bf16), zero], axis=1),
        ],
        axis=0,
    )


def decay_sums(decay, row, col, sums):
    wide = jnp.broadcast_to(decay, (CH, CH))
    cut = jnp.where(row <= col, wide, 0.0)
    r = jnp.concatenate(
        [jnp.concatenate(halves(wide), axis=1), jnp.concatenate(halves(cut), axis=1)], axis=0
    )
    out = fold(jnp.dot(sums, r, preferred_element_type=f32))
    return out[:CH], out[CH : 2 * CH], out[2 * CH :]


def shifted(x, by, row):
    if by == 0:
        return x
    return jnp.where(row >= by, pltpu.roll(x, by, 0), 0.0)


def shifted_back(x, by, row):
    if by == 0:
        return x
    return jnp.where(row < SEQ - by, pltpu.roll(x, SEQ - by, 0), 0.0)


def sigmoid(x):
    return 1.0 / (1.0 + jnp.exp(-x))


def conv_sum(x, taps, row):
    total = x * taps[TAPS - 1 : TAPS]
    for by in range(1, TAPS):
        total = total + shifted(x, by, row) * taps[TAPS - 1 - by : TAPS - by]
    return total


def conv_back(x, grad, taps, row):
    grad_x = grad * taps[TAPS - 1 : TAPS]
    sums = [jnp.sum(grad * x, 0, keepdims=True)]
    for by in range(1, TAPS):
        grad_x = grad_x + shifted_back(grad, by, row) * taps[TAPS - 1 - by : TAPS - by]
        sums.append(jnp.sum(grad * shifted(x, by, row), 0, keepdims=True))
    return grad_x, jnp.concatenate(sums[::-1], axis=0)


def norm_of(x):
    return lax.rsqrt(jnp.sum(x * x, -1, keepdims=True) + epsilon)


def softplus(x):
    return jnp.maximum(x, 0.0) + jnp.log(1.0 + jnp.exp(-jnp.abs(x)))


def forward_kernel(
    pre_ref, conv_ref, decay_ref, gain_ref,
    mixed_ref, inverse_ref, update_ref, delta_ref,
):
    heads = decay_ref.shape[1]
    inner = heads * CH

    def piece(index, h):
        return slice(index * inner + h * CH, index * inner + (h + 1) * CH)

    row, col = grids()
    long_row = lax.broadcasted_iota(jnp.int32, (SEQ, CH), 0)
    sums = sum_matrix(row, col)
    within = row >= col
    eye = (row == col).astype(f32)
    ab = pre_ref[:, 4 * inner :]
    decay_all = -jnp.exp(decay_ref[0:1, :]) * softplus(ab[:, :heads] + decay_ref[1:2, :])
    strength_all = sigmoid(ab[:, heads : 2 * heads])
    systems, inverses, kept = [], [], []
    for h in range(heads):
        at = slice(h * CH, (h + 1) * CH)
        parts = []
        for index in range(3):
            pre = conv_sum(pre_ref[:, piece(index, h)], conv_ref[index][:, at], long_row)
            parts.append(pre * sigmoid(pre))
        queries = parts[0] * norm_of(parts[0]) * CH ** (-0.5)
        keys = parts[1] * norm_of(parts[1])
        for c in range(2):
            span = slice(c * CH, (c + 1) * CH)
            q, k, v = queries[span], keys[span], parts[2][span]
            spread, start, tail = decay_sums(decay_all[span, h : h + 1], row, col, sums)
            falloff = jnp.where(within, jnp.exp(jnp.minimum(spread, 0.0)), 0.0)
            k_left = left(k)
            both = mm_t(jnp.concatenate([k_left, left(q)], axis=0), right_t(k))
            beta = jnp.broadcast_to(strength_all[span, h : h + 1], (CH, CH))
            system = jnp.where(row > col, beta * falloff * both[:CH], 0.0)
            systems.append(system)
            inverses.append(
                eye - jnp.where((row // 2 == col // 2) & (row % 2 > col % 2), system, 0.0)
            )
            kept.append((q, k_left, v, k, beta, falloff * both[CH:], jnp.exp(start), jnp.exp(tail)))
    size = 2
    while size < CH:
        mask = (row // (2 * size) == col // (2 * size)) & ((row // size) % 2 > (col // size) % 2)
        for i in range(len(systems)):
            inverse = inverses[i]
            step = mm(left(inverse), right(jnp.where(mask, systems[i], 0.0)))
            inverses[i] = inverse - mm(left(step), right(inverse))
        size *= 2
    for h in range(heads):
        at = slice(h * CH, (h + 1) * CH)
        q, k_left, v, k, beta, scores, start, tail = kept[2 * h]
        first_update = mm(left(inverses[2 * h]), right(beta * v))
        first_out = mm(left(scores), right(first_update))
        state = mm(left(k.T), right(tail * first_update))
        q, k_left, v, k, beta, scores, start, tail = kept[2 * h + 1]
        read = mm(jnp.concatenate([k_left, left(q)], axis=0), right(state))
        second_update = mm(left(inverses[2 * h + 1]), right(beta * (v - start * read[:CH])))
        second_out = start * read[CH:] + mm(left(scores), right(second_update))
        for c, (update, out) in enumerate(((first_update, first_out), (second_update, second_out))):
            span = slice(c * CH, (c + 1) * CH)
            update_ref[span, at] = update
            delta_ref[span, at] = out
            inverse_ref[span, at] = inverses[2 * h + c].T
            scale = lax.rsqrt(jnp.mean(out * out, -1, keepdims=True) + epsilon)
            gate = pre_ref[span, piece(3, h)]
            mixed_ref[span, at] = (
                out * scale * gain_ref[...] * (gate * sigmoid(gate))
            ).astype(bf16)


def backward_kernel(
    pre_ref, conv_ref, decay_ref, gain_ref,
    inverse_ref, update_ref, delta_ref, grad_ref,
    gpre_ref, gwide_ref, gdecay_ref,
):
    heads = decay_ref.shape[1]
    inner = heads * CH

    def piece(index, h):
        return slice(index * inner + h * CH, index * inner + (h + 1) * CH)

    row, col = grids()
    long_row = lax.broadcasted_iota(jnp.int32, (SEQ, CH), 0)
    sums = sum_matrix(row, col)
    within = row >= col
    strict = row > col
    upper = (row <= col).astype(bf16)
    upper2 = jnp.concatenate([upper, upper], axis=1)
    lower = strict.astype(bf16)
    lower2 = jnp.concatenate([lower, lower], axis=1)
    ab = pre_ref[:, 4 * inner :]
    rate = -jnp.exp(decay_ref[0:1, :])
    shift = ab[:, :heads] + decay_ref[1:2, :]
    decay_all = rate * softplus(shift)
    strength_all = sigmoid(ab[:, heads : 2 * heads])
    grad_decays, grad_strengths = [], []
    for h in range(heads):
        at = slice(h * CH, (h + 1) * CH)
        pres, parts = [], []
        for index in range(3):
            pre = conv_sum(pre_ref[:, piece(index, h)], conv_ref[index][:, at], long_row)
            pres.append(pre)
            parts.append(pre * sigmoid(pre))
        q_norm, k_norm = norm_of(parts[0]), norm_of(parts[1])
        queries = parts[0] * q_norm * CH ** (-0.5)
        keys = parts[1] * k_norm
        out = delta_ref[:, at]
        gate = pre_ref[:, piece(3, h)]
        grad = grad_ref[:, at]
        gain = gain_ref[...]
        scale = lax.rsqrt(jnp.mean(out * out, -1, keepdims=True) + epsilon)
        sig = sigmoid(gate)
        scaled = out * scale
        gpre_ref[:, piece(3, h)] = (grad * scaled * gain * sig * (1.0 + gate * (1.0 - sig))).astype(bf16)
        grad_normed = grad * gate * sig
        norm_gain_sum = jnp.sum(grad_normed * scaled, 0, keepdims=True)
        grad_scaled = grad_normed * gain
        grad_out = scale * (
            grad_scaled - scaled * jnp.mean(grad_scaled * scaled, -1, keepdims=True)
        )
        stuff = []
        for c in range(2):
            span = slice(c * CH, (c + 1) * CH)
            q, k, v = queries[span], keys[span], parts[2][span]
            spread, start, tail = decay_sums(decay_all[span, h : h + 1], row, col, sums)
            falloff = jnp.where(within, jnp.exp(jnp.minimum(spread, 0.0)), 0.0)
            q_left, k_left = left(q), left(k)
            both = mm_t(jnp.concatenate([k_left, q_left], axis=0), right_t(k))
            beta = jnp.broadcast_to(strength_all[span, h : h + 1], (CH, CH))
            stuff.append(
                (q, k, v, falloff, both[:CH] * falloff, both[CH:] * falloff, beta,
                 jnp.exp(start), jnp.exp(tail), q_left, k_left)
            )
        carry = None
        grads_q, grads_k, grads_v, grads_g, grads_b = [None] * 2, [None] * 2, [None] * 2, [None] * 2, [None] * 2
        first_update = update_ref[0:CH, at]
        tail_update = stuff[0][8] * first_update
        state = mm(left(stuff[0][1].T), right(tail_update))
        for c in (1, 0):
            span = slice(c * CH, (c + 1) * CH)
            q, k, v, falloff, similar, scores, beta, start, tail, q_left, k_left = stuff[c]
            update = update_ref[span, at]
            go = grad_out[span]
            grad_update = mm(left(scores.T), right(go))
            target = v
            if c == 1:
                read = mm(jnp.concatenate([k_left, q_left], axis=0), right(state))
                target = v - start * read[:CH]
            else:
                pushed = mm(k_left, right(carry))
                grad_update = grad_update + tail * pushed
            grad_write = mm(left(inverse_ref[span, at]), right(grad_update))
            outer = mm_t(
                jnp.concatenate([left(grad_write), left(go)], axis=0), right_t(update)
            )
            grad_system = jnp.where(strict, -outer[:CH], 0.0)
            grad_scores = jnp.where(within, outer[CH:], 0.0)
            grads_b[c] = jnp.sum(grad_write * target + grad_system * similar, -1, keepdims=True)
            grad_target = beta * grad_write
            grads_v[c] = grad_target
            grad_similar = grad_system * beta * falloff
            grad_dots = grad_scores * falloff
            moved = grad_system * beta * similar + grad_scores * scores
            k_right = right(k)
            back = mm(
                jnp.concatenate(
                    [left(grad_dots), left(grad_similar + grad_similar.T)], axis=0
                ),
                k_right,
            )
            gq = back[:CH]
            gk = back[CH:] + mm(left(grad_dots.T), right(q))
            if c == 1:
                through_out, through_read = start * go, -start * grad_target
                more = mm_t(
                    jnp.concatenate([left(through_out), left(through_read)], axis=0),
                    right_t(state),
                )
                gq = gq + more[:CH]
                gk = gk + more[CH:]
                carry = mm(left(q.T), right(through_out)) + mm(left(k.T), right(through_read))
                other = through_out * read[CH:] + through_read * read[:CH]
                turned = jnp.dot(
                    upper2,
                    jnp.concatenate(
                        [
                            jnp.concatenate([a, b], axis=1)
                            for a, b in zip(halves(moved), halves(other))
                        ],
                        axis=0,
                    ),
                    preferred_element_type=f32,
                )
                turned = jnp.where(strict, turned[:, :CH], 0.0) + turned[:, CH:]
            else:
                gk = gk + mm_t(left(tail_update), right_t(carry))
                other = pushed * tail_update
                r1 = jnp.dot(upper2, jnp.concatenate(halves(moved), axis=0), preferred_element_type=f32)
                r2 = jnp.dot(lower2, jnp.concatenate(halves(other), axis=0), preferred_element_type=f32)
                turned = jnp.where(strict, r1, 0.0) + r2
            grads_g[c] = jnp.sum(turned, -1, keepdims=True)
            grads_q[c] = gq
            grads_k[c] = gk
        grad_decays.append(jnp.concatenate(grads_g, axis=0))
        grad_strengths.append(jnp.concatenate(grads_b, axis=0))
        gq = jnp.concatenate(grads_q, axis=0)
        gk = jnp.concatenate(grads_k, axis=0)
        gv = jnp.concatenate(grads_v, axis=0)
        unit = parts[0] * q_norm
        gq = (CH ** (-0.5)) * q_norm * (gq - unit * jnp.sum(gq * unit, -1, keepdims=True))
        gk = k_norm * (gk - keys * jnp.sum(gk * keys, -1, keepdims=True))
        for index, g in enumerate((gq, gk, gv)):
            pre = pres[index]
            sig = sigmoid(pre)
            g = g * sig * (1.0 + pre * (1.0 - sig))
            gx, gw = conv_back(pre_ref[:, piece(index, h)], g, conv_ref[index][:, at], long_row)
            gpre_ref[:, piece(index, h)] = gx.astype(bf16)
            gwide_ref[0, TAPS * index : TAPS * (index + 1), at] = gw
        gwide_ref[0, 3 * TAPS : 3 * TAPS + 1, at] = norm_gain_sum
    lane = lax.broadcasted_iota(jnp.int32, (SEQ, CH), 1)
    gd = jnp.zeros((SEQ, CH), f32)
    gs = jnp.zeros((SEQ, CH), f32)
    for h in range(heads):
        gd = jnp.where(lane == h, grad_decays[h], gd)
        gs = jnp.where(lane == heads + h, grad_strengths[h], gs)
    sig = sigmoid(ab)
    grad_shift = gd[:, :heads] * rate * sigmoid(shift)
    gab = gs * sig * (1.0 - sig)
    for h in range(heads):
        gab = jnp.where(lane == h, grad_shift[:, h : h + 1], gab)
    gpre_ref[:, 4 * inner :] = gab.astype(bf16)
    gdecay_ref[0, 0:1, :] = jnp.sum(gd[:, :heads] * decay_all, 0, keepdims=True)
    gdecay_ref[0, 1:2, :] = jnp.sum(grad_shift, 0, keepdims=True)


def row_spec(width):
    return pl.BlockSpec((SEQ, width), lambda i: (i, 0))


def whole_spec(shape):
    return pl.BlockSpec(shape, lambda i: (0,) * len(shape))


def seq_spec(shape):
    return pl.BlockSpec((1,) + shape, lambda i: (i, 0, 0))


def mixer_forward(pre, conv_weight, decay, gain):
    rows = pre.shape[0]
    heads = decay.shape[1]
    width = heads * CH
    wide = jax.ShapeDtypeStruct((rows, width), f32)
    return pl.pallas_call(
        forward_kernel,
        grid=(rows // SEQ,),
        in_specs=[row_spec(pre.shape[1])]
        + [whole_spec(conv_weight.shape), whole_spec(decay.shape), whole_spec(gain.shape)],
        out_specs=[row_spec(width)] * 4,
        out_shape=[jax.ShapeDtypeStruct((rows, width), bf16), wide, wide, wide],
        compiler_params=pltpu.CompilerParams(vmem_limit_bytes=56 * 2**20),
        cost_estimate=pl.CostEstimate(flops=10**10, bytes_accessed=10**7, transcendentals=0),
        name="mixer_forward",
    )(pre, conv_weight, decay, gain)


def mixer_backward(pre, conv_weight, decay, gain, inverse, update, delta, grad):
    rows = pre.shape[0]
    heads = decay.shape[1]
    width = heads * CH
    count = rows // SEQ
    return pl.pallas_call(
        backward_kernel,
        grid=(count,),
        in_specs=[row_spec(pre.shape[1])]
        + [whole_spec(conv_weight.shape), whole_spec(decay.shape), whole_spec(gain.shape)]
        + [row_spec(width)] * 4,
        out_specs=[row_spec(pre.shape[1]), seq_spec((16, width)), seq_spec((2, heads))],
        out_shape=[
            jax.ShapeDtypeStruct(pre.shape, bf16),
            jax.ShapeDtypeStruct((count, 16, width), f32),
            jax.ShapeDtypeStruct((count, 2, heads), f32),
        ],
        compiler_params=pltpu.CompilerParams(vmem_limit_bytes=56 * 2**20),
        cost_estimate=pl.CostEstimate(flops=2 * 10**10, bytes_accessed=2 * 10**7, transcendentals=0),
        name="mixer_backward",
    )(pre, conv_weight, decay, gain, inverse, update, delta, grad)


def matmul(former, latter, kind=f32):
    return jnp.dot(former, latter, preferred_element_type=f32).astype(kind)


def matmul_rows(former, latter, kind=f32):
    return lax.dot_general(
        former, latter, (((0,), (0,)), ((), ())), preferred_element_type=f32
    ).astype(kind)


def matmul_back(former, latter, kind=f32):
    return lax.dot_general(
        former, latter, (((1,), (1,)), ((), ())), preferred_element_type=f32
    ).astype(kind)


def line_gather(own, axis, count, me):
    rightward, leftward = [own], [own]
    for step in range(1, count):
        rightward.append(
            lax.ppermute(rightward[-1], axis, [(d, d + 1) for d in range(step - 1, count - 1)])
        )
        leftward.append(
            lax.ppermute(leftward[-1], axis, [(d + 1, d) for d in range(count - step)])
        )
    blocks = []
    for block in range(count):
        chosen = own
        for device in range(count):
            if device > block:
                chosen = jnp.where(me == device, rightward[device - block], chosen)
            elif device < block:
                chosen = jnp.where(me == device, leftward[block - device], chosen)
        blocks.append(chosen)
    return blocks


def line_scatter(partial, axis, count, me):
    width = partial.shape[1] // count

    def block(index):
        at = jnp.clip(index, 0, count - 1) * width
        return lax.dynamic_slice_in_dim(partial, at, width, axis=1)

    rightward = leftward = None
    for step in range(1, count):
        send_right = block(count - step + me)
        send_left = block(step - count + me)
        if rightward is not None:
            send_right = (send_right.astype(f32) + rightward.astype(f32)).astype(bf16)
            send_left = (send_left.astype(f32) + leftward.astype(f32)).astype(bf16)
        rightward = lax.ppermute(send_right, axis, [(d, d + 1) for d in range(step)])
        leftward = lax.ppermute(
            send_left, axis, [(count - 1 - d, count - 2 - d) for d in range(step)]
        )
    total = block(me).astype(f32)
    return total + rightward.astype(f32) + leftward.astype(f32)


def sum_around(own, axis, count):
    total = own
    for step in range(1, count):
        total = total + lax.ppermute(own, axis, [(d, (d + step) % count) for d in range(count)])
    return total


def sum_doubling(own, axis, count):
    step = 1
    while step < count:
        own = own + lax.ppermute(own, axis, [(d, d ^ step) for d in range(count)])
        step *= 2
    return own


def body(
    block_input, cotangent, seq_count, attn_gain, w_query, w_key, w_value, w_gate,
    w_alpha, w_beta, conv_weight, decay_base, decay_bias, norm_gain, w_out, mlp_gain,
    w_mlp_gate, w_mlp_up, w_down, *, heads_count, groups_count,
):
    micro_count, row_count, width = block_input.shape
    me = lax.axis_index("head")
    features = heads_count * width
    heads = decay_base.shape[0]
    hidden_units = w_down.shape[0]
    inner = w_query.shape[1]
    pad = jnp.zeros((features, CH - 2 * heads), bf16)
    w_in = jnp.concatenate([w_query, w_key, w_value, w_gate, w_alpha, w_beta, pad], axis=1)
    w_up2 = jnp.concatenate([w_mlp_gate, w_mlp_up], axis=1)
    decay = jnp.stack([decay_base, decay_bias])
    gain_row = norm_gain[None]

    def gathered(own):
        return jnp.concatenate(line_gather(own, "head", heads_count, me), axis=1)

    def own_of(values):
        return lax.dynamic_slice_in_dim(values, me * width, width, axis=values.ndim - 1)

    with_gains = jnp.concatenate(
        [block_input[0], jnp.stack([attn_gain, mlp_gain]), jnp.zeros((14, width), bf16)], axis=0
    )
    sent = [with_gains] + [block_input[m] for m in range(1, micro_count)]
    attn_own = attn_gain.astype(f32)
    mlp_own = mlp_gain.astype(f32)

    raw = [gathered(x) for x in sent]
    attn_scale = raw[0][row_count].astype(f32)
    mlp_scale = raw[0][row_count + 1].astype(f32)
    steps = range(micro_count)
    st = [dict() for _ in steps]
    for m in steps:
        s = st[m]
        live = (jnp.arange(row_count) // SEQ < seq_count[m, 0])[:, None]
        low = jnp.where(live, raw[m][:row_count], jnp.zeros((), bf16))
        inputs = low.astype(f32)
        s["inputs_own"] = jnp.where(live, block_input[m], jnp.zeros((), bf16)).astype(f32)
        s["scale_in"] = lax.rsqrt(jnp.mean(inputs * inputs, -1, keepdims=True) + epsilon)
        s["normed"] = (inputs * s["scale_in"] * attn_scale).astype(bf16)
        s["pre"] = matmul(s["normed"], w_in)
        s["grad_output"] = jnp.where(live, cotangent[m], jnp.zeros((), bf16))
        s["mixed"], *s["saved"] = mixer_forward(s["pre"], conv_weight, decay, gain_row)
        attended = line_scatter(matmul(s["mixed"], w_out, bf16), "head", heads_count, me)
        s["hidden_own"] = s["inputs_own"] + attended
        s["hidden"] = gathered(s["hidden_own"].astype(bf16))
    for m in steps:
        s = st[m]
        hidden = s["hidden"].astype(f32)
        s["scale_mid"] = lax.rsqrt(jnp.mean(hidden * hidden, -1, keepdims=True) + epsilon)
        s["normed_mid"] = (hidden * s["scale_mid"] * mlp_scale).astype(bf16)
        acts = matmul(s["normed_mid"], w_up2)
        gate_act, up_act = acts[:, :hidden_units], acts[:, hidden_units:]
        sig = jax.nn.sigmoid(gate_act)
        silu = gate_act * sig
        s["product"] = (silu * up_act).astype(bf16)
        grad_product = matmul_back(s["grad_output"], w_down)
        grad_gate = (grad_product * up_act * sig * (1.0 + gate_act * (1.0 - sig))).astype(bf16)
        grad_up = (grad_product * silu).astype(bf16)
        s["grad_acts"] = jnp.concatenate([grad_gate, grad_up], axis=1)
        s["grad_mid_own"] = line_scatter(
            matmul_back(s["grad_acts"], w_up2, bf16), "head", heads_count, me
        )
        s["grad_mid"] = gathered(s["grad_mid_own"].astype(bf16))
        s["output"] = (
            s["hidden_own"]
            + line_scatter(matmul(s["product"], w_down, bf16), "head", heads_count, me)
        ).astype(bf16)

    def rows_of(name):
        return jnp.concatenate([st[m][name] for m in steps], axis=0)

    def scattered(values, dimension):
        return lax.psum_scatter(values, "dp", scatter_dimension=dimension, tiled=True).astype(f32)

    up2_grad = scattered(matmul_rows(rows_of("normed_mid"), rows_of("grad_acts"), bf16), 0)
    down_grad = scattered(matmul_rows(rows_of("product"), rows_of("grad_output"), bf16), 1)
    mlp_gain_grad = sum(
        jnp.sum(s["grad_mid_own"] * s["hidden_own"] * s["scale_mid"], 0) for s in st
    )
    for m in steps:
        s = st[m]
        hidden = s["hidden"].astype(f32)
        grad_mid = s["grad_mid"].astype(f32)
        scale_mid = s["scale_mid"]
        dot_mid = jnp.sum(grad_mid * mlp_scale * hidden, -1, keepdims=True)
        back = scale_mid**3 * dot_mid / features
        s["grad_low"] = (
            s["grad_output"].astype(f32) + scale_mid * mlp_scale * grad_mid - hidden * back
        ).astype(bf16)
        s["grad_hidden_own"] = (
            own_of(s["grad_output"]).astype(f32)
            + scale_mid * mlp_own * s["grad_mid_own"]
            - s["hidden_own"] * back
        )
        grad_mixed = matmul_back(s["grad_low"], w_out)
        s["grad_pre"], wide, s["decay_sums"] = mixer_backward(
            s["pre"], conv_weight, decay, gain_row, *s["saved"], grad_mixed
        )
        s["wide"] = wide
    out_grad = scattered(matmul_rows(rows_of("mixed"), rows_of("grad_low"), bf16), 1)
    in_grad = scattered(matmul_rows(rows_of("normed"), rows_of("grad_pre"), bf16), 0)
    input_grads = []
    attn_gain_grad = 0.0
    for m in steps:
        s = st[m]
        dot_in = sum_around(
            jnp.sum(s["grad_pre"].astype(f32) * s["pre"], -1) / s["scale_in"][:, 0],
            "head",
            heads_count,
        )[:, None]
        grad_in = line_scatter(matmul_back(s["grad_pre"], w_in, bf16), "head", heads_count, me)
        scale_in = s["scale_in"]
        input_grads.append(
            s["grad_hidden_own"]
            + scale_in * attn_own * grad_in
            - s["inputs_own"] * scale_in**3 * dot_in / features
        )
        attn_gain_grad = attn_gain_grad + jnp.sum(grad_in * s["inputs_own"] * scale_in, 0)
    wide = sum(jnp.sum(s["wide"], 0) for s in st)
    decays = sum(jnp.sum(s["decay_sums"], 0) for s in st)
    taps = 3 * TAPS
    norm_sum = jnp.sum(wide[taps].reshape(heads, CH), 0)
    norm_sum = sum_around(norm_sum, "head", heads_count)
    small = jnp.concatenate(
        [
            wide[:taps].reshape(-1), attn_gain_grad, mlp_gain_grad,
            jnp.pad(norm_sum, (0, inner - CH)),
            jnp.pad(decays.reshape(-1), (0, inner - 2 * heads)),
        ]
    ).reshape(-1, CH)
    small = sum_doubling(small, "dp", groups_count).reshape(-1)
    at = taps * inner
    return (
        jnp.stack([s["output"] for s in st]),
        jnp.stack(input_grads),
        small[at : at + width],
        in_grad[:, :inner],
        in_grad[:, inner : 2 * inner],
        in_grad[:, 2 * inner : 3 * inner],
        in_grad[:, 3 * inner : 4 * inner],
        in_grad[:, 4 * inner : 4 * inner + heads],
        in_grad[:, 4 * inner + heads : 4 * inner + 2 * heads],
        small[:at].reshape(3, TAPS, inner),
        small[at + 2 * width + inner : at + 2 * width + inner + heads],
        small[at + 2 * width + inner + heads : at + 2 * width + inner + 2 * heads],
        small[at + 2 * width : at + 2 * width + CH],
        out_grad,
        small[at + width : at + 2 * width],
        up2_grad[:, :hidden_units],
        up2_grad[:, hidden_units:],
        down_grad,
    )


def solution(mesh):
    return jax.shard_map(
        functools.partial(
            body, heads_count=mesh.shape["head"], groups_count=mesh.shape["dp"]
        ),
        mesh=mesh,
        in_specs=(
            P(None, "dp", "head"), P(None, "dp", None), P(None, "dp"), P("head"),
            P(None, "head"), P(None, "head"), P(None, "head"), P(None, "head"),
            P(None, "head"), P(None, "head"), P(None, None, "head"), P("head"), P("head"),
            P(), P("head", None), P("head"), P(None, "head"), P(None, "head"), P("head", None),
        ),
        out_specs=(
            P(None, "dp", "head"), P(None, "dp", "head"), P("head"),
            P("dp", "head"), P("dp", "head"), P("dp", "head"), P("dp", "head"),
            P("dp", "head"), P("dp", "head"), P(None, None, "head"), P("head"), P("head"),
            P(), P("head", "dp"), P("head"), P("dp", "head"), P("dp", "head"), P("head", "dp"),
        ),
        check_vma=False,
    )
```

time: 2860 us -> 834 us (0.29)
  other arithmetic: 937 us -> 74.5 us
  waiting for transfers between devices: 1020 us -> 230 us
  matrix products: 552 us -> 153 us
  starting transfers between devices: 1.17 us -> 226 us
  local copies, waits for them, and re-layouts: 248 us -> 53.9 us
  Pallas kernels: 0 us -> 73.6 us
  blocking collectives: 68.5 us -> 0 us
    another operation x122 -> x5, other arithmetic: 670 us -> 6.15 us  [the longest x3 4.04 us: body(): jnp.stack([s['output'] for s in st])]
    psum x4 -> x0, waiting for transfers between devices: 523 us -> none  [the longest x2 284 us: micro_step(): hidden = inputs + lax.psum(partial_attn, 'head')]
    reduce_scatter x12 -> x4, waiting for transfers between devices: 437 us -> 0.01 us  [scattered(): lax.psum_scatter(values, 'dp', scatter_dimension=dimension, tiled=True)]
    dot_general x172 -> x8, matrix products: 359 us -> 49.7 us  [matmul(): return jnp.dot(former, latter, preferred_element_type=f32).astype(kind)]
    ppermute x0 -> x96, waiting for transfers between devices: none -> 230 us  [the longest x18 109 us: line_gather(): lax.ppermute(leftward[-1], axis, [(d + 1, d) for d in range(count - step)])]
    ppermute x0 -> x96, starting transfers between devices: none -> 226 us  [the longest x24 90.9 us: line_scatter(): lax.ppermute(send_right, axis, [(d, d + 1) for d in range(step)])]
    pallas_call x0 -> x4, Pallas kernels: none -> 73.6 us  [the longest x2 44.3 us: mixer_backward(): pl.pallas_call(backward_kernel, grid=(count,), in_specs=[row_spec(pre.sha...]
    reduce_sum x58 -> x15, other arithmetic: 88.9 us -> 15.5 us  [the longest x2 4.91 us: body(): jnp.sum(s['grad_mid_own'] * s['hidden_own'] * s['scale_mid'], 0)]
  transfers between devices with their start and end apart: 19 -> 100, of which waited for: 16 -> 42; matrix products, arithmetic and copies ran while one was open for 37% -> 24% of each run, Pallas kernels for 0% -> 7%
where the time goes in v1:
time: 834 us; the launch traced here: 828 us
  waiting for transfers between devices  230 us (28%)
  starting transfers between devices  226 us (27%)
  matrix products  153 us (18%)
  other arithmetic  74.5 us (9%)
  Pallas kernels  73.6 us (9%)
  local copies, waits for them, and re-layouts  53.9 us (6%)
  between operations  16.5 us (2%)
    ppermute x18, waiting for transfers between devices, line_gather(): lax.ppermute(leftward[-1], axis, [(d + 1, d) for d in range(count - step)])  109 us
    ppermute x24, starting transfers between devices, line_scatter(): lax.ppermute(send_right, axis, [(d, d + 1) for d in range(step)])  90.9 us
    ppermute x24, waiting for transfers between devices, line_scatter(): lax.ppermute(send_right, axis, [(d, d + 1) for d in range(step)])  67.7 us
    ppermute x18, starting transfers between devices, line_gather(): lax.ppermute(rightward[-1], axis, [(d, d + 1) for d in range(step - 1, co...  58.3 us
    dot_general x8, matrix products, matmul_back(): lax.dot_general(former, latter, (((1,), (1,)), ((), ())), preferred_eleme...  57 us
    dot_general x8, matrix products, matmul(): return jnp.dot(former, latter, preferred_element_type=f32).astype(kind)  49.7 us
    dot_general x4, matrix products, matmul_rows(): lax.dot_general(former, latter, (((0,), (0,)), ((), ())), preferred_eleme...  46.1 us
    pallas_call x2, Pallas kernels, mixer_backward(): pl.pallas_call(backward_kernel, grid=(count,), in_specs=[row_spec(pre.sha...  44.3 us
  transfers between devices with their start and end apart: 100, of which 42 were waited for; matrix products, arithmetic and copies ran while one was open for 24% of the time, Pallas kernels for 7%

profile of v1, /device:TPU:0, one launch (start us, length us, event | category | flops | bytes accessed | tf_op | source)
XLA Modules:
  0.0 828.0 jit_solution(1066583784480789361)
XLA Ops:
  17.9 6.0 collective-permute-start
  31.7 10.4 %collective-permute-done.3 = bf16[528,512]{1,0:T(8,128)(2,1)} collective-permute-done((bf16[528,512]{1,0:T(8,128)(2,1)S(1)}, bf16[528,512]{1,0:T(8,128)(2,1)}, u32[]{:S(2)}, u32[]{:S(2)}) %collective-permute-start.3) | collective-permute-done | bytes 540704 | tf_op jit(solution)/shard_map/ppermute | solution.py:431
  46.4 7.0 collective-permute-done.28
  57.6 13.9 %concatenate.62 = bf16[2048,2176]{1,0:T(8,128)(2,1)} concatenate(bf16[2048,512]{1,0:T(8,128)(2,1)} %param.23, bf16[2048,512]{1,0:T(8,128)(2,1)} %param.24, bf16[2048,512]{1,0:T(8,128)(2,1)} %param.25, bf16[2048,512]{1,0:T(8,128)(2,1)} %param.26, bf16[2048,4]{1,0:T(8,128)(2,1)} %copy.41, bf16[2048,4]{1,0:T(8,128)(2,1)} %copy.42, bf16[2048,120]{1,0:T(8,128)(2,1)} %broadcast_in_dim.80), dimensions={1} | concatenate | bytes 17825792 | tf_op jit(solution)/shard_map/concatenate | solution.py:494
  79.3 9.1 %collective-permute-done.5 = bf16[528,512]{1,0:T(8,128)(2,1)S(1)} collective-permute-done((bf16[528,512]{1,0:T(8,128)(2,1)}, bf16[528,512]{1,0:T(8,128)(2,1)S(1)}, u32[]{:S(2)}, u32[]{:S(2)}) %collective-permute-start.5) | collective-permute-done | bytes 540704 | tf_op jit(solution)/shard_map/ppermute | solution.py:431
  94.3 6.6 fusion.100.pre_ref
  100.9 14.6 %mixer_forward.2 = (bf16[512,512]{1,0:T(8,128)(2,1)}, f32[512,512]{1,0:T(8,128)}, f32[512,512]{1,0:T(8,128)}, f32[512,512]{1,0:T(8,128)}) custom-call(f32[512,2176]{1,0:T(8,128)} %fusion.100.pre_ref, f32[3,4,512]{2,1,0:T(4,128)} %conv_ref.7, f32[2,4]{1,0:T(2,128)} %pad_maximum_fusion.7.decay_ref, f32[1,128]{1,0:T(1,128)} %bitcast.113), custom_call_target="tpu_custom_call" | custom-call | flops 10000000000 | bytes 10000000 | tf_op jit(solution)/shard_map/mixer_forward/pallas_call | solution.py:372
  123.8 10.1 %fusion.102.pre_ref = f32[512,2176]{1,0:T(8,128)} fusion(bf16[512,2048]{1,0:T(8,128)(2,1)S(1)} %get-tuple-element.178, bf16[2048,2176]{1,0:T(8,128)(2,1)} %concatenate.62), kind=kOutput, calls=%fused_computation.270 | convolution fusion | flops 4563402752 | bytes 15466496 | tf_op jit(solution)/shard_map/dot_general | solution.py:409
  133.9 14.6 %mixer_forward.3 = (bf16[512,512]{1,0:T(8,128)(2,1)}, f32[512,512]{1,0:T(8,128)}, f32[512,512]{1,0:T(8,128)}, f32[512,512]{1,0:T(8,128)}) custom-call(f32[512,2176]{1,0:T(8,128)} %fusion.102.pre_ref, f32[3,4,512]{2,1,0:T(4,128)} %conv_ref.7, f32[2,4]{1,0:T(2,128)} %pad_maximum_fusion.7.decay_ref, f32[1,128]{1,0:T(1,128)} %bitcast.114), custom_call_target="tpu_custom_call" | custom-call | flops 10000000000 | bytes 10000000 | tf_op jit(solution)/shard_map/mixer_forward/pallas_call | solution.py:372
  205.8 5.6 collective-permute-done.32
  211.4 6.1 collective-permute-done.11
  217.5 5.8 collective-permute-done.35
  227.1 7.7 collective-permute-start.12
  236.3 5.6 constant_dynamic-update-slice_fusion.1
  253.9 9.4 %collective-permute-done.39 = bf16[512,512]{1,0:T(8,128)(2,1)S(1)} collective-permute-done((bf16[512,512]{1,0:T(8,128)(2,1)S(1)}, bf16[512,512]{1,0:T(8,128)(2,1)S(1)}, u32[]{:S(2)}, u32[]{:S(2)}) %collective-permute-start.39) | collective-permute-done | bytes 524320 | tf_op jit(solution)/shard_map/ppermute | solution.py:431
  265.2 9.2 %collective-permute-done.16 = bf16[512,512]{1,0:T(8,128)(2,1)S(1)} collective-permute-done((bf16[512,512]{1,0:T(8,128)(2,1)S(1)}, bf16[512,512]{1,0:T(8,128)(2,1)S(1)}, u32[]{:S(2)}, u32[]{:S(2)}) %collective-permute-start.16) | collective-permute-done | bytes 524320 | tf_op jit(solution)/shard_map/ppermute | solution.py:431
  277.1 8.6 %collective-permute-done.40 = bf16[512,512]{1,0:T(8,128)(2,1)S(1)} collective-permute-done((bf16[512,512]{1,0:T(8,128)(2,1)S(1)}, bf16[512,512]{1,0:T(8,128)(2,1)S(1)}, u32[]{:S(2)}, u32[]{:S(2)}) %collective-permute-start.40) | collective-permute-done | bytes 524320 | tf_op jit(solution)/shard_map/ppermute | solution.py:431
  287.0 9.4 %collective-permute-done.17 = bf16[512,512]{1,0:T(8,128)(2,1)S(1)} collective-permute-done((bf16[512,512]{1,0:T(8,128)(2,1)S(1)}, bf16[512,512]{1,0:T(8,128)(2,1)S(1)}, u32[]{:S(2)}, u32[]{:S(2)}) %collective-permute-start.17) | collective-permute-done | bytes 524320 | tf_op jit(solution)/shard_map/ppermute | solution.py:431
  304.7 7.9 fusion.103
  312.6 7.9 fusion.101
  320.6 9.5 %multiply_convert_fusion.3 = (bf16[512,1408]{1,0:T(8,128)(2,1)S(1)}, bf16[512,1408]{1,0:T(8,128)(2,1)S(1)}, bf16[512,1408]{1,0:T(8,128)(2,1)}) fusion(f32[512,2816]{1,0:T(8,128)} %fusion.101, bf16[512,2048]{1,0:T(8,128)(2,1)S(1)} %get-tuple-element.100, bf16[1408,2048]{1,0:T(8,128)(2,1)} %param.37), kind=kOutput, calls=%fused_computation.85 | convolution fusion | flops 2963603456 | bytes 17956864 | tf_op jit(solution)/shard_map/dot_general | solution.py:419
  331.2 9.1 %convolution_convert_fusion.4 = bf16[512,2048]{1,0:T(8,128)(2,1)S(1)} fusion(bf16[2048,2816]{1,0:T(8,128)(2,1)} %constant_dynamic-update-slice_fusion, bf16[512,1408]{1,0:T(8,128)(2,1)S(1)} %get-tuple-element.93, bf16[512,1408]{1,0:T(8,128)(2,1)S(1)} %get-tuple-element.92), kind=kOutput, calls=%fused_computation.66 | convolution fusion | flops 5912395776 | bytes 16515072 | tf_op jit(solution)/shard_map/dot_general | solution.py:419
  342.2 7.8 multiply_convert_fusion.1
  350.0 9.9 %convolution_convert_fusion.3 = bf16[512,2048]{1,0:T(8,128)(2,1)S(1)} fusion(bf16[2048,2816]{1,0:T(8,128)(2,1)} %constant_dynamic-update-slice_fusion, bf16[512,1408]{1,0:T(8,128)(2,1)} %get-tuple-element.91, bf16[512,1408]{1,0:T(8,128)(2,1)} %get-tuple-element.90), kind=kOutput, calls=%fused_computation.65 | convolution fusion | flops 5912395776 | bytes 16515072 | tf_op jit(solution)/shard_map/dot_general | solution.py:419
  364.2 9.4 %collective-permute-done.69 = bf16[512,512]{1,0:T(8,128)(2,1)S(1)} collective-permute-done((bf16[512,512]{1,0:T(8,128)(2,1)S(1)}, bf16[512,512]{1,0:T(8,128)(2,1)S(1)}, u32[]{:S(2)}, u32[]{:S(2)}) %collective-permute-start.69) | collective-permute-done | bytes 524320 | tf_op jit(solution)/shard_map/ppermute | solution.py:459
  397.4 9.9 %collective-permute-start.71 = (bf16[512,512]{1,0:T(8,128)(2,1)S(1)}, bf16[512,512]{1,0:T(8,128)(2,1)S(1)}, u32[]{:S(2)}, u32[]{:S(2)}) collective-permute-start(bf16[512,512]{1,0:T(8,128)(2,1)S(1)} %get-tuple-element.112), channel_id=1, source_target_pairs={{0,1},{1,2},{2,3},{4,5},{5,6},{6,7},{8,9},{9,10},{10,11},{12,13},{... | collective-permute-start | bytes 1572872 | tf_op jit(solution)/shard_map/ppermute | solution.py:459
  413.3 14.6 %collective-permute-start.54 = (bf16[512,512]{1,0:T(8,128)(2,1)S(1)}, bf16[512,512]{1,0:T(8,128)(2,1)S(1)}, u32[]{:S(2)}, u32[]{:S(2)}) collective-permute-start(bf16[512,512]{1,0:T(8,128)(2,1)S(1)} %fusion.74), channel_id=1, source_target_pairs={{0,1},{1,2},{2,3},{4,5},{5,6},{6,7},{8,9},{9,10},{10,11},{12,13},{... | collective-permute-start | bytes 1572872 | tf_op jit(solution)/shard_map/ppermute | solution.py:428
  429.5 9.6 %collective-permute-start.75 = (bf16[512,512]{1,0:T(8,128)(2,1)S(1)}, bf16[512,512]{1,0:T(8,128)(2,1)S(1)}, u32[]{:S(2)}, u32[]{:S(2)}) collective-permute-start(bf16[512,512]{1,0:T(8,128)(2,1)S(1)} %fusion.75), channel_id=1, source_target_pairs={{0,1},{1,2},{2,3},{4,5},{5,6},{6,7},{8,9},{9,10},{10,11},{12,13},{... | collective-permute-start | bytes 1572872 | tf_op jit(solution)/shard_map/ppermute | solution.py:428
  446.5 7.4 collective-permute-done.78
  455.8 9.2 %collective-permute-done.58 = bf16[512,512]{1,0:T(8,128)(2,1)S(1)} collective-permute-done((bf16[512,512]{1,0:T(8,128)(2,1)S(1)}, bf16[512,512]{1,0:T(8,128)(2,1)S(1)}, u32[]{:S(2)}, u32[]{:S(2)}) %collective-permute-start.58) | collective-permute-done | bytes 524320 | tf_op jit(solution)/shard_map/ppermute | solution.py:431
  467.1 9.2 %collective-permute-done.79 = bf16[512,512]{1,0:T(8,128)(2,1)S(1)} collective-permute-done((bf16[512,512]{1,0:T(8,128)(2,1)S(1)}, bf16[512,512]{1,0:T(8,128)(2,1)S(1)}, u32[]{:S(2)}, u32[]{:S(2)}) %collective-permute-start.79) | collective-permute-done | bytes 524320 | tf_op jit(solution)/shard_map/ppermute | solution.py:431
  478.0 5.9 collective-permute-done.59
  501.0 10.1 %convolution_convert_fusion.2 = bf16[1408,2048]{1,0:T(8,128)(2,1)} fusion(bf16[512,2048]{1,0:T(8,128)(2,1)} %copy-done.5, bf16[512,2048]{1,0:T(8,128)(2,1)} %copy-done.4, bf16[512,1408]{1,0:T(8,128)(2,1)} %get-tuple-element.94, bf16[512,1408]{1,0:T(8,128)(2,1)S(1)} %copy-done.82), kind=kOutput, calls=%fused_computation.2 | convolution fusion | flops 5922619392 | bytes 12845056 | tf_op jit(solution)/shard_map/dot_general | solution.py:413
  517.7 22.0 %mixer_backward.3 = (bf16[512,2176]{1,0:T(8,128)(2,1)}, f32[2,16,512]{2,1,0:T(8,128)}, f32[2,2,4]{2,1,0:T(2,128)}) custom-call(f32[512,2176]{1,0:T(8,128)} %fusion.102.pre_ref, f32[3,4,512]{2,1,0:T(4,128)} %conv_ref.7, f32[2,4]{1,0:T(2,128)} %pad_maximum_fusion.7.decay_ref, f32[1,128]{1,0:T(1,128)} %bitcast.115, f32[512,512]{1,0:T(8,128)} %get-tuple-element.38.inverse_ref, ...), custom_call_target="tpu_custom_call" | custom-call | flops 20000000000 | bytes 20000000 | tf_op jit(solution)/shard_map/mixer_backward/pallas_call | solution.py:390
  539.7 22.4 %mixer_backward.2 = (bf16[512,2176]{1,0:T(8,128)(2,1)}, f32[2,16,512]{2,1,0:T(8,128)}, f32[2,2,4]{2,1,0:T(2,128)}) custom-call(f32[512,2176]{1,0:T(8,128)} %fusion.100.pre_ref, f32[3,4,512]{2,1,0:T(4,128)} %conv_ref.7, f32[2,4]{1,0:T(2,128)} %pad_maximum_fusion.7.decay_ref, f32[1,128]{1,0:T(1,128)} %bitcast.116, f32[512,512]{1,0:T(8,128)} %get-tuple-element.34.inverse_ref, ...), custom_call_target="tpu_custom_call" | custom-call | flops 20000000000 | bytes 20000000 | tf_op jit(solution)/shard_map/mixer_backward/pallas_call | solution.py:390
  562.1 13.8 %convolution_convert_fusion.1 = bf16[2048,2176]{1,0:T(8,128)(2,1)} fusion(bf16[512,2176]{1,0:T(8,128)(2,1)S(1)} %copy-done.24, bf16[512,2176]{1,0:T(8,128)(2,1)} %get-tuple-element.37, bf16[512,2048]{1,0:T(8,128)(2,1)S(1)} %copy-done.29, bf16[512,2048]{1,0:T(8,128)(2,1)S(1)} %copy-done.27), kind=kOutput, calls=%fused_computation.1 | convolution fusion | flops 9148563456 | bytes 17563648 | tf_op jit(solution)/shard_map/dot_general | solution.py:413
  577.5 18.5 %convolution_convert_fusion = bf16[2048,2816]{1,0:T(8,128)(2,1)} fusion(bf16[512,1408]{1,0:T(8,128)(2,1)} %get-tuple-element.91, bf16[512,1408]{1,0:T(8,128)(2,1)} %get-tuple-element.90, bf16[512,1408]{1,0:T(8,128)(2,1)} %copy-done.85, bf16[512,1408]{1,0:T(8,128)(2,1)} %copy-done.84, bf16[512,2048]{1,0:T(8,128)(2,1)} %copy-done.32, ...), kind=kOutput, calls=%fused_computation | convolution fusion | flops 11848384512 | bytes 21495808 | tf_op jit(solution)/shard_map/dot_general | solution.py:413
  597.3 6.3 convolution_convert_fusion.7
  605.2 6.3 convolution_convert_fusion.8
  622.7 5.9 collective-permute-done.18
  633.3 6.6 collective-permute-done.43
  641.0 5.9 collective-permute-start.44
  656.2 12.7 %collective-permute-done.47 = bf16[512,512]{1,0:T(8,128)(2,1)} collective-permute-done((bf16[512,512]{1,0:T(8,128)(2,1)S(1)}, bf16[512,512]{1,0:T(8,128)(2,1)}, u32[]{:S(2)}, u32[]{:S(2)}) %collective-permute-start.47) | collective-permute-done | bytes 524320 | tf_op jit(solution)/shard_map/ppermute | solution.py:460
  670.6 9.1 %convolution_convert_fusion.9 = bf16[512,2048]{1,0:T(8,128)(2,1)S(1)} fusion(bf16[512,2176]{1,0:T(8,128)(2,1)S(1)} %copy-done.25, bf16[2048,2176]{1,0:T(8,128)(2,1)} %concatenate.62), kind=kOutput, calls=%fused_computation.71 | convolution fusion | flops 4564451328 | bytes 13238272 | tf_op jit(solution)/shard_map/dot_general | solution.py:419
  681.4 8.4 %collective-permute-start.81 = (bf16[512,512]{1,0:T(8,128)(2,1)}, bf16[512,512]{1,0:T(8,128)(2,1)S(1)}, u32[]{:S(2)}, u32[]{:S(2)}) collective-permute-start(bf16[512,512]{1,0:T(8,128)(2,1)} %get-tuple-element.110), channel_id=1, source_target_pairs={{0,1},{4,5},{8,9},{12,13},{16,17},{20,21},{24,25},{28,29}} | collective-permute-start | bytes 1572872 | tf_op jit(solution)/shard_map/ppermute | solution.py:459
  707.9 5.7 collective-permute-done.60
  738.8 5.6 collective-permute-start.91
  769.8 15.1 %collective-permute-done.66 = f32[512]{0:T(512)S(1)} collective-permute-done((f32[512]{0:T(512)S(1)}, f32[512]{0:T(512)S(1)}, u32[]{:S(2)}, u32[]{:S(2)}) %collective-permute-start.66) | collective-permute-done | bytes 2080 | tf_op jit(solution)/shard_map/ppermute | solution.py:470
  (509 shorter events, 349.9 us)
Async XLA Ops:
  7.2 801.7 %reduce-scatter.7.cloned.1.call-start = ((), (), s32[]{:S(2)}) async-start(), calls=%async_computation.5 | async-start | bytes 2359296 | tf_op jit(solution)/shard_map/reduce_scatter | solution.py:558
  16.6 25.5 %collective-permute-start.3 = (bf16[528,512]{1,0:T(8,128)(2,1)S(1)}, bf16[528,512]{1,0:T(8,128)(2,1)}, u32[]{:S(2)}, u32[]{:S(2)}) collective-permute-start(bf16[528,512]{1,0:T(8,128)(2,1)S(1)} %maximum_maximum_fusion), channel_id=1, source_target_pairs={{1,0},{2,1},{3,2},{5,4},{6,5},{7,6},{9,8},{10,9},{11,10},{13,12},{... | collective-permute-start | bytes 1622024 | tf_op jit(solution)/shard_map/ppermute | solution.py:431
  17.9 25.5 %collective-permute-start = (bf16[528,512]{1,0:T(8,128)(2,1)S(1)}, bf16[528,512]{1,0:T(8,128)(2,1)}, u32[]{:S(2)}, u32[]{:S(2)}) collective-permute-start(bf16[528,512]{1,0:T(8,128)(2,1)S(1)} %maximum_maximum_fusion), channel_id=1, source_target_pairs={{0,1},{1,2},{2,3},{4,5},{5,6},{6,7},{8,9},{9,10},{10,11},{12,13},{... | collective-permute-start | bytes 1622024 | tf_op jit(solution)/shard_map/ppermute | solution.py:428
  25.9 18.9 %collective-permute-start.25 = (bf16[512,512]{1,0:T(8,128)(2,1)S(1)}, bf16[512,512]{1,0:T(8,128)(2,1)}, u32[]{:S(2)}, u32[]{:S(2)}) collective-permute-start(bf16[512,512]{1,0:T(8,128)(2,1)S(1)} %collective-permute-done.24), channel_id=1, source_target_pairs={{1,2},{2,3},{5,6},{6,7},{9,10},{10,11},{13,14},{14,15},{17,18},{18... | collective-permute-start | bytes 1572872 | tf_op jit(solution)/shard_map/ppermute | solution.py:428
  30.4 22.9 %collective-permute-start.28 = (bf16[512,512]{1,0:T(8,128)(2,1)S(1)}, bf16[512,512]{1,0:T(8,128)(2,1)}, u32[]{:S(2)}, u32[]{:S(2)}) collective-permute-start(bf16[512,512]{1,0:T(8,128)(2,1)S(1)} %collective-permute-done.27), channel_id=1, source_target_pairs={{1,0},{2,1},{5,4},{6,5},{9,8},{10,9},{13,12},{14,13},{17,16},{18,1... | collective-permute-start | bytes 1572872 | tf_op jit(solution)/shard_map/ppermute | solution.py:431
  42.1 31.9 %collective-permute-start.4 = (bf16[528,512]{1,0:T(8,128)(2,1)}, bf16[528,512]{1,0:T(8,128)(2,1)}, u32[]{:S(2)}, u32[]{:S(2)}) collective-permute-start(bf16[528,512]{1,0:T(8,128)(2,1)} %collective-permute-done.3), channel_id=1, source_target_pairs={{1,0},{2,1},{5,4},{6,5},{9,8},{10,9},{13,12},{14,13},{17,16},{18,1... | collective-permute-start | bytes 1622024 | tf_op jit(solution)/shard_map/ppermute | solution.py:431
  43.4 32.0 %collective-permute-start.1 = (bf16[528,512]{1,0:T(8,128)(2,1)}, bf16[528,512]{1,0:T(8,128)(2,1)}, u32[]{:S(2)}, u32[]{:S(2)}) collective-permute-start(bf16[528,512]{1,0:T(8,128)(2,1)} %collective-permute-done), channel_id=1, source_target_pairs={{1,2},{2,3},{5,6},{6,7},{9,10},{10,11},{13,14},{14,15},{17,18},{18... | collective-permute-start | bytes 1622024 | tf_op jit(solution)/shard_map/ppermute | solution.py:428
  44.9 31.5 %collective-permute-start.26 = (bf16[512,512]{1,0:T(8,128)(2,1)}, bf16[512,512]{1,0:T(8,128)(2,1)}, u32[]{:S(2)}, u32[]{:S(2)}) collective-permute-start(bf16[512,512]{1,0:T(8,128)(2,1)} %collective-permute-done.25), channel_id=1, source_target_pairs={{2,3},{6,7},{10,11},{14,15},{18,19},{22,23},{26,27},{30,31}} | collective-permute-start | bytes 1572872 | tf_op jit(solution)/shard_map/ppermute | solution.py:428
  53.3 23.0 %collective-permute-start.29 = (bf16[512,512]{1,0:T(8,128)(2,1)}, bf16[512,512]{1,0:T(8,128)(2,1)}, u32[]{:S(2)}, u32[]{:S(2)}) collective-permute-start(bf16[512,512]{1,0:T(8,128)(2,1)} %collective-permute-done.28), channel_id=1, source_target_pairs={{1,0},{5,4},{9,8},{13,12},{17,16},{21,20},{25,24},{29,28}} | collective-permute-start | bytes 1572872 | tf_op jit(solution)/shard_map/ppermute | solution.py:431
  120.2 36.6 %collective-permute-start.6 = (bf16[512,512]{1,0:T(8,128)(2,1)}, bf16[512,512]{1,0:T(8,128)(2,1)}, u32[]{:S(2)}, u32[]{:S(2)}) collective-permute-start(bf16[512,512]{1,0:T(8,128)(2,1)} %get-tuple-element.126), channel_id=1, source_target_pairs={{0,1},{4,5},{8,9},{12,13},{16,17},{20,21},{24,25},{28,29}} | collective-permute-start | bytes 1572872 | tf_op jit(solution)/shard_map/ppermute | solution.py:459
  155.4 19.2 %collective-permute-start.9 = (bf16[512,512]{1,0:T(8,128)(2,1)}, bf16[512,512]{1,0:T(8,128)(2,1)}, u32[]{:S(2)}, u32[]{:S(2)}) collective-permute-start(bf16[512,512]{1,0:T(8,128)(2,1)} %get-tuple-element.127), channel_id=1, source_target_pairs={{3,2},{7,6},{11,10},{15,14},{19,18},{23,22},{27,26},{31,30}} | collective-permute-start | bytes 1572872 | tf_op jit(solution)/shard_map/ppermute | solution.py:460
  159.0 19.5 %collective-permute-start.7 = (bf16[512,512]{1,0:T(8,128)(2,1)}, bf16[512,512]{1,0:T(8,128)(2,1)}, u32[]{:S(2)}, u32[]{:S(2)}) collective-permute-start(bf16[512,512]{1,0:T(8,128)(2,1)} %add_convert_fusion.33), channel_id=1, source_target_pairs={{0,1},{1,2},{4,5},{5,6},{8,9},{9,10},{12,13},{13,14},{16,17},{17,1... | collective-permute-start | bytes 1572872 | tf_op jit(solution)/shard_map/ppermute | solution.py:459
  161.0 21.7 %collective-permute-start.33 = (bf16[512,512]{1,0:T(8,128)(2,1)}, bf16[512,512]{1,0:T(8,128)(2,1)}, u32[]{:S(2)}, u32[]{:S(2)}) collective-permute-start(bf16[512,512]{1,0:T(8,128)(2,1)} %get-tuple-element.135), channel_id=1, source_target_pairs={{3,2},{7,6},{11,10},{15,14},{19,18},{23,22},{27,26},{31,30}} | collective-permute-start | bytes 1572872 | tf_op jit(solution)/shard_map/ppermute | solution.py:460
  204.1 19.2 %collective-permute-start.35 = (bf16[512,512]{1,0:T(8,128)(2,1)}, bf16[512,512]{1,0:T(8,128)(2,1)}, u32[]{:S(2)}, u32[]{:S(2)}) collective-permute-start(bf16[512,512]{1,0:T(8,128)(2,1)} %add_convert_fusion.21), channel_id=1, source_target_pairs={{3,2},{2,1},{1,0},{7,6},{6,5},{5,4},{11,10},{10,9},{9,8},{15,14},{... | collective-permute-start | bytes 1572872 | tf_op jit(solution)/shard_map/ppermute | solution.py:460
  227.1 20.7 %collective-permute-start.12 = (bf16[512,512]{1,0:T(8,128)(2,1)S(1)}, bf16[512,512]{1,0:T(8,128)(2,1)S(1)}, u32[]{:S(2)}, u32[]{:S(2)}) collective-permute-start(bf16[512,512]{1,0:T(8,128)(2,1)S(1)} %get-tuple-element.86), channel_id=1, source_target_pairs={{0,1},{1,2},{2,3},{4,5},{5,6},{6,7},{8,9},{9,10},{10,11},{12,13},{... | collective-permute-start | bytes 1572872 | tf_op jit(solution)/shard_map/ppermute | solution.py:428
  248.5 26.0 %collective-permute-start.16 = (bf16[512,512]{1,0:T(8,128)(2,1)S(1)}, bf16[512,512]{1,0:T(8,128)(2,1)S(1)}, u32[]{:S(2)}, u32[]{:S(2)}) collective-permute-start(bf16[512,512]{1,0:T(8,128)(2,1)S(1)} %collective-permute-done.15), channel_id=1, source_target_pairs={{1,0},{2,1},{5,4},{6,5},{9,8},{10,9},{13,12},{14,13},{17,16},{18,1... | collective-permute-start | bytes 1572872 | tf_op jit(solution)/shard_map/ppermute | solution.py:431
  253.2 23.2 %collective-permute-start.37 = (bf16[512,512]{1,0:T(8,128)(2,1)S(1)}, bf16[512,512]{1,0:T(8,128)(2,1)S(1)}, u32[]{:S(2)}, u32[]{:S(2)}) collective-permute-start(bf16[512,512]{1,0:T(8,128)(2,1)S(1)} %collective-permute-done.36), channel_id=1, source_target_pairs={{1,2},{2,3},{5,6},{6,7},{9,10},{10,11},{13,14},{14,15},{17,18},{18... | collective-permute-start | bytes 1572872 | tf_op jit(solution)/shard_map/ppermute | solution.py:428
  263.2 22.5 %collective-permute-start.40 = (bf16[512,512]{1,0:T(8,128)(2,1)S(1)}, bf16[512,512]{1,0:T(8,128)(2,1)S(1)}, u32[]{:S(2)}, u32[]{:S(2)}) collective-permute-start(bf16[512,512]{1,0:T(8,128)(2,1)S(1)} %collective-permute-done.39), channel_id=1, source_target_pairs={{1,0},{2,1},{5,4},{6,5},{9,8},{10,9},{13,12},{14,13},{17,16},{18,1... | collective-permute-start | bytes 1572872 | tf_op jit(solution)/shard_map/ppermute | solution.py:431
  264.5 22.5 %collective-permute-start.14 = (bf16[512,512]{1,0:T(8,128)(2,1)S(1)}, bf16[512,512]{1,0:T(8,128)(2,1)S(1)}, u32[]{:S(2)}, u32[]{:S(2)}) collective-permute-start(bf16[512,512]{1,0:T(8,128)(2,1)S(1)} %collective-permute-done.13), channel_id=1, source_target_pairs={{2,3},{6,7},{10,11},{14,15},{18,19},{22,23},{26,27},{30,31}} | collective-permute-start | bytes 1572872 | tf_op jit(solution)/shard_map/ppermute | solution.py:428
  274.5 22.0 %collective-permute-start.17 = (bf16[512,512]{1,0:T(8,128)(2,1)S(1)}, bf16[512,512]{1,0:T(8,128)(2,1)S(1)}, u32[]{:S(2)}, u32[]{:S(2)}) collective-permute-start(bf16[512,512]{1,0:T(8,128)(2,1)S(1)} %collective-permute-done.16), channel_id=1, source_target_pairs={{1,0},{5,4},{9,8},{13,12},{17,16},{21,20},{25,24},{29,28}} | collective-permute-start | bytes 1572872 | tf_op jit(solution)/shard_map/ppermute | solution.py:431
  276.4 20.8 %collective-permute-start.38 = (bf16[512,512]{1,0:T(8,128)(2,1)S(1)}, bf16[512,512]{1,0:T(8,128)(2,1)S(1)}, u32[]{:S(2)}, u32[]{:S(2)}) collective-permute-start(bf16[512,512]{1,0:T(8,128)(2,1)S(1)} %collective-permute-done.37), channel_id=1, source_target_pairs={{2,3},{6,7},{10,11},{14,15},{18,19},{22,23},{26,27},{30,31}} | collective-permute-start | bytes 1572872 | tf_op jit(solution)/shard_map/ppermute | solution.py:428
  340.5 21.5 %collective-permute-start.48 = (bf16[512,512]{1,0:T(8,128)(2,1)S(1)}, bf16[512,512]{1,0:T(8,128)(2,1)S(1)}, u32[]{:S(2)}, u32[]{:S(2)}) collective-permute-start(bf16[512,512]{1,0:T(8,128)(2,1)S(1)} %get-tuple-element.118), channel_id=1, source_target_pairs={{0,1},{4,5},{8,9},{12,13},{16,17},{20,21},{24,25},{28,29}} | collective-permute-start | bytes 1572872 | tf_op jit(solution)/shard_map/ppermute | solution.py:459
  362.2 21.4 %collective-permute-start.49 = (bf16[512,512]{1,0:T(8,128)(2,1)S(1)}, bf16[512,512]{1,0:T(8,128)(2,1)S(1)}, u32[]{:S(2)}, u32[]{:S(2)}) collective-permute-start(bf16[512,512]{1,0:T(8,128)(2,1)S(1)} %add_convert_fusion.15), channel_id=1, source_target_pairs={{0,1},{1,2},{4,5},{5,6},{8,9},{9,10},{12,13},{13,14},{16,17},{17,1... | collective-permute-start | bytes 1572872 | tf_op jit(solution)/shard_map/ppermute | solution.py:459
  363.5 21.1 %collective-permute-start.72 = (bf16[512,512]{1,0:T(8,128)(2,1)S(1)}, bf16[512,512]{1,0:T(8,128)(2,1)S(1)}, u32[]{:S(2)}, u32[]{:S(2)}) collective-permute-start(bf16[512,512]{1,0:T(8,128)(2,1)S(1)} %get-tuple-element.115), channel_id=1, source_target_pairs={{3,2},{7,6},{11,10},{15,14},{19,18},{23,22},{27,26},{31,30}} | collective-permute-start | bytes 1572872 | tf_op jit(solution)/shard_map/ppermute | solution.py:460
  397.4 31.8 %collective-permute-start.71 = (bf16[512,512]{1,0:T(8,128)(2,1)S(1)}, bf16[512,512]{1,0:T(8,128)(2,1)S(1)}, u32[]{:S(2)}, u32[]{:S(2)}) collective-permute-start(bf16[512,512]{1,0:T(8,128)(2,1)S(1)} %get-tuple-element.112), channel_id=1, source_target_pairs={{0,1},{1,2},{2,3},{4,5},{5,6},{6,7},{8,9},{9,10},{10,11},{12,13},{... | collective-permute-start | bytes 1572872 | tf_op jit(solution)/shard_map/ppermute | solution.py:459
  407.5 21.8 %collective-permute-start.74 = (bf16[512,512]{1,0:T(8,128)(2,1)S(1)}, bf16[512,512]{1,0:T(8,128)(2,1)S(1)}, u32[]{:S(2)}, u32[]{:S(2)}) collective-permute-start(bf16[512,512]{1,0:T(8,128)(2,1)S(1)} %add_convert_fusion.4), channel_id=1, source_target_pairs={{3,2},{2,1},{1,0},{7,6},{6,5},{5,4},{11,10},{10,9},{9,8},{15,14},{... | collective-permute-start | bytes 1572872 | tf_op jit(solution)/shard_map/ppermute | solution.py:460
  413.3 27.1 %collective-permute-start.54 = (bf16[512,512]{1,0:T(8,128)(2,1)S(1)}, bf16[512,512]{1,0:T(8,128)(2,1)S(1)}, u32[]{:S(2)}, u32[]{:S(2)}) collective-permute-start(bf16[512,512]{1,0:T(8,128)(2,1)S(1)} %fusion.74), channel_id=1, source_target_pairs={{0,1},{1,2},{2,3},{4,5},{5,6},{6,7},{8,9},{9,10},{10,11},{12,13},{... | collective-permute-start | bytes 1572872 | tf_op jit(solution)/shard_map/ppermute | solution.py:428
  442.6 22.5 %collective-permute-start.58 = (bf16[512,512]{1,0:T(8,128)(2,1)S(1)}, bf16[512,512]{1,0:T(8,128)(2,1)S(1)}, u32[]{:S(2)}, u32[]{:S(2)}) collective-permute-start(bf16[512,512]{1,0:T(8,128)(2,1)S(1)} %collective-permute-done.57), channel_id=1, source_target_pairs={{1,0},{2,1},{5,4},{6,5},{9,8},{10,9},{13,12},{14,13},{17,16},{18,1... | collective-permute-start | bytes 1572872 | tf_op jit(solution)/shard_map/ppermute | solution.py:431
  445.8 20.6 %collective-permute-start.76 = (bf16[512,512]{1,0:T(8,128)(2,1)S(1)}, bf16[512,512]{1,0:T(8,128)(2,1)S(1)}, u32[]{:S(2)}, u32[]{:S(2)}) collective-permute-start(bf16[512,512]{1,0:T(8,128)(2,1)S(1)} %collective-permute-done.75), channel_id=1, source_target_pairs={{1,2},{2,3},{5,6},{6,7},{9,10},{10,11},{13,14},{14,15},{17,18},{18... | collective-permute-start | bytes 1572872 | tf_op jit(solution)/shard_map/ppermute | solution.py:428
  453.8 22.5 %collective-permute-start.79 = (bf16[512,512]{1,0:T(8,128)(2,1)S(1)}, bf16[512,512]{1,0:T(8,128)(2,1)S(1)}, u32[]{:S(2)}, u32[]{:S(2)}) collective-permute-start(bf16[512,512]{1,0:T(8,128)(2,1)S(1)} %collective-permute-done.78), channel_id=1, source_target_pairs={{1,0},{2,1},{5,4},{6,5},{9,8},{10,9},{13,12},{14,13},{17,16},{18,1... | collective-permute-start | bytes 1572872 | tf_op jit(solution)/shard_map/ppermute | solution.py:431
  455.1 22.9 %collective-permute-start.56 = (bf16[512,512]{1,0:T(8,128)(2,1)S(1)}, bf16[512,512]{1,0:T(8,128)(2,1)S(1)}, u32[]{:S(2)}, u32[]{:S(2)}) collective-permute-start(bf16[512,512]{1,0:T(8,128)(2,1)S(1)} %collective-permute-done.55), channel_id=1, source_target_pairs={{2,3},{6,7},{10,11},{14,15},{18,19},{22,23},{26,27},{30,31}} | collective-permute-start | bytes 1572872 | tf_op jit(solution)/shard_map/ppermute | solution.py:428
  501.0 309.7 %reduce-scatter.11.cloned.1.call-start = ((), (), s32[]{:S(2)}) async-start(), calls=%async_computation.7 | async-start | bytes 6488064 | tf_op jit(solution)/shard_map/reduce_scatter | solution.py:558
  511.1 301.9 %reduce-scatter.5.cloned.1.call-start = ((), (), s32[]{:S(2)}) async-start(), calls=%async_computation.4 | async-start | bytes 10027008 | tf_op jit(solution)/shard_map/reduce_scatter | solution.py:558
  575.9 242.2 %reduce-scatter.9.cloned.1.call-start = ((), (), s32[]{:S(2)}) async-start(), calls=%async_computation.6 | async-start | bytes 12976128 | tf_op jit(solution)/shard_map/reduce_scatter | solution.py:558
  612.9 20.4 %collective-permute-start.45 = (bf16[512,512]{1,0:T(8,128)(2,1)S(1)}, bf16[512,512]{1,0:T(8,128)(2,1)S(1)}, u32[]{:S(2)}, u32[]{:S(2)}) collective-permute-start(bf16[512,512]{1,0:T(8,128)(2,1)S(1)} %get-tuple-element.131), channel_id=1, source_target_pairs={{3,2},{7,6},{11,10},{15,14},{19,18},{23,22},{27,26},{31,30}} | collective-permute-start | bytes 1572872 | tf_op jit(solution)/shard_map/ppermute | solution.py:460
  617.6 22.3 %collective-permute-start.43 = (bf16[512,512]{1,0:T(8,128)(2,1)S(1)}, bf16[512,512]{1,0:T(8,128)(2,1)S(1)}, u32[]{:S(2)}, u32[]{:S(2)}) collective-permute-start(bf16[512,512]{1,0:T(8,128)(2,1)S(1)} %add_convert_fusion.20), channel_id=1, source_target_pairs={{0,1},{1,2},{4,5},{5,6},{8,9},{9,10},{12,13},{13,14},{16,17},{17,1... | collective-permute-start | bytes 1572872 | tf_op jit(solution)/shard_map/ppermute | solution.py:459
  622.0 25.0 %collective-permute-start.21 = (bf16[512,512]{1,0:T(8,128)(2,1)S(1)}, bf16[512,512]{1,0:T(8,128)(2,1)S(1)}, u32[]{:S(2)}, u32[]{:S(2)}) collective-permute-start(bf16[512,512]{1,0:T(8,128)(2,1)S(1)} %get-tuple-element.123), channel_id=1, source_target_pairs={{3,2},{7,6},{11,10},{15,14},{19,18},{23,22},{27,26},{31,30}} | collective-permute-start | bytes 1572872 | tf_op jit(solution)/shard_map/ppermute | solution.py:460
  628.8 21.4 %collective-permute-start.19 = (bf16[512,512]{1,0:T(8,128)(2,1)S(1)}, bf16[512,512]{1,0:T(8,128)(2,1)S(1)}, u32[]{:S(2)}, u32[]{:S(2)}) collective-permute-start(bf16[512,512]{1,0:T(8,128)(2,1)S(1)} %add_convert_fusion.29), channel_id=1, source_target_pairs={{0,1},{1,2},{4,5},{5,6},{8,9},{9,10},{12,13},{13,14},{16,17},{17,1... | collective-permute-start | bytes 1572872 | tf_op jit(solution)/shard_map/ppermute | solution.py:459
  681.4 20.9 %collective-permute-start.81 = (bf16[512,512]{1,0:T(8,128)(2,1)}, bf16[512,512]{1,0:T(8,128)(2,1)S(1)}, u32[]{:S(2)}, u32[]{:S(2)}) collective-permute-start(bf16[512,512]{1,0:T(8,128)(2,1)} %get-tuple-element.110), channel_id=1, source_target_pairs={{0,1},{4,5},{8,9},{12,13},{16,17},{20,21},{24,25},{28,29}} | collective-permute-start | bytes 1572872 | tf_op jit(solution)/shard_map/ppermute | solution.py:459
  698.4 58.0 %collective-permute-start.89 = (f32[512]{0:T(512)S(1)}, f32[512]{0:T(512)S(1)}, u32[]{:S(2)}, u32[]{:S(2)}) collective-permute-start(f32[512]{0:T(512)S(1)} %get-tuple-element.182), channel_id=1, source_target_pairs={{0,3},{1,0},{2,1},{3,2},{4,7},{5,4},{6,5},{7,6},{8,11},{9,8},{10,9... | collective-permute-start | bytes 6152 | tf_op jit(solution)/shard_map/ppermute | solution.py:470
  698.5 24.4 %collective-permute-start.84 = (bf16[512,512]{1,0:T(8,128)(2,1)}, bf16[512,512]{1,0:T(8,128)(2,1)S(1)}, u32[]{:S(2)}, u32[]{:S(2)}) collective-permute-start(bf16[512,512]{1,0:T(8,128)(2,1)} %get-tuple-element.111), channel_id=1, source_target_pairs={{3,2},{7,6},{11,10},{15,14},{19,18},{23,22},{27,26},{31,30}} | collective-permute-start | bytes 1572872 | tf_op jit(solution)/shard_map/ppermute | solution.py:460
  699.2 28.3 %collective-permute-start.63 = (bf16[512,512]{1,0:T(8,128)(2,1)}, bf16[512,512]{1,0:T(8,128)(2,1)}, u32[]{:S(2)}, u32[]{:S(2)}) collective-permute-start(bf16[512,512]{1,0:T(8,128)(2,1)} %get-tuple-element.107), channel_id=1, source_target_pairs={{3,2},{7,6},{11,10},{15,14},{19,18},{23,22},{27,26},{31,30}} | collective-permute-start | bytes 1572872 | tf_op jit(solution)/shard_map/ppermute | solution.py:460
  703.5 21.0 %collective-permute-start.82 = (bf16[512,512]{1,0:T(8,128)(2,1)S(1)}, bf16[512,512]{1,0:T(8,128)(2,1)S(1)}, u32[]{:S(2)}, u32[]{:S(2)}) collective-permute-start(bf16[512,512]{1,0:T(8,128)(2,1)S(1)} %add_convert_fusion.3), channel_id=1, source_target_pairs={{0,1},{1,2},{4,5},{5,6},{8,9},{9,10},{12,13},{13,14},{16,17},{17,1... | collective-permute-start | bytes 1572872 | tf_op jit(solution)/shard_map/ppermute | solution.py:459
  722.9 36.5 %collective-permute-start.88 = (f32[512]{0:T(512)S(1)}, f32[512]{0:T(512)S(1)}, u32[]{:S(2)}, u32[]{:S(2)}) collective-permute-start(f32[512]{0:T(512)S(1)} %get-tuple-element.182), channel_id=1, source_target_pairs={{0,2},{1,3},{2,0},{3,1},{4,6},{5,7},{6,4},{7,5},{8,10},{9,11},{10,... | collective-permute-start | bytes 6152 | tf_op jit(solution)/shard_map/ppermute | solution.py:470
  756.5 29.7 %collective-permute-start.83 = (bf16[512,512]{1,0:T(8,128)(2,1)S(1)}, bf16[512,512]{1,0:T(8,128)(2,1)S(1)}, u32[]{:S(2)}, u32[]{:S(2)}) collective-permute-start(bf16[512,512]{1,0:T(8,128)(2,1)S(1)} %copy-done.46), channel_id=1, source_target_pairs={{0,1},{1,2},{2,3},{4,5},{5,6},{6,7},{8,9},{9,10},{10,11},{12,13},{... | collective-permute-start | bytes 1572872 | tf_op jit(solution)/shard_map/ppermute | solution.py:459
  759.5 28.3 %collective-permute-start.62 = (bf16[512,512]{1,0:T(8,128)(2,1)}, bf16[512,512]{1,0:T(8,128)(2,1)S(1)}, u32[]{:S(2)}, u32[]{:S(2)}) collective-permute-start(bf16[512,512]{1,0:T(8,128)(2,1)} %get-tuple-element.104), channel_id=1, source_target_pairs={{0,1},{1,2},{2,3},{4,5},{5,6},{6,7},{8,9},{9,10},{10,11},{12,13},{... | collective-permute-start | bytes 1572872 | tf_op jit(solution)/shard_map/ppermute | solution.py:459
  763.8 23.9 %collective-permute-start.86 = (bf16[512,512]{1,0:T(8,128)(2,1)S(1)}, bf16[512,512]{1,0:T(8,128)(2,1)S(1)}, u32[]{:S(2)}, u32[]{:S(2)}) collective-permute-start(bf16[512,512]{1,0:T(8,128)(2,1)S(1)} %add_convert_fusion), channel_id=1, source_target_pairs={{3,2},{2,1},{1,0},{7,6},{6,5},{5,4},{11,10},{10,9},{9,8},{15,14},{... | collective-permute-start | bytes 1572872 | tf_op jit(solution)/shard_map/ppermute | solution.py:460
  765.1 22.6 %collective-permute-start.65 = (bf16[512,512]{1,0:T(8,128)(2,1)S(1)}, bf16[512,512]{1,0:T(8,128)(2,1)S(1)}, u32[]{:S(2)}, u32[]{:S(2)}) collective-permute-start(bf16[512,512]{1,0:T(8,128)(2,1)S(1)} %add_convert_fusion.8), channel_id=1, source_target_pairs={{3,2},{2,1},{1,0},{7,6},{6,5},{5,4},{11,10},{10,9},{9,8},{15,14},{... | collective-permute-start | bytes 1572872 | tf_op jit(solution)/shard_map/ppermute | solution.py:460
  (153 other events, 4007.0 us)
Sparse Core Ops, SparseCore 0:
  501.1 39.4 reduce-scatter.6
  544.4 59.0 reduce-scatter.10
  607.1 73.7 reduce-scatter.4
  684.3 86.7 reduce-scatter.8

commit v2 on v1

v2 whole, which is shorter than its diff:
```python
import functools
import jax
import jax.numpy as jnp
from jax import lax
from jax.experimental import pallas as pl
from jax.experimental.pallas import tpu as pltpu
from jax.experimental.layout import Layout, with_layout_constraint
from jax.sharding import PartitionSpec as P

SEQ = 256
CH = 128
TAPS = 4
epsilon = 1e-06
f32 = jnp.float32
bf16 = jnp.bfloat16


def halves(x):
    high = x.astype(bf16)
    return high, (x - high.astype(f32)).astype(bf16)


def left(x):
    return jnp.concatenate(halves(x), axis=1)


def right(x):
    row = jnp.concatenate(halves(x), axis=1)
    return jnp.concatenate([row, row], axis=0)


def right_t(x):
    high, low = halves(x)
    return jnp.concatenate(
        [jnp.concatenate([high, high], axis=1), jnp.concatenate([low, low], axis=1)], axis=0
    )


def fold(r):
    return r[:, :CH] + r[:, CH:]


def mm(l, r):
    return fold(jnp.dot(l, r, preferred_element_type=f32))


def mm_t(l, r):
    return fold(lax.dot_general(l, r, (((1,), (1,)), ((), ())), preferred_element_type=f32))


def grids():
    row = lax.broadcasted_iota(jnp.int32, (CH, CH), 0)
    col = lax.broadcasted_iota(jnp.int32, (CH, CH), 1)
    return row, col


def sum_matrix(row, col):
    lower = (row >= col).astype(bf16)
    zero = jnp.zeros((CH, CH), bf16)
    return jnp.concatenate(
        [
            jnp.concatenate([lower, jnp.full((CH, CH), -1, bf16)], axis=1),
            jnp.concatenate([lower, zero], axis=1),
            jnp.concatenate([(row < col).astype(bf16), zero], axis=1),
        ],
        axis=0,
    )


def decay_sums(decay, row, col, sums):
    wide = jnp.broadcast_to(decay, (CH, CH))
    cut = jnp.where(row <= col, wide, 0.0)
    r = jnp.concatenate(
        [jnp.concatenate(halves(wide), axis=1), jnp.concatenate(halves(cut), axis=1)], axis=0
    )
    out = fold(jnp.dot(sums, r, preferred_element_type=f32))
    return out[:CH], out[CH : 2 * CH], out[2 * CH :]


def shifted(x, by, row):
    if by == 0:
        return x
    return jnp.where(row >= by, pltpu.roll(x, by, 0), 0.0)


def shifted_back(x, by, row):
    if by == 0:
        return x
    return jnp.where(row < SEQ - by, pltpu.roll(x, SEQ - by, 0), 0.0)


def sigmoid(x):
    return 0.5 + 0.5 * jnp.tanh(0.5 * x)


def conv_sum(x, taps, row):
    total = x * taps[TAPS - 1 : TAPS]
    for by in range(1, TAPS):
        total = total + shifted(x, by, row) * taps[TAPS - 1 - by : TAPS - by]
    return total


def conv_back(x, grad, taps, row):
    grad_x = grad * taps[TAPS - 1 : TAPS]
    sums = [jnp.sum(grad * x, 0, keepdims=True)]
    for by in range(1, TAPS):
        moved = shifted_back(grad, by, row)
        grad_x = grad_x + moved * taps[TAPS - 1 - by : TAPS - by]
        sums.append(jnp.sum(moved * x, 0, keepdims=True))
    return grad_x, jnp.concatenate(sums[::-1], axis=0)


def norm_of(x):
    return lax.rsqrt(jnp.sum(x * x, -1, keepdims=True) + epsilon)


def softplus(x):
    return jnp.maximum(x, 0.0) + jnp.log(1.0 + jnp.exp(-jnp.abs(x)))


def take_turns(workers):
    while workers:
        workers = [worker for worker in workers if next(worker, workers) is None]


def forward_kernel(
    pre_ref, conv_ref, decay_ref, gain_ref,
    mixed_ref, inverse_ref, update_ref, delta_ref,
):
    heads = decay_ref.shape[1]
    inner = heads * CH

    def piece(index, h):
        return slice(index * inner + h * CH, index * inner + (h + 1) * CH)

    row, col = grids()
    long_row = lax.broadcasted_iota(jnp.int32, (SEQ, CH), 0)
    sums = sum_matrix(row, col)
    within = row >= col
    eye = (row == col).astype(f32)
    ab = pre_ref[:, 4 * inner :]
    decay_all = -jnp.exp(decay_ref[0:1, :]) * softplus(ab[:, :heads] + decay_ref[1:2, :])
    strength_all = sigmoid(ab[:, heads : 2 * heads])
    systems, inverses, kept = [None] * 2 * heads, [None] * 2 * heads, [None] * 2 * heads

    def prepare(h):
        at = slice(h * CH, (h + 1) * CH)
        parts = []
        for index in range(3):
            pre = conv_sum(pre_ref[:, piece(index, h)], conv_ref[index][:, at], long_row)
            parts.append(pre * sigmoid(pre))
        queries = parts[0] * norm_of(parts[0]) * CH ** (-0.5)
        keys = parts[1] * norm_of(parts[1])
        yield
        for c in range(2):
            span = slice(c * CH, (c + 1) * CH)
            q, k, v = queries[span], keys[span], parts[2][span]
            spread, start, tail = decay_sums(decay_all[span, h : h + 1], row, col, sums)
            falloff = jnp.where(within, jnp.exp(jnp.minimum(spread, 0.0)), 0.0)
            k_left = left(k)
            both = mm_t(jnp.concatenate([k_left, left(q)], axis=0), right_t(k))
            yield
            beta = jnp.broadcast_to(strength_all[span, h : h + 1], (CH, CH))
            system = jnp.where(row > col, beta * falloff * both[:CH], 0.0)
            systems[2 * h + c] = system
            inverses[2 * h + c] = eye - jnp.where(
                (row // 2 == col // 2) & (row % 2 > col % 2), system, 0.0
            )
            kept[2 * h + c] = (
                q, k_left, v, k, beta, falloff * both[CH:], jnp.exp(start), jnp.exp(tail)
            )

    take_turns([prepare(h) for h in range(heads)])
    size = 2
    while size < CH:
        mask = (row // (2 * size) == col // (2 * size)) & ((row // size) % 2 > (col // size) % 2)
        steps = [
            mm(left(inverse), right(jnp.where(mask, system, 0.0)))
            for inverse, system in zip(inverses, systems)
        ]
        inverses = [
            inverse - mm(left(step), right(inverse)) for inverse, step in zip(inverses, steps)
        ]
        size *= 2

    def solve(h):
        at = slice(h * CH, (h + 1) * CH)
        q, k_left, v, k, beta, scores, start, tail = kept[2 * h]
        first_update = mm(left(inverses[2 * h]), right(beta * v))
        yield
        first_out = mm(left(scores), right(first_update))
        yield
        state = mm(left(k.T), right(tail * first_update))
        yield
        q, k_left, v, k, beta, scores, start, tail = kept[2 * h + 1]
        read = mm(jnp.concatenate([k_left, left(q)], axis=0), right(state))
        yield
        second_update = mm(left(inverses[2 * h + 1]), right(beta * (v - start * read[:CH])))
        yield
        second_out = start * read[CH:] + mm(left(scores), right(second_update))
        yield
        for c, (update, out) in enumerate(((first_update, first_out), (second_update, second_out))):
            span = slice(c * CH, (c + 1) * CH)
            update_ref[span, at] = update
            delta_ref[span, at] = out
            inverse_ref[span, at] = inverses[2 * h + c].T
            scale = lax.rsqrt(jnp.mean(out * out, -1, keepdims=True) + epsilon)
            gate = pre_ref[span, piece(3, h)]
            mixed_ref[span, at] = (
                out * scale * gain_ref[...] * (gate * sigmoid(gate))
            ).astype(bf16)

    take_turns([solve(h) for h in range(heads)])


def backward_kernel(
    pre_ref, conv_ref, decay_ref, gain_ref,
    inverse_ref, update_ref, delta_ref, grad_ref,
    gpre_ref, gwide_ref, gdecay_ref, gdot_ref,
):
    heads = decay_ref.shape[1]
    inner = heads * CH

    def piece(index, h):
        return slice(index * inner + h * CH, index * inner + (h + 1) * CH)

    row, col = grids()
    long_row = lax.broadcasted_iota(jnp.int32, (SEQ, CH), 0)
    sums = sum_matrix(row, col)
    within = row >= col
    strict = row > col
    upper = (row <= col).astype(bf16)
    upper2 = jnp.concatenate([upper, upper], axis=1)
    lower = strict.astype(bf16)
    lower2 = jnp.concatenate([lower, lower], axis=1)
    ab = pre_ref[:, 4 * inner :]
    rate = -jnp.exp(decay_ref[0:1, :])
    shift = ab[:, :heads] + decay_ref[1:2, :]
    decay_all = rate * softplus(shift)
    strength_all = sigmoid(ab[:, heads : 2 * heads])
    grad_decays, grad_strengths, dots = [None] * heads, [None] * heads, [None] * heads

    def one_head(h):
        at = slice(h * CH, (h + 1) * CH)
        pres, parts = [], []
        for index in range(3):
            pre = conv_sum(pre_ref[:, piece(index, h)], conv_ref[index][:, at], long_row)
            pres.append(pre)
            parts.append(pre * sigmoid(pre))
        q_norm, k_norm = norm_of(parts[0]), norm_of(parts[1])
        queries = parts[0] * q_norm * CH ** (-0.5)
        keys = parts[1] * k_norm
        yield
        out = delta_ref[:, at]
        gate = pre_ref[:, piece(3, h)]
        grad = grad_ref[:, at]
        gain = gain_ref[...]
        scale = lax.rsqrt(jnp.mean(out * out, -1, keepdims=True) + epsilon)
        sig = sigmoid(gate)
        scaled = out * scale
        grad_gate = grad * scaled * gain * sig * (1.0 + gate * (1.0 - sig))
        gpre_ref[:, piece(3, h)] = grad_gate.astype(bf16)
        dots[h] = grad_gate * gate
        grad_normed = grad * gate * sig
        norm_gain_sum = jnp.sum(grad_normed * scaled, 0, keepdims=True)
        grad_scaled = grad_normed * gain
        grad_out = scale * (
            grad_scaled - scaled * jnp.mean(grad_scaled * scaled, -1, keepdims=True)
        )
        yield
        stuff = []
        for c in range(2):
            span = slice(c * CH, (c + 1) * CH)
            q, k, v = queries[span], keys[span], parts[2][span]
            spread, start, tail = decay_sums(decay_all[span, h : h + 1], row, col, sums)
            falloff = jnp.where(within, jnp.exp(jnp.minimum(spread, 0.0)), 0.0)
            q_left, k_left = left(q), left(k)
            both = mm_t(jnp.concatenate([k_left, q_left], axis=0), right_t(k))
            yield
            beta = jnp.broadcast_to(strength_all[span, h : h + 1], (CH, CH))
            stuff.append(
                (q, k, v, falloff, both[:CH] * falloff, both[CH:] * falloff, beta,
                 jnp.exp(start), jnp.exp(tail), q_left, k_left)
            )
        carry = None
        grads_q, grads_k, grads_v, grads_g, grads_b = [None] * 2, [None] * 2, [None] * 2, [None] * 2, [None] * 2
        first_update = update_ref[0:CH, at]
        tail_update = stuff[0][8] * first_update
        state = mm(left(stuff[0][1].T), right(tail_update))
        yield
        for c in (1, 0):
            span = slice(c * CH, (c + 1) * CH)
            q, k, v, falloff, similar, scores, beta, start, tail, q_left, k_left = stuff[c]
            update = update_ref[span, at]
            go = grad_out[span]
            grad_update = mm(left(scores.T), right(go))
            yield
            target = v
            if c == 1:
                read = mm(jnp.concatenate([k_left, q_left], axis=0), right(state))
                yield
                target = v - start * read[:CH]
            else:
                pushed = mm(k_left, right(carry))
                yield
                grad_update = grad_update + tail * pushed
            grad_write = mm(left(inverse_ref[span, at]), right(grad_update))
            yield
            outer = mm_t(
                jnp.concatenate([left(grad_write), left(go)], axis=0), right_t(update)
            )
            yield
            grad_system = jnp.where(strict, -outer[:CH], 0.0)
            grad_scores = jnp.where(within, outer[CH:], 0.0)
            grads_b[c] = jnp.sum(grad_write * target + grad_system * similar, -1, keepdims=True)
            grad_target = beta * grad_write
            grads_v[c] = grad_target
            grad_similar = grad_system * beta * falloff
            grad_dots = grad_scores * falloff
            moved = grad_system * beta * similar + grad_scores * scores
            k_right = right(k)
            back = mm(
                jnp.concatenate(
                    [left(grad_dots), left(grad_similar + grad_similar.T)], axis=0
                ),
                k_right,
            )
            yield
            gq = back[:CH]
            gk = back[CH:] + mm(left(grad_dots.T), right(q))
            yield
            if c == 1:
                through_out, through_read = start * go, -start * grad_target
                more = mm_t(
                    jnp.concatenate([left(through_out), left(through_read)], axis=0),
                    right_t(state),
                )
                yield
                gq = gq + more[:CH]
                gk = gk + more[CH:]
                carry = mm(left(q.T), right(through_out)) + mm(left(k.T), right(through_read))
                yield
                other = through_out * read[CH:] + through_read * read[:CH]
                turned = jnp.dot(
                    upper2,
                    jnp.concatenate(
                        [
                            jnp.concatenate([a, b], axis=1)
                            for a, b in zip(halves(moved), halves(other))
                        ],
                        axis=0,
                    ),
                    preferred_element_type=f32,
                )
                turned = jnp.where(strict, turned[:, :CH], 0.0) + turned[:, CH:]
            else:
                gk = gk + mm_t(left(tail_update), right_t(carry))
                yield
                other = pushed * tail_update
                r1 = jnp.dot(upper2, jnp.concatenate(halves(moved), axis=0), preferred_element_type=f32)
                r2 = jnp.dot(lower2, jnp.concatenate(halves(other), axis=0), preferred_element_type=f32)
                turned = jnp.where(strict, r1, 0.0) + r2
            grads_g[c] = jnp.sum(turned, -1, keepdims=True)
            grads_q[c] = gq
            grads_k[c] = gk
        grad_decays[h] = jnp.concatenate(grads_g, axis=0)
        grad_strengths[h] = jnp.concatenate(grads_b, axis=0)
        gq = jnp.concatenate(grads_q, axis=0)
        gk = jnp.concatenate(grads_k, axis=0)
        gv = jnp.concatenate(grads_v, axis=0)
        yield
        unit = parts[0] * q_norm
        gq = (CH ** (-0.5)) * q_norm * (gq - unit * jnp.sum(gq * unit, -1, keepdims=True))
        gk = k_norm * (gk - keys * jnp.sum(gk * keys, -1, keepdims=True))
        for index, g in enumerate((gq, gk, gv)):
            pre = pres[index]
            sig = sigmoid(pre)
            g = g * sig * (1.0 + pre * (1.0 - sig))
            gx, gw = conv_back(pre_ref[:, piece(index, h)], g, conv_ref[index][:, at], long_row)
            gpre_ref[:, piece(index, h)] = gx.astype(bf16)
            dots[h] = dots[h] + gx * pre_ref[:, piece(index, h)]
            gwide_ref[0, TAPS * index : TAPS * (index + 1), at] = gw
        gwide_ref[0, 3 * TAPS : 3 * TAPS + 1, at] = norm_gain_sum

    take_turns([one_head(h) for h in range(heads)])
    lane = lax.broadcasted_iota(jnp.int32, (SEQ, CH), 1)
    gd = jnp.zeros((SEQ, CH), f32)
    gs = jnp.zeros((SEQ, CH), f32)
    for h in range(heads):
        gd = jnp.where(lane == h, grad_decays[h], gd)
        gs = jnp.where(lane == heads + h, grad_strengths[h], gs)
    sig = sigmoid(ab)
    grad_shift = gd[:, :heads] * rate * sigmoid(shift)
    gab = gs * sig * (1.0 - sig)
    for h in range(heads):
        gab = jnp.where(lane == h, grad_shift[:, h : h + 1], gab)
    gpre_ref[:, 4 * inner :] = gab.astype(bf16)
    total = jnp.where(lane < 2 * heads, gab * ab, 0.0)
    for h in range(heads):
        total = total + dots[h]
    gdot_ref[...] = jnp.sum(total, -1, keepdims=True)
    gdecay_ref[0, 0:1, :] = jnp.sum(gd[:, :heads] * decay_all, 0, keepdims=True)
    gdecay_ref[0, 1:2, :] = jnp.sum(grad_shift, 0, keepdims=True)


def row_spec(width):
    return pl.BlockSpec((SEQ, width), lambda i: (i, 0))


def whole_spec(shape):
    return pl.BlockSpec(shape, lambda i: (0,) * len(shape))


def seq_spec(shape):
    return pl.BlockSpec((1,) + shape, lambda i: (i, 0, 0))


def mixer_forward(pre, conv_weight, decay, gain):
    rows = pre.shape[0]
    heads = decay.shape[1]
    width = heads * CH
    wide = jax.ShapeDtypeStruct((rows, width), f32)
    return pl.pallas_call(
        forward_kernel,
        grid=(rows // SEQ,),
        in_specs=[row_spec(pre.shape[1])]
        + [whole_spec(conv_weight.shape), whole_spec(decay.shape), whole_spec(gain.shape)],
        out_specs=[row_spec(width)] * 4,
        out_shape=[jax.ShapeDtypeStruct((rows, width), bf16), wide, wide, wide],
        compiler_params=pltpu.CompilerParams(vmem_limit_bytes=56 * 2**20),
        cost_estimate=pl.CostEstimate(flops=10**10, bytes_accessed=10**7, transcendentals=0),
        name="mixer_forward",
    )(pre, conv_weight, decay, gain)


def mixer_backward(pre, conv_weight, decay, gain, inverse, update, delta, grad, sequence, shared, slot, slots):
    heads = decay.shape[1]
    width = heads * CH

    def rows(columns):
        return pl.BlockSpec((SEQ, columns), lambda i: (sequence, 0))

    def kernel(*refs):
        backward_kernel(*refs[:8], *refs[-4:])

    operands = [pre, conv_weight, decay, gain, inverse, update, delta, grad]
    in_specs = (
        [rows(pre.shape[1])]
        + [whole_spec(x.shape) for x in (conv_weight, decay, gain)]
        + [rows(width)] * 4
    )
    if shared is not None:
        operands.append(shared)
        in_specs.append(pl.BlockSpec(memory_space=pl.ANY))
    return pl.pallas_call(
        kernel,
        grid=(1,),
        in_specs=in_specs,
        out_specs=[
            pl.BlockSpec((SEQ, pre.shape[1]), lambda i: (slot, 0)),
            seq_spec((16, width)),
            seq_spec((2, heads)),
            pl.BlockSpec((SEQ, 1), lambda i: (0, 0)),
        ],
        out_shape=[
            jax.ShapeDtypeStruct((slots * SEQ, pre.shape[1]), bf16),
            jax.ShapeDtypeStruct((1, 16, width), f32),
            jax.ShapeDtypeStruct((1, 2, heads), f32),
            jax.ShapeDtypeStruct((SEQ, 1), f32),
        ],
        input_output_aliases={} if shared is None else {8: 0},
        compiler_params=pltpu.CompilerParams(vmem_limit_bytes=56 * 2**20),
        cost_estimate=pl.CostEstimate(flops=10**10, bytes_accessed=10**7, transcendentals=0),
        name="mixer_backward",
    )(*operands)


HEAD = "head"
DP = "dp"


def matmul(former, latter, kind=f32):
    return jnp.dot(former, latter, preferred_element_type=f32).astype(kind)


def matmul_rows(former, latter, kind=f32):
    return lax.dot_general(
        former, latter, (((0,), (0,)), ((), ())), preferred_element_type=f32
    ).astype(kind)


def matmul_back(former, latter, kind=f32):
    return lax.dot_general(
        former, latter, (((1,), (1,)), ((), ())), preferred_element_type=f32
    ).astype(kind)


def row_major(x):
    return with_layout_constraint(x, Layout(major_to_minor=tuple(range(x.ndim))))


def ring_order(count):
    return [0] + list(range(1, count, 2)) + [d for d in range(count - 1, 0, -1) if d % 2 == 0]


class Bag:
    pass


class Ring:
    def __init__(self, count):
        self.count = count
        self.order = ring_order(count)
        self.pairs = [(self.order[i], self.order[(i + 1) % count]) for i in range(count)]
        self.me = lax.axis_index(HEAD)
        self.place = self.lookup([self.order.index(d) for d in range(count)], self.me)
        self.bags = []
        self.transfers = []

    def lookup(self, table, index):
        found = jnp.int32(table[0])
        for i in range(1, self.count):
            found = jnp.where(index == i, table[i], found)
        return found

    def bag(self):
        self.bags.append(Bag())
        return self.bags[-1]

    def gather(self, own):
        return Gather(self, own)

    def scatter(self, partial):
        return Scatter(self, partial)

    def tick(self, *landing):
        for transfer in landing:
            transfer.land()
        state = [vars(bag) for bag in self.bags] + [t.state for t in self.transfers]
        flat, tree = jax.tree.flatten(state)
        state = jax.tree.unflatten(tree, lax.optimization_barrier(flat))
        for bag, values in zip(self.bags, state):
            vars(bag).update(values)
        for transfer, values in zip(self.transfers, state[len(self.bags) :]):
            transfer.state = values

    def hops(self, part):
        return [s for s in range(1, self.count) if (s - 1) * 3 // (self.count - 1) == part]

    def send(self, block):
        return lax.ppermute(block, HEAD, self.pairs)


class Gather:
    def __init__(self, ring, own):
        self.ring = ring
        self.state = [own]
        self.air = []
        self.part = 0
        ring.transfers.append(self)

    def hop(self):
        for _ in self.ring.hops(self.part):
            self.air.append(self.ring.send((self.state + self.air)[-1]))
        self.part += 1

    def land(self):
        self.state = self.state + self.air
        self.air = []

    def take(self):
        return jnp.concatenate(self.take_blocks(), axis=1)

    def take_blocks(self):
        self.ring.transfers.remove(self)
        return self.blocks()

    def blocks(self):
        ring = self.ring
        blocks = []
        for block in range(ring.count):
            chosen = self.state[0]
            at = ring.order.index(block)
            for device in range(ring.count):
                back = (ring.order.index(device) - at) % ring.count
                if back:
                    chosen = jnp.where(ring.me == device, self.state[back], chosen)
            blocks.append(chosen)
        return blocks


class Scatter:
    def __init__(self, ring, partial):
        self.ring = ring
        self.state = [partial]
        self.part = 0
        ring.transfers.append(self)

    def block(self, back):
        ring, partial = self.ring, self.state[0]
        width = partial.shape[1] // ring.count
        index = ring.lookup(ring.order, (ring.place + ring.count - back) % ring.count)
        return lax.dynamic_slice_in_dim(partial, index * width, width, axis=1)

    def hop(self):
        for step in self.ring.hops(self.part):
            send = self.block(step)
            if step > 1:
                send = (send.astype(f32) + self.state[1].astype(f32)).astype(bf16)
            self.state = [self.state[0], self.ring.send(send)]
        self.air = self.state.pop()
        self.part += 1

    def land(self):
        self.state = [self.state[0], self.air]

    def take(self):
        self.ring.transfers.remove(self)
        return self.block(0).astype(f32) + self.state[1].astype(f32)


class Cube:
    def __init__(self, total, cut, count, ring):
        self.count = count
        self.me = lax.axis_index(DP)
        bits = list(range(1, count.bit_length() - 1))
        self.halves = [total[:, :cut], total[:, cut:]]
        self.state = []
        self.todo = [bits, bits[::-1]]
        self.left = [list(bits), list(bits)]
        ring.transfers.append(self)

    def pick(self, x, todo, left, flip):
        blocks = 2 ** len(left)
        size = x.shape[0] // blocks
        at = 1 << left.index(todo[0])
        high = (((self.me >> todo[0]) & 1) ^ flip) == 1
        rows = [
            jnp.where(high, x[(i + at) * size : (i + at + 1) * size], x[i * size : (i + 1) * size])
            for i in range(blocks)
            if not i & at
        ]
        return jnp.concatenate(rows, axis=0)

    def hop(self):
        self.air = [
            lax.ppermute(
                self.pick(x, todo, left, 1), DP, [(d, d ^ (1 << todo[0])) for d in range(self.count)]
            )
            for x, todo, left in zip(self.halves, self.todo, self.left)
        ]

    def land(self):
        self.state = self.air

    def add(self):
        halves = []
        for i in range(2):
            x, todo, left, got = self.halves[i], self.todo[i], self.left[i], self.state[i]
            total = self.pick(x, todo, left, 0).astype(f32) + got.astype(f32)
            self.left[i] = [bit for bit in left if bit != todo[0]]
            self.todo[i] = todo[1:]
            halves.append(total.astype(bf16) if self.todo[i] else total)
        self.halves, self.state = halves, []


class Sums:
    def __init__(self, ring, own):
        self.state = [own]
        self.step = 1
        ring.transfers.append(self)

    def around(self, count):
        own = self.state[0]
        self.air = [
            lax.ppermute(own, HEAD, [(d, (d + step) % count) for d in range(count)])
            for step in range(1, count)
        ]

    def double(self, count, times):
        total = self.state[0]
        for _ in range(times):
            if self.step < count:
                total = total + lax.ppermute(total, DP, [(d, d ^ self.step) for d in range(count)])
                self.step *= 2
        self.state, self.air = [], [total]

    def land(self):
        self.state = [sum(self.state + self.air)]


def body(
    block_input, cotangent, seq_count, attn_gain, w_query, w_key, w_value, w_gate,
    w_alpha, w_beta, conv_weight, decay_base, decay_bias, norm_gain, w_out, mlp_gain,
    w_mlp_gate, w_mlp_up, w_down, *, heads_count, groups_count,
):
    micro_count, row_count, width = block_input.shape
    ring = Ring(heads_count)
    every, a, b = ring.bag(), ring.bag(), ring.bag()
    micros = (a, b)
    index = {a: 0, b: 1}
    features = heads_count * width
    heads = decay_base.shape[0]
    hidden_units = w_down.shape[0]
    inner = w_query.shape[1]
    per_micro = row_count // SEQ
    decay = jnp.stack([decay_base, decay_bias])
    gain_row = norm_gain[None]
    attn_own = attn_gain.astype(f32)
    mlp_own = mlp_gain.astype(f32)
    core = lax.axis_index(DP) & 1

    def own_of(values):
        return lax.dynamic_slice_in_dim(values, ring.me * width, width, axis=values.ndim - 1)

    def live_rows(m):
        return (jnp.arange(row_count) // SEQ < seq_count[index[m], 0])[:, None]

    def inputs_own(m):
        return jnp.where(live_rows(m), block_input[index[m]], jnp.zeros((), bf16)).astype(f32)

    def grad_output(m):
        return jnp.where(live_rows(m), cotangent[index[m]], jnp.zeros((), bf16))

    def normalise(m, raw):
        m.low = jnp.where(live_rows(m), raw, jnp.zeros((), bf16))
        inputs = m.low.astype(f32)
        m.scale_in = lax.rsqrt(jnp.mean(inputs * inputs, -1, keepdims=True) + epsilon)
        m.normed = (inputs * m.scale_in * every.gains[:1]).astype(bf16)

    def project(m):
        m.pre = matmul(m.normed, every.w_in)

    def mix(m):
        m.mixed, *m.saved = mixer_forward(m.pre, conv_weight, decay, gain_row)

    def attend(m, mixed):
        m.hidden = m.low.astype(f32) + matmul(mixed, every.w_out)

    def normalise_mid(m):
        hidden = m.hidden
        m.scale_mid = lax.rsqrt(jnp.mean(hidden * hidden, -1, keepdims=True) + epsilon)
        m.normed_mid = (hidden * m.scale_mid * every.gains[1:]).astype(bf16)

    def expand(m):
        m.acts = matmul(m.normed_mid, every.w_up2)

    def activate(m):
        gate_act, up_act = m.acts[:, :hidden_units], m.acts[:, hidden_units:]
        del m.acts
        sig = jax.nn.sigmoid(gate_act)
        silu = gate_act * sig
        m.product = (silu * up_act).astype(bf16)
        grad_product = matmul_back(grad_output(m), w_down)
        grad_gate = (grad_product * up_act * sig * (1.0 + gate_act * (1.0 - sig))).astype(bf16)
        grad_up = (grad_product * silu).astype(bf16)
        m.grad_acts = jnp.concatenate([grad_gate, grad_up], axis=1)

    def back_mid(m):
        m.part_mid = matmul_back(m.grad_acts, every.w_up2, bf16)

    def contract(m):
        m.part_out = matmul(m.product, w_down, bf16)

    def back_hidden(m, grad_mid):
        grad_mid = grad_mid.astype(f32)
        scale, gain = m.scale_mid, every.gains[1:]
        dot_mid = jnp.sum(grad_mid * gain * m.hidden, -1, keepdims=True)
        back = scale**3 * dot_mid / features
        out = grad_output(m)
        m.grad_low = (out.astype(f32) + scale * gain * grad_mid - m.hidden * back).astype(bf16)
        m.grad_hidden_own = (
            own_of(out).astype(f32) + scale * mlp_own * m.grad_mid_own - own_of(m.hidden) * back
        )
        m.grad_mixed = matmul_back(m.grad_low, w_out)

    def mix_back(m, sequence):
        slot = index[m] * per_micro + sequence
        every.grad_pre, wide, decays, dots = mixer_backward(
            m.pre, conv_weight, decay, gain_row, *m.saved, m.grad_mixed, sequence,
            every.grad_pre if slot else None, slot, micro_count * per_micro,
        )
        every.wide = every.wide + wide[0] if slot else wide[0]
        every.decays = every.decays + decays[0] if slot else decays[0]
        m.dots = (m.dots if sequence else []) + [dots[:, 0]]

    def back_in(m):
        grad_pre = every.grad_pre[index[m] * row_count : (index[m] + 1) * row_count]
        m.part_in = matmul_back(grad_pre, every.w_in, bf16)
        m.dot_in = jnp.concatenate(m.dots) / m.scale_in[:, 0]

    def gain_in(m):
        m.gain_in = jnp.sum(m.part_in.astype(f32) * m.low.astype(f32) * m.scale_in, 0)

    def finish_output(m, summed):
        m.output = (own_of(m.hidden) + summed).astype(bf16)

    def finish_input(m, grad_in, dot_in):
        m.input_grad = (
            m.grad_hidden_own
            + m.scale_in * attn_own * grad_in
            - inputs_own(m) * m.scale_in**3 * dot_in[:, None] / features
        )

    def rows_of(former, latter):
        return jnp.concatenate([former, latter], axis=0)

    def by_core(rows, which):
        size = features // groups_count
        return jnp.concatenate(
            [
                jnp.where(which == 1, rows[:, at + size : at + 2 * size], rows[:, at : at + size])
                for at in range(0, features, 2 * size)
            ],
            axis=1,
        )

    in_a = ring.gather(block_input[0])
    slice_rows = w_out.shape[0] // groups_count
    gain_rows = jnp.concatenate([attn_gain, mlp_gain, jnp.zeros((16 * features - 2 * width,), bf16)])
    shares = ring.gather(
        jnp.concatenate(
            [
                lax.dynamic_slice_in_dim(w_out, lax.axis_index(DP) * slice_rows, slice_rows, axis=0),
                gain_rows.reshape(16, features),
            ],
            axis=0,
        )
    )
    every.blocks = block_input
    in_a.hop()
    shares.hop()
    pad = jnp.zeros((features, CH - 2 * heads), bf16)
    last = lax.optimization_barrier(jnp.concatenate([w_alpha, w_beta, pad], axis=1))
    every.w_in = jnp.concatenate([w_query, w_key, w_value, w_gate, last], axis=1)
    ring.tick(in_a, shares)
    in_b = ring.gather(every.blocks[1])
    del every.blocks
    in_a.hop()
    shares.hop()
    ring.tick(in_a, shares)
    in_a.hop()
    shares.hop()
    ring.tick(in_a, shares)
    in_b.hop()
    gain_blocks = [block[slice_rows:] for block in shares.blocks()]
    gain_blocks = [block.reshape(-1)[: 2 * width] for block in gain_blocks]
    every.gains = jnp.stack(
        [
            jnp.concatenate([g[:width] for g in gain_blocks]),
            jnp.concatenate([g[width:] for g in gain_blocks]),
        ]
    ).astype(f32)
    normalise(a, in_a.take())
    project(a)
    ring.tick(in_b)
    in_b.hop()
    w_out_full = lax.all_gather(
        jnp.stack([block[:slice_rows] for block in shares.take_blocks()]), DP, axis=1, tiled=True
    ).reshape(-1, features)
    mix(a)
    every.w_ups = [w_mlp_gate, w_mlp_up]
    ring.tick(in_b)
    in_b.hop()
    mixed_a = ring.gather(a.mixed)
    mixed_a.hop()
    every.w_up2 = jnp.concatenate(every.w_ups, axis=1)
    del every.w_ups
    ring.tick(in_b)
    normalise(b, in_b.take())
    project(b)
    ring.tick(mixed_a)
    mixed_a.hop()
    mix(b)
    ring.tick(mixed_a)
    mixed_a.hop()
    mixed_b = ring.gather(b.mixed)
    mixed_b.hop()
    every.w_out = w_out_full
    ring.tick(mixed_a)
    attend(a, mixed_a.take())
    ring.tick(mixed_b)
    mixed_b.hop()
    normalise_mid(a)
    expand(a)
    ring.tick(mixed_b)
    mixed_b.hop()
    activate(a)
    ring.tick(mixed_b)
    back_mid(a)
    ring.tick()
    mid_a = ring.scatter(a.part_mid)
    del a.part_mid
    mid_a.hop()
    attend(b, mixed_b.take())
    ring.tick(mid_a)
    del every.w_out
    mid_a.hop()
    normalise_mid(b)
    expand(b)
    ring.tick(mid_a)
    mid_a.hop()
    activate(b)
    ring.tick(mid_a)
    a.grad_mid_own = mid_a.take()
    back_a = ring.gather(a.grad_mid_own.astype(bf16))
    back_a.hop()
    back_mid(b)
    ring.tick()
    mid_b = ring.scatter(b.part_mid)
    del b.part_mid
    mid_b.hop()
    every.down = matmul_rows(
        rows_of(a.product, b.product), rows_of(grad_output(a), grad_output(b)), bf16
    )
    ring.tick(back_a)
    down_sum = lax.psum_scatter(every.down, DP, scatter_dimension=1, tiled=True)
    del every.down
    back_a.hop()
    every.up2 = matmul_rows(
        rows_of(a.normed_mid, b.normed_mid), rows_of(a.grad_acts, b.grad_acts), bf16
    )
    ring.tick(mid_b)
    del a.normed_mid, b.normed_mid, a.grad_acts, b.grad_acts
    mid_b.hop()
    contract(a)
    contract(b)
    ring.tick(back_a)
    del a.product, b.product
    back_a.hop()
    normed = rows_of(a.normed, b.normed)
    every.normed_away = by_core(normed, 1 - core)
    every.normed_here = by_core(normed, core)
    ring.tick(mid_b)
    del a.normed, b.normed
    mid_b.hop()
    ring.tick(back_a)
    back_hidden(a, back_a.take())
    ring.tick(mid_b)
    b.grad_mid_own = mid_b.take()
    back_b = ring.gather(b.grad_mid_own.astype(bf16))
    back_b.hop()
    mix_back(a, 0)
    every.down_sum = down_sum
    ring.tick(back_b)
    up2_sum = lax.psum_scatter(every.up2, DP, scatter_dimension=0, tiled=True)
    del every.up2
    back_b.hop()
    for sequence in range(1, per_micro):
        mix_back(a, sequence)
    ring.tick(back_b)
    back_b.hop()
    back_in(a)
    ring.tick(back_b)
    out_a = ring.scatter(a.part_out)
    del a.part_out
    out_a.hop()
    back_hidden(b, back_b.take())
    ring.tick()
    in_grad_a = ring.scatter(a.part_in)
    in_grad_a.hop()
    mix_back(b, 0)
    ring.tick(out_a)
    out_a.hop()
    for sequence in range(1, per_micro):
        mix_back(b, sequence)
    ring.tick(in_grad_a)
    in_grad_a.hop()
    every.away = row_major(matmul_rows(every.normed_away, every.grad_pre, bf16))
    ring.tick(out_a)
    del every.normed_away
    out_a.hop()
    got = lax.ppermute(every.away, DP, [(d, d ^ 1) for d in range(groups_count)])
    del every.away
    back_in(b)
    every.up2_sum = up2_sum
    ring.tick(in_grad_a)
    in_grad_a.hop()
    every.total = row_major(
        (matmul_rows(every.normed_here, every.grad_pre) + got.astype(f32)).astype(bf16)
    )
    ring.tick(out_a)
    del every.normed_here, every.grad_pre
    cube = Cube(every.total, 2 * inner, groups_count, ring)
    del every.total
    cube.hop()
    out_b = ring.scatter(b.part_out)
    del b.part_out
    out_b.hop()
    every.out = matmul_rows(rows_of(a.mixed, b.mixed), rows_of(a.grad_low, b.grad_low), bf16)
    gain_in(a)
    gain_in(b)
    ring.tick(in_grad_a)
    del a.mixed, b.mixed, a.grad_low, b.grad_low
    out_sum = lax.psum_scatter(every.out, DP, scatter_dimension=1, tiled=True)
    del every.out
    in_grad_b = ring.scatter(b.part_in)
    in_grad_b.hop()
    del a.part_in, b.part_in
    taps = 3 * TAPS
    sums = Sums(
        ring,
        jnp.concatenate(
            [
                a.dot_in, b.dot_in, a.gain_in + b.gain_in,
                jnp.sum(every.wide[taps].reshape(heads, CH), 0),
            ]
        ),
    )
    sums.around(heads_count)
    every.mlp_gain = jnp.sum(a.grad_mid_own * own_of(a.hidden) * a.scale_mid, 0) + jnp.sum(
        b.grad_mid_own * own_of(b.hidden) * b.scale_mid, 0
    )
    ring.tick(out_b)
    out_b.hop()
    every.down_grad = every.down_sum.astype(f32)
    every.up2_grad = [
        every.up2_sum[:, :hidden_units].astype(f32), every.up2_sum[:, hidden_units:].astype(f32)
    ]
    del every.down_sum, every.up2_sum
    finish_output(a, out_a.take())
    ring.tick(in_grad_b, sums, cube)
    in_grad_b.hop()
    cube.add()
    while cube.todo[0]:
        cube.hop()
        if len(cube.todo[0]) == 1:
            break
        cube.land()
        cube.add()
    [around] = sums.state
    small = Sums(
        ring,
        jnp.concatenate(
            [
                every.wide[:taps].reshape(-1),
                own_of(around[2 * row_count : 2 * row_count + features]),
                every.mlp_gain,
                jnp.pad(around[2 * row_count + features :], (0, inner - CH)),
                jnp.pad(every.decays.reshape(-1), (0, inner - 2 * heads)),
            ]
        ).reshape(-1, CH),
    )
    small.double(groups_count, 1)
    ring.tick(out_b, small)
    out_b.hop()
    finish_input(a, in_grad_a.take(), around[:row_count])
    ring.tick(in_grad_b, cube)
    in_grad_b.hop()
    small.double(groups_count, groups_count)
    cube.add()
    every.out_sum = out_sum
    ring.tick(out_b, small)
    out_grad = every.out_sum.astype(f32)
    finish_output(b, out_b.take())
    every.outputs = jnp.stack([m.output for m in micros])
    ring.tick(in_grad_b)
    finish_input(b, in_grad_b.take(), around[row_count : 2 * row_count])
    in_query_key, in_others = cube.halves
    small = small.state[0].reshape(-1)
    at = taps * inner
    return (
        every.outputs,
        jnp.stack([m.input_grad for m in micros]),
        small[at : at + width],
        in_query_key[:, :inner],
        in_query_key[:, inner:],
        in_others[:, :inner],
        in_others[:, inner : 2 * inner],
        in_others[:, 2 * inner : 2 * inner + heads],
        in_others[:, 2 * inner + heads : 2 * inner + 2 * heads],
        small[:at].reshape(3, TAPS, inner),
        small[at + 2 * width + inner : at + 2 * width + inner + heads],
        small[at + 2 * width + inner + heads : at + 2 * width + inner + 2 * heads],
        small[at + 2 * width : at + 2 * width + CH],
        out_grad,
        small[at + width : at + 2 * width],
        *every.up2_grad,
        every.down_grad,
    )


def solution(mesh):
    each = P(None, HEAD)
    return jax.shard_map(
        functools.partial(body, heads_count=mesh.shape[HEAD], groups_count=mesh.shape[DP]),
        mesh=mesh,
        in_specs=(
            P(None, DP, HEAD), P(None, DP, None), P(None, DP), P(HEAD),
            each, each, each, each, each, each, P(None, None, HEAD), P(HEAD), P(HEAD),
            P(), P(HEAD, None), P(HEAD), each, each, P(HEAD, None),
        ),
        out_specs=(
            P(None, DP, HEAD), P(None, DP, HEAD), P(HEAD),
            P(DP, HEAD), P(DP, HEAD), P(DP, HEAD), P(DP, HEAD),
            P(DP, HEAD), P(DP, HEAD), P(None, None, HEAD), P(HEAD), P(HEAD),
            P(), P(HEAD, DP), P(HEAD), P(DP, HEAD), P(DP, HEAD), P(HEAD, DP),
        ),
        check_vma=False,
    )
```

time: 834 us -> 575 us (0.69)
  starting transfers between devices: 226 us -> 62.4 us
  waiting for transfers between devices: 230 us -> 121 us
  other arithmetic: 74.5 us -> 105 us
  local copies, waits for them, and re-layouts: 53.9 us -> 32.4 us
    ppermute x96 -> x50, starting transfers between devices: 226 us -> 62.3 us  [the longest x39 52.9 us: send(): return lax.ppermute(block, HEAD, self.pairs)]
    ppermute x96 -> x50, waiting for transfers between devices: 230 us -> 121 us  [the longest x39 111 us: send(): return lax.ppermute(block, HEAD, self.pairs)]
    concatenate x4, local copies, waits for them, and re-layouts: 17.3 us -> 0.35 us  [the longest x1 0.14 us: rows_of(): return jnp.concatenate([former, latter], axis=0)]
    concatenate x2 -> x12, other arithmetic: 0.47 us -> 16.9 us  [the longest x1 9.85 us: body(): every.w_up2 = jnp.concatenate(every.w_ups, axis=1)]
    select_n x8 -> x12, other arithmetic: 6.34 us -> 15.1 us  [the longest x6 9.87 us: blocks(): chosen = jnp.where(ring.me == device, self.state[back], chosen)]
    convert_element_type x33 -> x28, other arithmetic: 44.6 us -> 37.2 us  [the longest x12 16.3 us: hop(): send = (send.astype(f32) + self.state[1].astype(f32)).astype(bf16)]
    dot_general x4 -> x5, matrix products: 46.1 us -> 48.2 us  [matmul_rows(): lax.dot_general(former, latter, (((0,), (0,)), ((), ())), preferred_eleme...]
    unnamed x209 -> x197, local copies, waits for them, and re-layouts: 18.1 us -> 17.2 us
  transfers between devices with their start and end apart: 100 -> 54, of which waited for: 42 -> 21; matrix products, arithmetic and copies ran while one was open for 24% -> 46% of each run, Pallas kernels for 7% -> 12%
where the time goes in v2:
time: 575 us; the launch traced here: 565 us
  matrix products  158 us (27%)
  waiting for transfers between devices  121 us (21%)
  other arithmetic  105 us (18%)
  Pallas kernels  70 us (12%)
  starting transfers between devices  62.4 us (11%)
  local copies, waits for them, and re-layouts  32.4 us (6%)
  between operations  15.9 us (3%)
    ppermute x39, waiting for transfers between devices, send(): return lax.ppermute(block, HEAD, self.pairs)  111 us
    dot_general x8, matrix products, matmul(): return jnp.dot(former, latter, preferred_element_type=f32).astype(kind)  56.1 us
    dot_general x8, matrix products, matmul_back(): lax.dot_general(former, latter, (((1,), (1,)), ((), ())), preferred_eleme...  54.2 us
    ppermute x39, starting transfers between devices, send(): return lax.ppermute(block, HEAD, self.pairs)  52.9 us
    dot_general x5, matrix products, matmul_rows(): lax.dot_general(former, latter, (((0,), (0,)), ((), ())), preferred_eleme...  48.2 us
    pallas_call x4, Pallas kernels, mixer_backward(): pl.pallas_call(kernel, grid=(1,), in_specs=in_specs, out_specs=[pl.BlockS...  44.2 us
    pallas_call x2, Pallas kernels, mixer_forward(): pl.pallas_call(forward_kernel, grid=(rows // SEQ,), in_specs=[row_spec(pr...  25.8 us
    unnamed x197, local copies, waits for them, and re-layouts  17.2 us
  transfers between devices with their start and end apart: 54, of which 21 were waited for; matrix products, arithmetic and copies ran while one was open for 46% of the time, Pallas kernels for 12%

profile of v2, /device:TPU:0, one launch (start us, length us, event | category | flops | bytes accessed | tf_op | source)
XLA Modules:
  0.0 564.7 jit_solution(10547367843911666737)
XLA Ops:
  8.9 3.1 collective-permute-start.1
  22.5 9.5 %collective-permute-done = bf16[512,512]{1,0:T(8,128)(2,1)} collective-permute-done((bf16[512,512]{1,0:T(8,128)(2,1)}, bf16[512,512]{1,0:T(8,128)(2,1)}, u32[]{:S(2)}, u32[]{:S(2)}) %collective-permute-start) | collective-permute-done | bytes 524320 | tf_op jit(solution)/shard_map/ppermute | solution.py:551
  32.8 3.4 collective-permute-start.3
  36.3 17.0 %collective-permute-done.3 = bf16[80,2048]{1,0:T(8,128)(2,1)S(1)} collective-permute-done((bf16[80,2048]{1,0:T(8,128)(2,1)}, bf16[80,2048]{1,0:T(8,128)(2,1)S(1)}, u32[]{:S(2)}, u32[]{:S(2)}) %collective-permute-start.3) | collective-permute-done | bytes 327712 | tf_op jit(solution)/shard_map/ppermute | solution.py:551
  53.9 3.3 collective-permute-start.5
  59.1 14.6 %collective-permute-done.5 = bf16[80,2048]{1,0:T(8,128)(2,1)} collective-permute-done((bf16[80,2048]{1,0:T(8,128)(2,1)S(1)}, bf16[80,2048]{1,0:T(8,128)(2,1)}, u32[]{:S(2)}, u32[]{:S(2)}) %collective-permute-start.5) | collective-permute-done | bytes 327712 | tf_op jit(solution)/shard_map/ppermute | solution.py:551
  81.6 6.6 %fusion.85.pre_ref.refs_0_ = f32[512,2176]{1,0:T(8,128)} fusion(bf16[512,2048]{1,0:T(8,128)(2,1)S(1)} %fusion.5, bf16[2048,2176]{1,0:T(8,128)(2,1)S(1)} %copy-done.57), kind=kOutput, calls=%fused_computation.264 | convolution fusion | flops 4563402752 | bytes 15466496 | tf_op jit(solution)/shard_map/dot_general | solution.py:483
  88.1 2.8 collective-permute-done.6
  95.6 12.9 %mixer_forward.2 = (bf16[512,512]{1,0:T(8,128)(2,1)}, f32[512,512]{1,0:T(8,128)}, f32[512,512]{1,0:T(8,128)}, f32[512,512]{1,0:T(8,128)}) custom-call(f32[512,2176]{1,0:T(8,128)} %fusion.85.pre_ref.refs_0_, f32[3,4,512]{2,1,0:T(4,128)} %refs_1_.7, f32[2,4]{1,0:T(2,128)} %pad_maximum_fusion.17.decay_ref.refs_2_, f32[1,128]{1,0:T(1,128)} %bitcast.173), custom_call_target="tpu_custom_call" | custom-call | flops 10000000000 | bytes 10000000 | tf_op jit(solution)/shard_map/mixer_forward/pallas_call | solution.py:423
  108.6 3.3 collective-permute-start.9
  112.4 9.8 %pad_maximum_fusion = bf16[2048,2816]{1,0:T(8,128)(2,1)} fusion(bf16[2048,1408]{1,0:T(8,128)(2,1)S(1)} %bitcast.131, bf16[2048,1408]{1,0:T(8,128)(2,1)} %param.35), kind=kLoop, calls=%fused_computation | loop fusion | flops 23068672 | bytes 23068672 | tf_op jit(solution)/shard_map/concatenate | solution.py:867
  122.3 9.0 %collective-permute-done.8 = bf16[512,512]{1,0:T(8,128)(2,1)S(1)} collective-permute-done((bf16[512,512]{1,0:T(8,128)(2,1)}, bf16[512,512]{1,0:T(8,128)(2,1)S(1)}, u32[]{:S(2)}, u32[]{:S(2)}) %collective-permute-start.8) | collective-permute-done | bytes 524320 | tf_op jit(solution)/shard_map/ppermute | solution.py:551
  135.8 6.6 %fusion.86.pre_ref.refs_0_ = f32[512,2176]{1,0:T(8,128)} fusion(bf16[512,2048]{1,0:T(8,128)(2,1)S(1)} %fusion.8, bf16[2048,2176]{1,0:T(8,128)(2,1)S(1)} %bitcast.136), kind=kOutput, calls=%fused_computation.265 | convolution fusion | flops 4563402752 | bytes 15466496 | tf_op jit(solution)/shard_map/dot_general | solution.py:483
  144.2 12.9 %mixer_forward.3 = (bf16[512,512]{1,0:T(8,128)(2,1)}, f32[512,512]{1,0:T(8,128)}, f32[512,512]{1,0:T(8,128)}, f32[512,512]{1,0:T(8,128)}) custom-call(f32[512,2176]{1,0:T(8,128)} %fusion.86.pre_ref.refs_0_, f32[3,4,512]{2,1,0:T(4,128)} %refs_1_.7, f32[2,4]{1,0:T(2,128)} %pad_maximum_fusion.17.decay_ref.refs_2_, f32[1,128]{1,0:T(1,128)} %bitcast.174), custom_call_target="tpu_custom_call" | custom-call | flops 10000000000 | bytes 10000000 | tf_op jit(solution)/shard_map/mixer_forward/pallas_call | solution.py:423
  161.6 10.9 %collective-permute-done.11 = bf16[512,512]{1,0:T(8,128)(2,1)} collective-permute-done((bf16[512,512]{1,0:T(8,128)(2,1)S(1)}, bf16[512,512]{1,0:T(8,128)(2,1)}, u32[]{:S(2)}, u32[]{:S(2)}) %collective-permute-start.11) | collective-permute-done | bytes 524320 | tf_op jit(solution)/shard_map/ppermute | solution.py:551
  174.5 7.2 %convert_add_fusion.1 = f32[512,2048]{1,0:T(8,128)S(1)} fusion(bf16[512,2048]{1,0:T(8,128)(2,1)S(1)} %copy-done.6, bf16[2048,2048]{1,0:T(8,128)(2,1)} %bitcast.169, bf16[512,512]{1,0:T(8,128)(2,1)S(1)} %get-tuple-element.2069, bf16[512,512]{1,0:T(8,128)(2,1)S(1)} %get-tuple-element.2070, bf16[512,512]{1,0:T(8,128)(2,1)S(1)} %get-tuple-element.2071, ...), kind=kOutput, calls=%fused_computation.49 | convolution fusion | flops 4305453056 | bytes 16777216 | tf_op jit(solution)/shard_map/dot_general | solution.py:483
  183.7 7.9 %fusion.87 = f32[512,2816]{1,0:T(8,128)} fusion(bf16[512,2048]{1,0:T(8,128)(2,1)S(1)} %multiply_convert_fusion.1, bf16[2048,2816]{1,0:T(8,128)(2,1)S(1)} %bitcast.129), kind=kOutput, calls=%fused_computation.266 | convolution fusion | flops 5905580032 | bytes 19398656 | tf_op jit(solution)/shard_map/dot_general | solution.py:483
  191.6 6.5 %collective-permute-done.13 = bf16[512,512]{1,0:T(8,128)(2,1)S(1)} collective-permute-done((bf16[512,512]{1,0:T(8,128)(2,1)}, bf16[512,512]{1,0:T(8,128)(2,1)S(1)}, u32[]{:S(2)}, u32[]{:S(2)}) %collective-permute-start.13) | collective-permute-done | bytes 524320 | tf_op jit(solution)/shard_map/ppermute | solution.py:551
  198.1 8.9 %multiply_convert_fusion.7 = (bf16[512,1408]{1,0:T(8,128)(2,1)S(1)}, bf16[512,1408]{1,0:T(8,128)(2,1)S(1)}, bf16[512,1408]{1,0:T(8,128)(2,1)}) fusion(f32[512,2816]{1,0:T(8,128)} %fusion.87, bf16[512,2048]{1,0:T(8,128)(2,1)S(1)} %copy-done.13, bf16[1408,2048]{1,0:T(8,128)(2,1)} %param.37), kind=kOutput, calls=%fused_computation.69 | convolution fusion | flops 2963603456 | bytes 17956864 | tf_op jit(solution)/shard_map/dot_general | solution.py:493
  208.5 6.4 %convolution_convert_fusion.4 = bf16[512,2048]{1,0:T(8,128)(2,1)S(1)} fusion(bf16[512,2816]{1,0:T(8,128)(2,1)S(1)} %pad_maximum_fusion.1, bf16[2048,2816]{1,0:T(8,128)(2,1)S(1)} %bitcast.129), kind=kOutput, calls=%fused_computation.52 | convolution fusion | flops 5906628608 | bytes 16515072 | tf_op jit(solution)/shard_map/dot_general | solution.py:493
  217.6 7.0 %convert_add_fusion = f32[512,2048]{1,0:T(8,128)S(1)} fusion(bf16[512,2048]{1,0:T(8,128)(2,1)S(1)} %copy-done.9, bf16[2048,2048]{1,0:T(8,128)(2,1)} %bitcast.170, bf16[512,512]{1,0:T(8,128)(2,1)S(1)} %get-tuple-element.2065, bf16[512,512]{1,0:T(8,128)(2,1)S(1)} %get-tuple-element.2066, bf16[512,512]{1,0:T(8,128)(2,1)S(1)} %get-tuple-element.2067, ...), kind=kOutput, calls=%fused_computation.46 | convolution fusion | flops 4305453056 | bytes 16777216 | tf_op jit(solution)/shard_map/dot_general | solution.py:483
  224.7 4.6 collective-permute-done.15
  230.6 7.9 %fusion.88 = f32[512,2816]{1,0:T(8,128)} fusion(bf16[512,2048]{1,0:T(8,128)(2,1)S(1)} %multiply_convert_fusion, bf16[2048,2816]{1,0:T(8,128)(2,1)S(1)} %bitcast.129), kind=kOutput, calls=%fused_computation.267 | convolution fusion | flops 5905580032 | bytes 19398656 | tf_op jit(solution)/shard_map/dot_general | solution.py:483
  238.5 4.3 collective-permute-done.16
  243.1 8.9 %multiply_convert_fusion.4 = (bf16[512,1408]{1,0:T(8,128)(2,1)S(1)}, bf16[512,1408]{1,0:T(8,128)(2,1)S(1)}, bf16[512,1408]{1,0:T(8,128)(2,1)}) fusion(f32[512,2816]{1,0:T(8,128)} %fusion.88, bf16[512,2048]{1,0:T(8,128)(2,1)S(1)} %copy-done.11, bf16[1408,2048]{1,0:T(8,128)(2,1)} %param.37), kind=kOutput, calls=%fused_computation.64 | convolution fusion | flops 2963603456 | bytes 17956864 | tf_op jit(solution)/shard_map/dot_general | solution.py:493
  252.3 6.7 %collective-permute-done.17 = bf16[512,512]{1,0:T(8,128)(2,1)} collective-permute-done((bf16[512,512]{1,0:T(8,128)(2,1)S(1)}, bf16[512,512]{1,0:T(8,128)(2,1)}, u32[]{:S(2)}, u32[]{:S(2)}) %collective-permute-start.17) | collective-permute-done | bytes 524320 | tf_op jit(solution)/shard_map/ppermute | solution.py:551
  261.1 7.4 %convolution_convert_fusion.3 = bf16[512,2048]{1,0:T(8,128)(2,1)} fusion(bf16[512,2816]{1,0:T(8,128)(2,1)S(1)} %pad_maximum_fusion.2, bf16[2048,2816]{1,0:T(8,128)(2,1)S(1)} %bitcast.129), kind=kOutput, calls=%fused_computation.51 | convolution fusion | flops 5906628608 | bytes 16515072 | tf_op jit(solution)/shard_map/dot_general | solution.py:493
  272.6 8.1 %convolution_convert_fusion.1 = bf16[1408,2048]{1,0:T(8,128)(2,1)} fusion(bf16[512,2048]{1,0:T(8,128)(2,1)S(1)} %copy-done.11, bf16[512,2048]{1,0:T(8,128)(2,1)S(1)} %copy-done.13, bf16[512,1408]{1,0:T(8,128)(2,1)S(1)} %copy-done.78, bf16[512,1408]{1,0:T(8,128)(2,1)S(1)} %copy-done.77), kind=kOutput, calls=%fused_computation.3 | convolution fusion | flops 5922619392 | bytes 12845056 | tf_op jit(solution)/shard_map/dot_general | solution.py:487
  281.3 18.4 %convolution_convert_fusion = bf16[2048,2816]{1,0:T(8,128)(2,1)} fusion(bf16[512,2816]{1,0:T(8,128)(2,1)} %copy-done.30, bf16[512,2816]{1,0:T(8,128)(2,1)} %copy-done.29, bf16[512,2048]{1,0:T(8,128)(2,1)} %copy-done.34, bf16[512,2048]{1,0:T(8,128)(2,1)} %copy-done.33), kind=kOutput, calls=%fused_computation.1 | convolution fusion | flops 11836850176 | bytes 21495808 | tf_op jit(solution)/shard_map/dot_general | solution.py:487
  301.2 2.8 collective-permute-start.21
  304.0 8.2 %convolution_convert_fusion.6 = bf16[512,2048]{1,0:T(8,128)(2,1)} fusion(bf16[512,1408]{1,0:T(8,128)(2,1)} %get-tuple-element.1413, bf16[1408,2048]{1,0:T(8,128)(2,1)} %param.37), kind=kOutput, calls=%fused_computation.54 | convolution fusion | flops 2953838592 | bytes 9306112 | tf_op jit(solution)/shard_map/dot_general | solution.py:483
  312.2 4.6 convolution_convert_fusion.5
  324.6 7.5 %collective-permute-done.22 = bf16[512,512]{1,0:T(8,128)(2,1)S(1)} collective-permute-done((bf16[512,512]{1,0:T(8,128)(2,1)}, bf16[512,512]{1,0:T(8,128)(2,1)S(1)}, u32[]{:S(2)}, u32[]{:S(2)}) %collective-permute-start.22) | collective-permute-done | bytes 524320 | tf_op jit(solution)/shard_map/ppermute | solution.py:551
  342.1 10.9 %mixer_backward.4 = (bf16[1024,2176]{1,0:T(8,128)(2,1)}, f32[1,16,512]{2,1,0:T(8,128)}, f32[1,2,4]{2,1,0:T(2,128)}, f32[256,1]{1,0:T(8,128)}) custom-call(f32[512,2176]{1,0:T(8,128)} %fusion.85.pre_ref.refs_0_, f32[3,4,512]{2,1,0:T(4,128)} %refs_1_.7, f32[2,4]{1,0:T(2,128)} %pad_maximum_fusion.17.decay_ref.refs_2_, f32[1,128]{1,0:T(1,128)} %bitcast.175, ...), custom_call_target="tpu_custom_call" | custom-call | flops 10000000000 | bytes 10000000 | tf_op jit(solution)/shard_map/mixer_backward/pallas_call | solution.py:455
  357.0 11.0 %mixer_backward.5 = (bf16[1024,2176]{1,0:T(8,128)(2,1)}, f32[1,16,512]{2,1,0:T(8,128)}, f32[1,2,4]{2,1,0:T(2,128)}, f32[256,1]{1,0:T(8,128)}) custom-call(f32[512,2176]{1,0:T(8,128)} %fusion.85.pre_ref.refs_0_, f32[3,4,512]{2,1,0:T(4,128)} %refs_1_.7, f32[2,4]{1,0:T(2,128)} %pad_maximum_fusion.17.decay_ref.refs_2_, ...), custom_call_target="tpu_custom_call", output_to_operand_aliasing={{0}: (8, {})} | custom-call | flops 10000000000 | bytes 10000000 | tf_op jit(solution)/shard_map/mixer_backward/pallas_call | solution.py:455
  372.9 8.6 %convolution_convert_fusion.8 = bf16[512,2048]{1,0:T(8,128)(2,1)S(1)} fusion(bf16[2048,2176]{1,0:T(8,128)(2,1)} %copy-done.56, bf16[1024,2176]{1,0:T(8,128)(2,1)} %get-tuple-element.1681.refs_8_), kind=kOutput, calls=%fused_computation.56 | convolution fusion | flops 4564451328 | bytes 13238272 | tf_op jit(solution)/shard_map/dot_general | solution.py:493
  381.5 4.0 collective-permute-done.26
  387.4 2.8 collective-permute-start.27
  400.7 11.3 %mixer_backward.6 = (bf16[1024,2176]{1,0:T(8,128)(2,1)}, f32[1,16,512]{2,1,0:T(8,128)}, f32[1,2,4]{2,1,0:T(2,128)}, f32[256,1]{1,0:T(8,128)}) custom-call(f32[512,2176]{1,0:T(8,128)} %fusion.86.pre_ref.refs_0_, f32[3,4,512]{2,1,0:T(4,128)} %refs_1_.7, f32[2,4]{1,0:T(2,128)} %pad_maximum_fusion.17.decay_ref.refs_2_, ...), custom_call_target="tpu_custom_call", output_to_operand_aliasing={{0}: (8, {})} | custom-call | flops 10000000000 | bytes 10000000 | tf_op jit(solution)/shard_map/mixer_backward/pallas_call | solution.py:455
  416.7 11.0 %mixer_backward.7 = (bf16[1024,2176]{1,0:T(8,128)(2,1)}, f32[1,16,512]{2,1,0:T(8,128)}, f32[1,2,4]{2,1,0:T(2,128)}, f32[256,1]{1,0:T(8,128)}) custom-call(f32[512,2176]{1,0:T(8,128)} %fusion.86.pre_ref.refs_0_, f32[3,4,512]{2,1,0:T(4,128)} %refs_1_.7, f32[2,4]{1,0:T(2,128)} %pad_maximum_fusion.17.decay_ref.refs_2_, ...), custom_call_target="tpu_custom_call", output_to_operand_aliasing={{0}: (8, {})} | custom-call | flops 10000000000 | bytes 10000000 | tf_op jit(solution)/shard_map/mixer_backward/pallas_call | solution.py:455
  430.2 9.3 %convolution_convert_fusion.2 = bf16[1024,2176]{1,0:T(8,128)(2,1)} fusion(bf16[1024,1024]{1,0:T(8,128)(2,1)} %pad_maximum_fusion.3, bf16[1024,2176]{1,0:T(8,128)(2,1)} %get-tuple-element.1813), kind=kOutput, calls=%fused_computation.7 | convolution fusion | flops 4565630976 | bytes 11010048 | tf_op jit(solution)/shard_map/dot_general | solution.py:487
  447.1 9.3 %convolution_convert_fusion.7 = bf16[512,2048]{1,0:T(8,128)(2,1)} fusion(bf16[2048,2176]{1,0:T(8,128)(2,1)} %copy-done.56, bf16[1024,2176]{1,0:T(8,128)(2,1)} %get-tuple-element.1813), kind=kOutput, calls=%fused_computation.55 | convolution fusion | flops 4564451328 | bytes 13238272 | tf_op jit(solution)/shard_map/dot_general | solution.py:493
  459.6 8.6 %add_convert_fusion = bf16[1024,2176]{1,0:T(8,128)(2,1)S(1)} fusion(bf16[1024,2176]{1,0:T(8,128)(2,1)} %collective-permute-done.31, bf16[1024,1024]{1,0:T(8,128)(2,1)} %pad_maximum_fusion.4, bf16[1024,2176]{1,0:T(8,128)(2,1)} %get-tuple-element.1813), kind=kOutput, calls=%fused_computation.2 | convolution fusion | flops 4570087424 | bytes 15466496 | tf_op jit(solution)/shard_map/dot_general | solution.py:487
  470.1 3.0 collective-permute-start.34
  482.8 3.8 fusion.29
  505.2 3.8 collective-permute-done.38
  524.3 5.5 collective-permute-done.45
  529.7 4.2 collective-permute-done.44
  (442 shorter events, 182.7 us)
Async XLA Ops:
  7.2 165.2 %all-gather.2.cloned.1.call-start = ((), (), s32[]{:S(2)}) async-start(), calls=%async_computation.3 | async-start | bytes 9437184 | tf_op jit(solution)/shard_map/all_gather | solution.py:858
  8.9 13.7 %collective-permute-start.1 = (bf16[80,2048]{1,0:T(8,128)(2,1)S(1)}, bf16[80,2048]{1,0:T(8,128)(2,1)}, u32[]{:S(2)}, u32[]{:S(2)}) collective-permute-start(bf16[80,2048]{1,0:T(8,128)(2,1)S(1)} %pad_maximum_fusion.12), channel_id=1, source_target_pairs={{0,1},{1,3},{3,2},{2,0},{4,5},{5,7},{7,6},{6,4},{8,9},{9,11},{11,1... | collective-permute-start | bytes 983048 | tf_op jit(solution)/shard_map/ppermute | solution.py:551
  13.8 18.2 %collective-permute-start = (bf16[512,512]{1,0:T(8,128)(2,1)}, bf16[512,512]{1,0:T(8,128)(2,1)}, u32[]{:S(2)}, u32[]{:S(2)}) collective-permute-start(bf16[512,512]{1,0:T(8,128)(2,1)} %slice_bitcast_fusion.1), channel_id=1, source_target_pairs={{0,1},{1,3},{3,2},{2,0},{4,5},{5,7},{7,6},{6,4},{8,9},{9,11},{11,1... | collective-permute-start | bytes 1572872 | tf_op jit(solution)/shard_map/ppermute | solution.py:551
  32.0 21.2 %collective-permute-start.2 = (bf16[512,512]{1,0:T(8,128)(2,1)}, bf16[512,512]{1,0:T(8,128)(2,1)}, u32[]{:S(2)}, u32[]{:S(2)}) collective-permute-start(bf16[512,512]{1,0:T(8,128)(2,1)} %collective-permute-done), channel_id=1, source_target_pairs={{0,1},{1,3},{3,2},{2,0},{4,5},{5,7},{7,6},{6,4},{8,9},{9,11},{11,1... | collective-permute-start | bytes 1572872 | tf_op jit(solution)/shard_map/ppermute | solution.py:551
  32.8 20.4 %collective-permute-start.3 = (bf16[80,2048]{1,0:T(8,128)(2,1)}, bf16[80,2048]{1,0:T(8,128)(2,1)S(1)}, u32[]{:S(2)}, u32[]{:S(2)}) collective-permute-start(bf16[80,2048]{1,0:T(8,128)(2,1)} %collective-permute-done.1), channel_id=1, source_target_pairs={{0,1},{1,3},{3,2},{2,0},{4,5},{5,7},{7,6},{6,4},{8,9},{9,11},{11,1... | collective-permute-start | bytes 983048 | tf_op jit(solution)/shard_map/ppermute | solution.py:551
  53.3 20.4 %collective-permute-start.4 = (bf16[512,512]{1,0:T(8,128)(2,1)}, bf16[512,512]{1,0:T(8,128)(2,1)}, u32[]{:S(2)}, u32[]{:S(2)}) collective-permute-start(bf16[512,512]{1,0:T(8,128)(2,1)} %collective-permute-done.2), channel_id=1, source_target_pairs={{0,1},{1,3},{3,2},{2,0},{4,5},{5,7},{7,6},{6,4},{8,9},{9,11},{11,1... | collective-permute-start | bytes 1572872 | tf_op jit(solution)/shard_map/ppermute | solution.py:551
  53.9 19.8 %collective-permute-start.5 = (bf16[80,2048]{1,0:T(8,128)(2,1)S(1)}, bf16[80,2048]{1,0:T(8,128)(2,1)}, u32[]{:S(2)}, u32[]{:S(2)}) collective-permute-start(bf16[80,2048]{1,0:T(8,128)(2,1)S(1)} %collective-permute-done.3), channel_id=1, source_target_pairs={{0,1},{1,3},{3,2},{2,0},{4,5},{5,7},{7,6},{6,4},{8,9},{9,11},{11,1... | collective-permute-start | bytes 983048 | tf_op jit(solution)/shard_map/ppermute | solution.py:551
  78.6 12.3 %collective-permute-start.6 = (bf16[512,512]{1,0:T(8,128)(2,1)S(1)}, bf16[512,512]{1,0:T(8,128)(2,1)}, u32[]{:S(2)}, u32[]{:S(2)}) collective-permute-start(bf16[512,512]{1,0:T(8,128)(2,1)S(1)} %slice_bitcast_fusion), channel_id=1, source_target_pairs={{0,1},{1,3},{3,2},{2,0},{4,5},{5,7},{7,6},{6,4},{8,9},{9,11},{11,1... | collective-permute-start | bytes 1572872 | tf_op jit(solution)/shard_map/ppermute | solution.py:551
  94.3 260.8 %reduce-scatter.4.cloned.1.call-start = ((), (), s32[]{:S(2)}) async-start(), calls=%async_computation.4 | async-start | bytes 6488064 | tf_op jit(solution)/shard_map/reduce_scatter | solution.py:917
  95.6 12.9 %collective-permute-start.7 = (bf16[512,512]{1,0:T(8,128)(2,1)}, bf16[512,512]{1,0:T(8,128)(2,1)}, u32[]{:S(2)}, u32[]{:S(2)}) collective-permute-start(bf16[512,512]{1,0:T(8,128)(2,1)} %collective-permute-done.6), channel_id=1, source_target_pairs={{0,1},{1,3},{3,2},{2,0},{4,5},{5,7},{7,6},{6,4},{8,9},{9,11},{11,1... | collective-permute-start | bytes 1572872 | tf_op jit(solution)/shard_map/ppermute | solution.py:551
  108.6 33.8 %collective-permute-start.9 = (bf16[512,512]{1,0:T(8,128)(2,1)}, bf16[512,512]{1,0:T(8,128)(2,1)}, u32[]{:S(2)}, u32[]{:S(2)}) collective-permute-start(bf16[512,512]{1,0:T(8,128)(2,1)} %get-tuple-element.1844), channel_id=1, source_target_pairs={{0,1},{1,3},{3,2},{2,0},{4,5},{5,7},{7,6},{6,4},{8,9},{9,11},{11,1... | collective-permute-start | bytes 1572872 | tf_op jit(solution)/shard_map/ppermute | solution.py:551
  111.9 19.4 %collective-permute-start.8 = (bf16[512,512]{1,0:T(8,128)(2,1)}, bf16[512,512]{1,0:T(8,128)(2,1)S(1)}, u32[]{:S(2)}, u32[]{:S(2)}) collective-permute-start(bf16[512,512]{1,0:T(8,128)(2,1)} %collective-permute-done.7), channel_id=1, source_target_pairs={{0,1},{1,3},{3,2},{2,0},{4,5},{5,7},{7,6},{6,4},{8,9},{9,11},{11,1... | collective-permute-start | bytes 1572872 | tf_op jit(solution)/shard_map/ppermute | solution.py:551
  142.4 14.7 %collective-permute-start.10 = (bf16[512,512]{1,0:T(8,128)(2,1)}, bf16[512,512]{1,0:T(8,128)(2,1)S(1)}, u32[]{:S(2)}, u32[]{:S(2)}) collective-permute-start(bf16[512,512]{1,0:T(8,128)(2,1)} %collective-permute-done.9), channel_id=1, source_target_pairs={{0,1},{1,3},{3,2},{2,0},{4,5},{5,7},{7,6},{6,4},{8,9},{9,11},{11,1... | collective-permute-start | bytes 1572872 | tf_op jit(solution)/shard_map/ppermute | solution.py:551
  157.1 15.3 %collective-permute-start.11 = (bf16[512,512]{1,0:T(8,128)(2,1)S(1)}, bf16[512,512]{1,0:T(8,128)(2,1)}, u32[]{:S(2)}, u32[]{:S(2)}) collective-permute-start(bf16[512,512]{1,0:T(8,128)(2,1)S(1)} %collective-permute-done.10), channel_id=1, source_target_pairs={{0,1},{1,3},{3,2},{2,0},{4,5},{5,7},{7,6},{6,4},{8,9},{9,11},{11,1... | collective-permute-start | bytes 1572872 | tf_op jit(solution)/shard_map/ppermute | solution.py:551
  160.7 21.1 %collective-permute-start.12 = (bf16[512,512]{1,0:T(8,128)(2,1)S(1)}, bf16[512,512]{1,0:T(8,128)(2,1)}, u32[]{:S(2)}, u32[]{:S(2)}) collective-permute-start(bf16[512,512]{1,0:T(8,128)(2,1)S(1)} %copy-done.53), channel_id=1, source_target_pairs={{0,1},{1,3},{3,2},{2,0},{4,5},{5,7},{7,6},{6,4},{8,9},{9,11},{11,1... | collective-permute-start | bytes 1572872 | tf_op jit(solution)/shard_map/ppermute | solution.py:551
  182.5 15.6 %collective-permute-start.13 = (bf16[512,512]{1,0:T(8,128)(2,1)}, bf16[512,512]{1,0:T(8,128)(2,1)S(1)}, u32[]{:S(2)}, u32[]{:S(2)}) collective-permute-start(bf16[512,512]{1,0:T(8,128)(2,1)} %collective-permute-done.12), channel_id=1, source_target_pairs={{0,1},{1,3},{3,2},{2,0},{4,5},{5,7},{7,6},{6,4},{8,9},{9,11},{11,1... | collective-permute-start | bytes 1572872 | tf_op jit(solution)/shard_map/ppermute | solution.py:551
  215.0 14.3 %collective-permute-start.15 = (bf16[512,512]{1,0:T(8,128)(2,1)S(1)}, bf16[512,512]{1,0:T(8,128)(2,1)S(1)}, u32[]{:S(2)}, u32[]{:S(2)}) collective-permute-start(bf16[512,512]{1,0:T(8,128)(2,1)S(1)} %constant_dynamic-slice_fusion.5), channel_id=1, source_target_pairs={{0,1},{1,3},{3,2},{2,0},{4,5},{5,7},{7,6},{6,4},{8,9},{9,11},{11,1... | collective-permute-start | bytes 1572872 | tf_op jit(solution)/shard_map/ppermute | solution.py:551
  229.8 13.0 %collective-permute-start.16 = (bf16[512,512]{1,0:T(8,128)(2,1)S(1)}, bf16[512,512]{1,0:T(8,128)(2,1)S(1)}, u32[]{:S(2)}, u32[]{:S(2)}) collective-permute-start(bf16[512,512]{1,0:T(8,128)(2,1)S(1)} %add_convert_fusion.16), channel_id=1, source_target_pairs={{0,1},{1,3},{3,2},{2,0},{4,5},{5,7},{7,6},{6,4},{8,9},{9,11},{11,1... | collective-permute-start | bytes 1572872 | tf_op jit(solution)/shard_map/ppermute | solution.py:551
  243.0 15.9 %collective-permute-start.17 = (bf16[512,512]{1,0:T(8,128)(2,1)S(1)}, bf16[512,512]{1,0:T(8,128)(2,1)}, u32[]{:S(2)}, u32[]{:S(2)}) collective-permute-start(bf16[512,512]{1,0:T(8,128)(2,1)S(1)} %add_convert_fusion.15), channel_id=1, source_target_pairs={{0,1},{1,3},{3,2},{2,0},{4,5},{5,7},{7,6},{6,4},{8,9},{9,11},{11,1... | collective-permute-start | bytes 1572872 | tf_op jit(solution)/shard_map/ppermute | solution.py:551
  261.1 19.6 %collective-permute-start.18 = (bf16[512,512]{1,0:T(8,128)(2,1)}, bf16[512,512]{1,0:T(8,128)(2,1)}, u32[]{:S(2)}, u32[]{:S(2)}) collective-permute-start(bf16[512,512]{1,0:T(8,128)(2,1)} %get-tuple-element.1509), channel_id=1, source_target_pairs={{0,1},{1,3},{3,2},{2,0},{4,5},{5,7},{7,6},{6,4},{8,9},{9,11},{11,1... | collective-permute-start | bytes 1572872 | tf_op jit(solution)/shard_map/ppermute | solution.py:551
  270.5 29.2 %collective-permute-start.19 = (bf16[512,512]{1,0:T(8,128)(2,1)}, bf16[512,512]{1,0:T(8,128)(2,1)}, u32[]{:S(2)}, u32[]{:S(2)}) collective-permute-start(bf16[512,512]{1,0:T(8,128)(2,1)} %constant_dynamic-slice_fusion.4), channel_id=1, source_target_pairs={{0,1},{1,3},{3,2},{2,0},{4,5},{5,7},{7,6},{6,4},{8,9},{9,11},{11,1... | collective-permute-start | bytes 1572872 | tf_op jit(solution)/shard_map/ppermute | solution.py:551
  280.7 176.0 %reduce-scatter.6.cloned.1.call-start = ((), (), s32[]{:S(2)}) async-start(), calls=%async_computation.5 | async-start | bytes 12976128 | tf_op jit(solution)/shard_map/reduce_scatter | solution.py:946
  280.8 36.1 %collective-permute-start.20 = (bf16[512,512]{1,0:T(8,128)(2,1)}, bf16[512,512]{1,0:T(8,128)(2,1)}, u32[]{:S(2)}, u32[]{:S(2)}) collective-permute-start(bf16[512,512]{1,0:T(8,128)(2,1)} %collective-permute-done.18), channel_id=1, source_target_pairs={{0,1},{1,3},{3,2},{2,0},{4,5},{5,7},{7,6},{6,4},{8,9},{9,11},{11,1... | collective-permute-start | bytes 1572872 | tf_op jit(solution)/shard_map/ppermute | solution.py:551
  301.2 21.0 %collective-permute-start.21 = (bf16[512,512]{1,0:T(8,128)(2,1)S(1)}, bf16[512,512]{1,0:T(8,128)(2,1)S(1)}, u32[]{:S(2)}, u32[]{:S(2)}) collective-permute-start(bf16[512,512]{1,0:T(8,128)(2,1)S(1)} %add_convert_fusion.14), channel_id=1, source_target_pairs={{0,1},{1,3},{3,2},{2,0},{4,5},{5,7},{7,6},{6,4},{8,9},{9,11},{11,1... | collective-permute-start | bytes 1572872 | tf_op jit(solution)/shard_map/ppermute | solution.py:551
  316.8 15.2 %collective-permute-start.22 = (bf16[512,512]{1,0:T(8,128)(2,1)}, bf16[512,512]{1,0:T(8,128)(2,1)S(1)}, u32[]{:S(2)}, u32[]{:S(2)}) collective-permute-start(bf16[512,512]{1,0:T(8,128)(2,1)} %collective-permute-done.20), channel_id=1, source_target_pairs={{0,1},{1,3},{3,2},{2,0},{4,5},{5,7},{7,6},{6,4},{8,9},{9,11},{11,1... | collective-permute-start | bytes 1572872 | tf_op jit(solution)/shard_map/ppermute | solution.py:551
  323.0 17.5 %collective-permute-start.23 = (bf16[512,512]{1,0:T(8,128)(2,1)S(1)}, bf16[512,512]{1,0:T(8,128)(2,1)S(1)}, u32[]{:S(2)}, u32[]{:S(2)}) collective-permute-start(bf16[512,512]{1,0:T(8,128)(2,1)S(1)} %add_convert_fusion.13), channel_id=1, source_target_pairs={{0,1},{1,3},{3,2},{2,0},{4,5},{5,7},{7,6},{6,4},{8,9},{9,11},{11,1... | collective-permute-start | bytes 1572872 | tf_op jit(solution)/shard_map/ppermute | solution.py:551
  341.8 13.2 %collective-permute-start.24 = (bf16[512,512]{1,0:T(8,128)(2,1)}, bf16[512,512]{1,0:T(8,128)(2,1)}, u32[]{:S(2)}, u32[]{:S(2)}) collective-permute-start(bf16[512,512]{1,0:T(8,128)(2,1)} %get-tuple-element.1665), channel_id=1, source_target_pairs={{0,1},{1,3},{3,2},{2,0},{4,5},{5,7},{7,6},{6,4},{8,9},{9,11},{11,1... | collective-permute-start | bytes 1572872 | tf_op jit(solution)/shard_map/ppermute | solution.py:551
  355.1 189.3 %reduce-scatter.8.cloned.1.call-start = ((), (), s32[]{:S(2)}) async-start(), calls=%async_computation.6 | async-start | bytes 2359296 | tf_op jit(solution)/shard_map/reduce_scatter | solution.py:995
  355.2 15.4 %collective-permute-start.25 = (bf16[512,512]{1,0:T(8,128)(2,1)}, bf16[512,512]{1,0:T(8,128)(2,1)}, u32[]{:S(2)}, u32[]{:S(2)}) collective-permute-start(bf16[512,512]{1,0:T(8,128)(2,1)} %collective-permute-done.24), channel_id=1, source_target_pairs={{0,1},{1,3},{3,2},{2,0},{4,5},{5,7},{7,6},{6,4},{8,9},{9,11},{11,1... | collective-permute-start | bytes 1572872 | tf_op jit(solution)/shard_map/ppermute | solution.py:551
  370.5 15.0 %collective-permute-start.26 = (bf16[512,512]{1,0:T(8,128)(2,1)}, bf16[512,512]{1,0:T(8,128)(2,1)S(1)}, u32[]{:S(2)}, u32[]{:S(2)}) collective-permute-start(bf16[512,512]{1,0:T(8,128)(2,1)} %collective-permute-done.25), channel_id=1, source_target_pairs={{0,1},{1,3},{3,2},{2,0},{4,5},{5,7},{7,6},{6,4},{8,9},{9,11},{11,1... | collective-permute-start | bytes 1572872 | tf_op jit(solution)/shard_map/ppermute | solution.py:551
  387.4 27.0 %collective-permute-start.27 = (bf16[512,512]{1,0:T(8,128)(2,1)}, bf16[512,512]{1,0:T(8,128)(2,1)}, u32[]{:S(2)}, u32[]{:S(2)}) collective-permute-start(bf16[512,512]{1,0:T(8,128)(2,1)} %constant_dynamic-slice_fusion.3), channel_id=1, source_target_pairs={{0,1},{1,3},{3,2},{2,0},{4,5},{5,7},{7,6},{6,4},{8,9},{9,11},{11,1... | collective-permute-start | bytes 1572872 | tf_op jit(solution)/shard_map/ppermute | solution.py:551
  399.7 30.5 %collective-permute-start.28 = (bf16[512,512]{1,0:T(8,128)(2,1)}, bf16[512,512]{1,0:T(8,128)(2,1)}, u32[]{:S(2)}, u32[]{:S(2)}) collective-permute-start(bf16[512,512]{1,0:T(8,128)(2,1)} %constant_dynamic-slice_fusion.2), channel_id=1, source_target_pairs={{0,1},{1,3},{3,2},{2,0},{4,5},{5,7},{7,6},{6,4},{8,9},{9,11},{11,1... | collective-permute-start | bytes 1572872 | tf_op jit(solution)/shard_map/ppermute | solution.py:551
  416.5 23.0 %collective-permute-start.29 = (bf16[512,512]{1,0:T(8,128)(2,1)}, bf16[512,512]{1,0:T(8,128)(2,1)}, u32[]{:S(2)}, u32[]{:S(2)}) collective-permute-start(bf16[512,512]{1,0:T(8,128)(2,1)} %add_convert_fusion.12), channel_id=1, source_target_pairs={{0,1},{1,3},{3,2},{2,0},{4,5},{5,7},{7,6},{6,4},{8,9},{9,11},{11,1... | collective-permute-start | bytes 1572872 | tf_op jit(solution)/shard_map/ppermute | solution.py:551
  439.5 20.1 %collective-permute-start.31 = (bf16[1024,2176]{1,0:T(8,128)(2,1)}, bf16[1024,2176]{1,0:T(8,128)(2,1)}, u32[]{:S(2)}, u32[]{:S(2)}) collective-permute-start(bf16[1024,2176]{1,0:T(8,128)(2,1)} %convolution_convert_fusion.2), channel_id=1, source_target_pairs={{0,4},{4,0},{8,12},{12,8},{16,20},{20,16},{24,28},{28,24},{1,5},{5... | collective-permute-start | bytes 13369352 | tf_op jit(solution)/shard_map/ppermute | solution.py:973
  440.9 15.9 %collective-permute-start.30 = (bf16[512,512]{1,0:T(8,128)(2,1)S(1)}, bf16[512,512]{1,0:T(8,128)(2,1)}, u32[]{:S(2)}, u32[]{:S(2)}) collective-permute-start(bf16[512,512]{1,0:T(8,128)(2,1)S(1)} %add_convert_fusion.11), channel_id=1, source_target_pairs={{0,1},{1,3},{3,2},{2,0},{4,5},{5,7},{7,6},{6,4},{8,9},{9,11},{11,1... | collective-permute-start | bytes 1572872 | tf_op jit(solution)/shard_map/ppermute | solution.py:551
  444.5 23.7 %collective-permute-start.32 = (bf16[512,512]{1,0:T(8,128)(2,1)}, bf16[512,512]{1,0:T(8,128)(2,1)}, u32[]{:S(2)}, u32[]{:S(2)}) collective-permute-start(bf16[512,512]{1,0:T(8,128)(2,1)} %add_convert_fusion.10), channel_id=1, source_target_pairs={{0,1},{1,3},{3,2},{2,0},{4,5},{5,7},{7,6},{6,4},{8,9},{9,11},{11,1... | collective-permute-start | bytes 1572872 | tf_op jit(solution)/shard_map/ppermute | solution.py:551
  458.9 27.7 %collective-permute-start.33 = (bf16[512,512]{1,0:T(8,128)(2,1)}, bf16[512,512]{1,0:T(8,128)(2,1)}, u32[]{:S(2)}, u32[]{:S(2)}) collective-permute-start(bf16[512,512]{1,0:T(8,128)(2,1)} %add_convert_fusion.9), channel_id=1, source_target_pairs={{0,1},{1,3},{3,2},{2,0},{4,5},{5,7},{7,6},{6,4},{8,9},{9,11},{11,1... | collective-permute-start | bytes 1572872 | tf_op jit(solution)/shard_map/ppermute | solution.py:551
  470.1 23.7 %collective-permute-start.34 = (bf16[512,512]{1,0:T(8,128)(2,1)}, bf16[512,512]{1,0:T(8,128)(2,1)}, u32[]{:S(2)}, u32[]{:S(2)}) collective-permute-start(bf16[512,512]{1,0:T(8,128)(2,1)} %constant_dynamic-slice_fusion.1), channel_id=1, source_target_pairs={{0,1},{1,3},{3,2},{2,0},{4,5},{5,7},{7,6},{6,4},{8,9},{9,11},{11,1... | collective-permute-start | bytes 1572872 | tf_op jit(solution)/shard_map/ppermute | solution.py:551
  475.3 33.7 %collective-permute-start.35 = (bf16[512,1024]{1,0:T(8,128)(2,1)}, bf16[512,1024]{1,0:T(8,128)(2,1)}, u32[]{:S(2)}, u32[]{:S(2)}) collective-permute-start(bf16[512,1024]{1,0:T(8,128)(2,1)} %pad_maximum_fusion.10), channel_id=1, source_target_pairs={{0,8},{4,12},{8,0},{12,4},{16,24},{20,28},{24,16},{28,20},{1,9},{5... | collective-permute-start | bytes 3145736 | tf_op jit(solution)/shard_map/ppermute | solution.py:647
  477.7 31.3 %collective-permute-start.36 = (bf16[512,1152]{1,0:T(8,128)(2,1)}, bf16[512,1152]{1,0:T(8,128)(2,1)}, u32[]{:S(2)}, u32[]{:S(2)}) collective-permute-start(bf16[512,1152]{1,0:T(8,128)(2,1)} %pad_maximum_fusion.8), channel_id=1, source_target_pairs={{0,16},{4,20},{8,24},{12,28},{16,0},{20,4},{24,8},{28,12},{1,17},{... | collective-permute-start | bytes 3538952 | tf_op jit(solution)/shard_map/ppermute | solution.py:647
  488.6 15.3 %collective-permute-start.39 = (f32[3200]{0:T(1024)S(1)}, f32[3200]{0:T(1024)S(1)}, u32[]{:S(2)}, u32[]{:S(2)}) collective-permute-start(f32[3200]{0:T(1024)S(1)} %pad_maximum_fusion.14), channel_id=1, source_target_pairs={{0,2},{1,3},{2,0},{3,1},{4,6},{5,7},{6,4},{7,5},{8,10},{9,11},{10,... | collective-permute-start | bytes 38408 | tf_op jit(solution)/shard_map/ppermute | solution.py:676
  493.8 15.3 %collective-permute-start.37 = (bf16[512,512]{1,0:T(8,128)(2,1)S(1)}, bf16[512,512]{1,0:T(8,128)(2,1)}, u32[]{:S(2)}, u32[]{:S(2)}) collective-permute-start(bf16[512,512]{1,0:T(8,128)(2,1)S(1)} %constant_dynamic-slice_fusion), channel_id=1, source_target_pairs={{0,1},{1,3},{3,2},{2,0},{4,5},{5,7},{7,6},{6,4},{8,9},{9,11},{11,1... | collective-permute-start | bytes 1572872 | tf_op jit(solution)/shard_map/ppermute | solution.py:551
  503.9 14.7 %collective-permute-start.41 = (bf16[512,512]{1,0:T(8,128)(2,1)}, bf16[512,512]{1,0:T(8,128)(2,1)}, u32[]{:S(2)}, u32[]{:S(2)}) collective-permute-start(bf16[512,512]{1,0:T(8,128)(2,1)} %add_convert_fusion.7), channel_id=1, source_target_pairs={{0,1},{1,3},{3,2},{2,0},{4,5},{5,7},{7,6},{6,4},{8,9},{9,11},{11,1... | collective-permute-start | bytes 1572872 | tf_op jit(solution)/shard_map/ppermute | solution.py:551
  512.5 17.2 %collective-permute-start.45 = (bf16[512,512]{1,0:T(8,128)(2,1)S(1)}, bf16[512,512]{1,0:T(8,128)(2,1)S(1)}, u32[]{:S(2)}, u32[]{:S(2)}) collective-permute-start(bf16[512,512]{1,0:T(8,128)(2,1)S(1)} %add_convert_fusion.6), channel_id=1, source_target_pairs={{0,1},{1,3},{3,2},{2,0},{4,5},{5,7},{7,6},{6,4},{8,9},{9,11},{11,1... | collective-permute-start | bytes 1572872 | tf_op jit(solution)/shard_map/ppermute | solution.py:551
  512.8 16.9 %collective-permute-start.43 = (bf16[256,1024]{1,0:T(8,128)(2,1)S(1)}, bf16[256,1024]{1,0:T(8,128)(2,1)S(1)}, u32[]{:S(2)}, u32[]{:S(2)}) collective-permute-start(bf16[256,1024]{1,0:T(8,128)(2,1)S(1)} %broadcast_select_fusion.7), channel_id=1, source_target_pairs={{0,16},{4,20},{8,24},{12,28},{16,0},{20,4},{24,8},{28,12},{1,17},{... | collective-permute-start | bytes 1572872 | tf_op jit(solution)/shard_map/ppermute | solution.py:647
  515.9 18.0 %collective-permute-start.44 = (bf16[256,1152]{1,0:T(8,128)(2,1)S(1)}, bf16[256,1152]{1,0:T(8,128)(2,1)S(1)}, u32[]{:S(2)}, u32[]{:S(2)}) collective-permute-start(bf16[256,1152]{1,0:T(8,128)(2,1)S(1)} %broadcast_select_fusion.2), channel_id=1, source_target_pairs={{0,8},{4,12},{8,0},{12,4},{16,24},{20,28},{24,16},{28,20},{1,9},{5... | collective-permute-start | bytes 1769480 | tf_op jit(solution)/shard_map/ppermute | solution.py:647
  520.7 23.7 %collective-permute-start.46 = (bf16[512,512]{1,0:T(8,128)(2,1)}, bf16[512,512]{1,0:T(8,128)(2,1)}, u32[]{:S(2)}, u32[]{:S(2)}) collective-permute-start(bf16[512,512]{1,0:T(8,128)(2,1)} %add_convert_fusion.5), channel_id=1, source_target_pairs={{0,1},{1,3},{3,2},{2,0},{4,5},{5,7},{7,6},{6,4},{8,9},{9,11},{11,1... | collective-permute-start | bytes 1572872 | tf_op jit(solution)/shard_map/ppermute | solution.py:551
  538.1 13.7 %collective-permute-start.49 = (bf16[512,512]{1,0:T(8,128)(2,1)}, bf16[512,512]{1,0:T(8,128)(2,1)}, u32[]{:S(2)}, u32[]{:S(2)}) collective-permute-start(bf16[512,512]{1,0:T(8,128)(2,1)} %add_convert_fusion.3), channel_id=1, source_target_pairs={{0,1},{1,3},{3,2},{2,0},{4,5},{5,7},{7,6},{6,4},{8,9},{9,11},{11,1... | collective-permute-start | bytes 1572872 | tf_op jit(solution)/shard_map/ppermute | solution.py:551
  (97 other events, 1060.7 us)
Sparse Core Ops, SparseCore 0:
  94.4 54.7 all-gather.1
  280.8 58.9 reduce-scatter.3
  355.2 86.7 reduce-scatter.5
  489.6 44.8 reduce-scatter.7

commit v3 on v2

--- a/solution.py
+++ b/solution.py
@@ -215,7 +215,7 @@
 
 def backward_kernel(
     pre_ref, conv_ref, decay_ref, gain_ref,
-    inverse_ref, update_ref, delta_ref, grad_ref,
+    inverse_ref, update_ref, delta_ref, grad_ref, wide_ref, sums_ref,
     gpre_ref, gwide_ref, gdecay_ref, gdot_ref,
 ):
     heads = decay_ref.shape[1]
@@ -379,8 +379,10 @@
             gx, gw = conv_back(pre_ref[:, piece(index, h)], g, conv_ref[index][:, at], long_row)
             gpre_ref[:, piece(index, h)] = gx.astype(bf16)
             dots[h] = dots[h] + gx * pre_ref[:, piece(index, h)]
-            gwide_ref[0, TAPS * index : TAPS * (index + 1), at] = gw
-        gwide_ref[0, 3 * TAPS : 3 * TAPS + 1, at] = norm_gain_sum
+            taps = slice(TAPS * index, TAPS * (index + 1))
+            gwide_ref[taps, at] = wide_ref[taps, at] + gw
+        last = slice(3 * TAPS, 3 * TAPS + 1)
+        gwide_ref[last, at] = wide_ref[last, at] + norm_gain_sum
 
     take_turns([one_head(h) for h in range(heads)])
     lane = lax.broadcasted_iota(jnp.int32, (SEQ, CH), 1)
@@ -399,8 +401,8 @@
     for h in range(heads):
         total = total + dots[h]
     gdot_ref[...] = jnp.sum(total, -1, keepdims=True)
-    gdecay_ref[0, 0:1, :] = jnp.sum(gd[:, :heads] * decay_all, 0, keepdims=True)
-    gdecay_ref[0, 1:2, :] = jnp.sum(grad_shift, 0, keepdims=True)
+    gdecay_ref[0:1, :] = sums_ref[0:1, :] + jnp.sum(gd[:, :heads] * decay_all, 0, keepdims=True)
+    gdecay_ref[1:2, :] = sums_ref[1:2, :] + jnp.sum(grad_shift, 0, keepdims=True)
 
 
 def row_spec(width):
@@ -409,10 +411,6 @@
 
 def whole_spec(shape):
     return pl.BlockSpec(shape, lambda i: (0,) * len(shape))
-
-
-def seq_spec(shape):
-    return pl.BlockSpec((1,) + shape, lambda i: (i, 0, 0))
 
 
 def mixer_forward(pre, conv_weight, decay, gain):
@@ -433,7 +431,9 @@
     )(pre, conv_weight, decay, gain)
 
 
-def mixer_backward(pre, conv_weight, decay, gain, inverse, update, delta, grad, sequence, shared, slot, slots):
+def mixer_backward(
+    pre, conv_weight, decay, gain, inverse, update, delta, grad, wide, sums, sequence, shared, slot, slots
+):
     heads = decay.shape[1]
     width = heads * CH
 
@@ -441,13 +441,14 @@
         return pl.BlockSpec((SEQ, columns), lambda i: (sequence, 0))
 
     def kernel(*refs):
-        backward_kernel(*refs[:8], *refs[-4:])
-
-    operands = [pre, conv_weight, decay, gain, inverse, update, delta, grad]
+        backward_kernel(*refs[:10], *refs[-4:])
+
+    operands = [pre, conv_weight, decay, gain, inverse, update, delta, grad, wide, sums]
     in_specs = (
         [rows(pre.shape[1])]
         + [whole_spec(x.shape) for x in (conv_weight, decay, gain)]
         + [rows(width)] * 4
+        + [whole_spec(wide.shape), whole_spec(sums.shape)]
     )
     if shared is not None:
         operands.append(shared)
@@ -458,17 +459,17 @@
         in_specs=in_specs,
         out_specs=[
             pl.BlockSpec((SEQ, pre.shape[1]), lambda i: (slot, 0)),
-            seq_spec((16, width)),
-            seq_spec((2, heads)),
+            whole_spec(wide.shape),
+            whole_spec(sums.shape),
             pl.BlockSpec((SEQ, 1), lambda i: (0, 0)),
         ],
         out_shape=[
             jax.ShapeDtypeStruct((slots * SEQ, pre.shape[1]), bf16),
-            jax.ShapeDtypeStruct((1, 16, width), f32),
-            jax.ShapeDtypeStruct((1, 2, heads), f32),
+            jax.ShapeDtypeStruct(wide.shape, f32),
+            jax.ShapeDtypeStruct(sums.shape, f32),
             jax.ShapeDtypeStruct((SEQ, 1), f32),
         ],
-        input_output_aliases={} if shared is None else {8: 0},
+        input_output_aliases={} if shared is None else {10: 0},
         compiler_params=pltpu.CompilerParams(vmem_limit_bytes=56 * 2**20),
         cost_estimate=pl.CostEstimate(flops=10**10, bytes_accessed=10**7, transcendentals=0),
         name="mixer_backward",
@@ -751,7 +752,8 @@
         sig = jax.nn.sigmoid(gate_act)
         silu = gate_act * sig
         m.product = (silu * up_act).astype(bf16)
-        grad_product = matmul_back(grad_output(m), w_down)
+        grad_product = m.grad_product.astype(f32)
+        del m.grad_product
         grad_gate = (grad_product * up_act * sig * (1.0 + gate_act * (1.0 - sig))).astype(bf16)
         grad_up = (grad_product * silu).astype(bf16)
         m.grad_acts = jnp.concatenate([grad_gate, grad_up], axis=1)
@@ -776,18 +778,17 @@
 
     def mix_back(m, sequence):
         slot = index[m] * per_micro + sequence
-        every.grad_pre, wide, decays, dots = mixer_backward(
-            m.pre, conv_weight, decay, gain_row, *m.saved, m.grad_mixed, sequence,
-            every.grad_pre if slot else None, slot, micro_count * per_micro,
+        every.grad_pre, every.wide, every.decays, dots = mixer_backward(
+            m.pre, conv_weight, decay, gain_row, *m.saved, m.grad_mixed,
+            every.wide if slot else jnp.zeros((16, inner), f32),
+            every.decays if slot else jnp.zeros((2, heads), f32),
+            sequence, every.grad_pre if slot else None, slot, micro_count * per_micro,
         )
-        every.wide = every.wide + wide[0] if slot else wide[0]
-        every.decays = every.decays + decays[0] if slot else decays[0]
-        m.dots = (m.dots if sequence else []) + [dots[:, 0]]
+        m.dots = (m.dots if sequence else []) + [dots]
 
     def back_in(m):
         grad_pre = every.grad_pre[index[m] * row_count : (index[m] + 1) * row_count]
         m.part_in = matmul_back(grad_pre, every.w_in, bf16)
-        m.dot_in = jnp.concatenate(m.dots) / m.scale_in[:, 0]
 
     def gain_in(m):
         m.gain_in = jnp.sum(m.part_in.astype(f32) * m.low.astype(f32) * m.scale_in, 0)
@@ -817,12 +818,12 @@
 
     in_a = ring.gather(block_input[0])
     slice_rows = w_out.shape[0] // groups_count
-    gain_rows = jnp.concatenate([attn_gain, mlp_gain, jnp.zeros((16 * features - 2 * width,), bf16)])
+    gain_rows = jnp.pad(jnp.stack([attn_gain, mlp_gain]), ((0, 14), (0, features - width)))
     shares = ring.gather(
         jnp.concatenate(
             [
                 lax.dynamic_slice_in_dim(w_out, lax.axis_index(DP) * slice_rows, slice_rows, axis=0),
-                gain_rows.reshape(16, features),
+                gain_rows,
             ],
             axis=0,
         )
@@ -838,18 +839,15 @@
     del every.blocks
     in_a.hop()
     shares.hop()
+    for m in micros:
+        m.grad_product = matmul_back(grad_output(m), w_down, bf16)
     ring.tick(in_a, shares)
     in_a.hop()
     shares.hop()
     ring.tick(in_a, shares)
     in_b.hop()
-    gain_blocks = [block[slice_rows:] for block in shares.blocks()]
-    gain_blocks = [block.reshape(-1)[: 2 * width] for block in gain_blocks]
-    every.gains = jnp.stack(
-        [
-            jnp.concatenate([g[:width] for g in gain_blocks]),
-            jnp.concatenate([g[width:] for g in gain_blocks]),
-        ]
+    every.gains = jnp.concatenate(
+        [block[slice_rows : slice_rows + 2, :width] for block in shares.blocks()], axis=1
     ).astype(f32)
     normalise(a, in_a.take())
     project(a)
@@ -886,9 +884,8 @@
     ring.tick(mixed_b)
     mixed_b.hop()
     activate(a)
+    back_mid(a)
     ring.tick(mixed_b)
-    back_mid(a)
-    ring.tick()
     mid_a = ring.scatter(a.part_mid)
     del a.part_mid
     mid_a.hop()
@@ -998,11 +995,14 @@
     in_grad_b.hop()
     del a.part_in, b.part_in
     taps = 3 * TAPS
+    dots = jnp.concatenate(
+        [jnp.concatenate(m.dots, axis=0) / m.scale_in for m in micros], axis=0
+    ).reshape(-1)
     sums = Sums(
         ring,
         jnp.concatenate(
             [
-                a.dot_in, b.dot_in, a.gain_in + b.gain_in,
+                dots, a.gain_in + b.gain_in,
                 jnp.sum(every.wide[taps].reshape(heads, CH), 0),
             ]
         ),

time: 575 us -> 565 us (0.983)
  matrix products: 158 us -> 147 us
  local copies, waits for them, and re-layouts: 32.4 us -> 39.9 us
    dot_general x8, matrix products: 54.2 us -> 45 us  [matmul_back(): lax.dot_general(former, latter, (((1,), (1,)), ((), ())), preferred_eleme...]
    unnamed x197 -> x209, local copies, waits for them, and re-layouts: 17.2 us -> 20.9 us
  transfers between devices with their start and end apart: 54 -> 54, of which waited for: 21 -> 23; matrix products, arithmetic and copies ran while one was open for 46% -> 46% of each run, Pallas kernels for 12% -> 13%
where the time goes in v3:
time: 565 us; the launch traced here: 557 us
  matrix products  147 us (26%)
  waiting for transfers between devices  124 us (22%)
  other arithmetic  101 us (18%)
  Pallas kernels  69.9 us (12%)
  starting transfers between devices  58.8 us (10%)
  local copies, waits for them, and re-layouts  39.9 us (7%)
  between operations  15.7 us (3%)
    ppermute x39, waiting for transfers between devices, send(): return lax.ppermute(block, HEAD, self.pairs)  114 us
    dot_general x8, matrix products, matmul(): return jnp.dot(former, latter, preferred_element_type=f32).astype(kind)  52.5 us
    dot_general x5, matrix products, matmul_rows(): lax.dot_general(former, latter, (((0,), (0,)), ((), ())), preferred_eleme...  49.6 us
    ppermute x39, starting transfers between devices, send(): return lax.ppermute(block, HEAD, self.pairs)  47.6 us
    dot_general x8, matrix products, matmul_back(): lax.dot_general(former, latter, (((1,), (1,)), ((), ())), preferred_eleme...  45 us
    pallas_call x4, Pallas kernels, mixer_backward(): pl.pallas_call(kernel, grid=(1,), in_specs=in_specs, out_specs=[pl.BlockS...  44.4 us
    pallas_call x2, Pallas kernels, mixer_forward(): pl.pallas_call(forward_kernel, grid=(rows // SEQ,), in_specs=[row_spec(pr...  25.5 us
    unnamed x209, local copies, waits for them, and re-layouts  20.9 us
  transfers between devices with their start and end apart: 54, of which 23 were waited for; matrix products, arithmetic and copies ran while one was open for 46% of the time, Pallas kernels for 13%

profile of v3, /device:TPU:0, one launch (start us, length us, event | category | flops | bytes accessed | tf_op | source)
XLA Modules:
  0.0 556.6 jit_solution(16649869609792644744)
XLA Ops:
  8.9 3.1 collective-permute-start.1
  23.7 3.5 copy-done.86
  27.2 4.5 convolution_convert_fusion.6
  36.2 4.5 convolution_convert_fusion.5
  40.8 5.4 collective-permute-done.3
  46.2 9.6 %collective-permute-done.2 = bf16[512,512]{1,0:T(8,128)(2,1)} collective-permute-done((bf16[512,512]{1,0:T(8,128)(2,1)}, bf16[512,512]{1,0:T(8,128)(2,1)}, u32[]{:S(2)}, u32[]{:S(2)}) %collective-permute-start.2) | collective-permute-done | bytes 524320 | tf_op jit(solution)/shard_map/ppermute | solution.py:552
  57.2 18.9 %collective-permute-done.5 = bf16[80,2048]{1,0:T(8,128)(2,1)} collective-permute-done((bf16[80,2048]{1,0:T(8,128)(2,1)S(1)}, bf16[80,2048]{1,0:T(8,128)(2,1)}, u32[]{:S(2)}, u32[]{:S(2)}) %collective-permute-start.5) | collective-permute-done | bytes 327712 | tf_op jit(solution)/shard_map/ppermute | solution.py:552
  82.6 6.6 %fusion.98.pre_ref.refs_0_ = f32[512,2176]{1,0:T(8,128)} fusion(bf16[512,2048]{1,0:T(8,128)(2,1)S(1)} %fusion.5, bf16[2048,2176]{1,0:T(8,128)(2,1)S(1)} %copy-done.66), kind=kOutput, calls=%fused_computation.279 | convolution fusion | flops 4563402752 | bytes 15466496 | tf_op jit(solution)/shard_map/dot_general | solution.py:484
  94.8 12.9 %mixer_forward.2 = (bf16[512,512]{1,0:T(8,128)(2,1)}, f32[512,512]{1,0:T(8,128)}, f32[512,512]{1,0:T(8,128)}, f32[512,512]{1,0:T(8,128)}) custom-call(f32[512,2176]{1,0:T(8,128)} %fusion.98.pre_ref.refs_0_, f32[3,4,512]{2,1,0:T(4,128)} %refs_1_.7, f32[2,4]{1,0:T(2,128)} %pad_maximum_fusion.15.decay_ref.refs_2_, f32[1,128]{1,0:T(1,128)} %bitcast.142), custom_call_target="tpu_custom_call" | custom-call | flops 10000000000 | bytes 10000000 | tf_op jit(solution)/shard_map/mixer_forward/pallas_call | solution.py:421
  108.2 3.2 collective-permute-start.8
  111.5 9.8 %pad_maximum_fusion = bf16[2048,2816]{1,0:T(8,128)(2,1)} fusion(bf16[2048,1408]{1,0:T(8,128)(2,1)S(1)} %bitcast.103, bf16[2048,1408]{1,0:T(8,128)(2,1)} %param.35), kind=kLoop, calls=%fused_computation | loop fusion | flops 23068672 | bytes 23068672 | tf_op jit(solution)/shard_map/concatenate | solution.py:865
  121.3 9.1 %collective-permute-done.8 = bf16[512,512]{1,0:T(8,128)(2,1)S(1)} collective-permute-done((bf16[512,512]{1,0:T(8,128)(2,1)}, bf16[512,512]{1,0:T(8,128)(2,1)S(1)}, u32[]{:S(2)}, u32[]{:S(2)}) %collective-permute-start.8) | collective-permute-done | bytes 524320 | tf_op jit(solution)/shard_map/ppermute | solution.py:552
  134.9 6.6 %fusion.99.pre_ref.refs_0_ = f32[512,2176]{1,0:T(8,128)} fusion(bf16[512,2048]{1,0:T(8,128)(2,1)S(1)} %fusion.8, bf16[2048,2176]{1,0:T(8,128)(2,1)S(1)} %bitcast.108), kind=kOutput, calls=%fused_computation.280 | convolution fusion | flops 4563402752 | bytes 15466496 | tf_op jit(solution)/shard_map/dot_general | solution.py:484
  142.6 12.7 %mixer_forward.3 = (bf16[512,512]{1,0:T(8,128)(2,1)}, f32[512,512]{1,0:T(8,128)}, f32[512,512]{1,0:T(8,128)}, f32[512,512]{1,0:T(8,128)}) custom-call(f32[512,2176]{1,0:T(8,128)} %fusion.99.pre_ref.refs_0_, f32[3,4,512]{2,1,0:T(4,128)} %refs_1_.7, f32[2,4]{1,0:T(2,128)} %pad_maximum_fusion.15.decay_ref.refs_2_, f32[1,128]{1,0:T(1,128)} %bitcast.143), custom_call_target="tpu_custom_call" | custom-call | flops 10000000000 | bytes 10000000 | tf_op jit(solution)/shard_map/mixer_forward/pallas_call | solution.py:421
  155.3 3.3 collective-permute-start.11
  158.8 12.4 %collective-permute-done.11 = bf16[512,512]{1,0:T(8,128)(2,1)} collective-permute-done((bf16[512,512]{1,0:T(8,128)(2,1)S(1)}, bf16[512,512]{1,0:T(8,128)(2,1)}, u32[]{:S(2)}, u32[]{:S(2)}) %collective-permute-start.11) | collective-permute-done | bytes 524320 | tf_op jit(solution)/shard_map/ppermute | solution.py:552
  173.1 7.2 %convert_add_fusion.1 = f32[512,2048]{1,0:T(8,128)S(1)} fusion(bf16[512,2048]{1,0:T(8,128)(2,1)S(1)} %copy-done.6, bf16[2048,2048]{1,0:T(8,128)(2,1)} %bitcast.138, bf16[512,512]{1,0:T(8,128)(2,1)S(1)} %get-tuple-element.2097, bf16[512,512]{1,0:T(8,128)(2,1)S(1)} %get-tuple-element.2098, bf16[512,512]{1,0:T(8,128)(2,1)S(1)} %get-tuple-element.2099, ...), kind=kOutput, calls=%fused_computation.49 | convolution fusion | flops 4305453056 | bytes 16777216 | tf_op jit(solution)/shard_map/dot_general | solution.py:484
  184.2 6.2 %fusion.100 = f32[512,2816]{1,0:T(8,128)S(1)} fusion(bf16[512,2048]{1,0:T(8,128)(2,1)S(1)} %multiply_convert_fusion.1, bf16[2048,2816]{1,0:T(8,128)(2,1)S(1)} %bitcast.101), kind=kOutput, calls=%fused_computation.281 | convolution fusion | flops 5905580032 | bytes 19398656 | tf_op jit(solution)/shard_map/dot_general | solution.py:484
  190.3 6.5 %collective-permute-done.13 = bf16[512,512]{1,0:T(8,128)(2,1)} collective-permute-done((bf16[512,512]{1,0:T(8,128)(2,1)}, bf16[512,512]{1,0:T(8,128)(2,1)}, u32[]{:S(2)}, u32[]{:S(2)}) %collective-permute-start.13) | collective-permute-done | bytes 524320 | tf_op jit(solution)/shard_map/ppermute | solution.py:552
  201.4 6.4 %convolution_convert_fusion.4 = bf16[512,2048]{1,0:T(8,128)(2,1)S(1)} fusion(bf16[2048,2816]{1,0:T(8,128)(2,1)S(1)} %bitcast.101, bf16[512,1408]{1,0:T(8,128)(2,1)S(1)} %get-tuple-element.2063, bf16[512,1408]{1,0:T(8,128)(2,1)S(1)} %get-tuple-element.2062), kind=kOutput, calls=%fused_computation.56 | convolution fusion | flops 5912395776 | bytes 16515072 | tf_op jit(solution)/shard_map/dot_general | solution.py:494
  214.4 7.0 %convert_add_fusion = f32[512,2048]{1,0:T(8,128)S(1)} fusion(bf16[512,2048]{1,0:T(8,128)(2,1)S(1)} %copy-done.9, bf16[2048,2048]{1,0:T(8,128)(2,1)} %bitcast.139, bf16[512,512]{1,0:T(8,128)(2,1)S(1)} %get-tuple-element.2093, bf16[512,512]{1,0:T(8,128)(2,1)S(1)} %get-tuple-element.2094, bf16[512,512]{1,0:T(8,128)(2,1)S(1)} %get-tuple-element.2095, ...), kind=kOutput, calls=%fused_computation.46 | convolution fusion | flops 4305453056 | bytes 16777216 | tf_op jit(solution)/shard_map/dot_general | solution.py:484
  221.4 5.8 %collective-permute-done.15 = bf16[512,512]{1,0:T(8,128)(2,1)S(1)} collective-permute-done((bf16[512,512]{1,0:T(8,128)(2,1)S(1)}, bf16[512,512]{1,0:T(8,128)(2,1)S(1)}, u32[]{:S(2)}, u32[]{:S(2)}) %collective-permute-start.15) | collective-permute-done | bytes 524320 | tf_op jit(solution)/shard_map/ppermute | solution.py:552
  228.6 6.2 %fusion.101 = f32[512,2816]{1,0:T(8,128)S(1)} fusion(bf16[512,2048]{1,0:T(8,128)(2,1)S(1)} %multiply_convert_fusion, bf16[2048,2816]{1,0:T(8,128)(2,1)S(1)} %bitcast.101), kind=kOutput, calls=%fused_computation.282 | convolution fusion | flops 5905580032 | bytes 19398656 | tf_op jit(solution)/shard_map/dot_general | solution.py:484
  234.8 6.7 %collective-permute-done.16 = bf16[512,512]{1,0:T(8,128)(2,1)S(1)} collective-permute-done((bf16[512,512]{1,0:T(8,128)(2,1)S(1)}, bf16[512,512]{1,0:T(8,128)(2,1)S(1)}, u32[]{:S(2)}, u32[]{:S(2)}) %collective-permute-start.16) | collective-permute-done | bytes 524320 | tf_op jit(solution)/shard_map/ppermute | solution.py:552
  245.0 12.5 %collective-permute-done.17 = bf16[512,512]{1,0:T(8,128)(2,1)S(1)} collective-permute-done((bf16[512,512]{1,0:T(8,128)(2,1)S(1)}, bf16[512,512]{1,0:T(8,128)(2,1)S(1)}, u32[]{:S(2)}, u32[]{:S(2)}) %collective-permute-start.17) | collective-permute-done | bytes 524320 | tf_op jit(solution)/shard_map/ppermute | solution.py:552
  258.7 6.4 %convolution_convert_fusion.3 = bf16[512,2048]{1,0:T(8,128)(2,1)S(1)} fusion(bf16[512,2816]{1,0:T(8,128)(2,1)S(1)} %pad_maximum_fusion.2, bf16[2048,2816]{1,0:T(8,128)(2,1)S(1)} %bitcast.101), kind=kOutput, calls=%fused_computation.55 | convolution fusion | flops 5906628608 | bytes 16515072 | tf_op jit(solution)/shard_map/dot_general | solution.py:494
  267.2 3.4 collective-permute-start.19
  270.6 9.8 %convolution_convert_fusion.1 = bf16[1408,2048]{1,0:T(8,128)(2,1)} fusion(bf16[512,2048]{1,0:T(8,128)(2,1)S(1)} %copy-done.12, bf16[512,2048]{1,0:T(8,128)(2,1)S(1)} %copy-done.15, bf16[512,1408]{1,0:T(8,128)(2,1)} %get-tuple-element.1423, bf16[512,1408]{1,0:T(8,128)(2,1)} %get-tuple-element.1412), kind=kOutput, calls=%fused_computation.3 | convolution fusion | flops 5922619392 | bytes 12845056 | tf_op jit(solution)/shard_map/dot_general | solution.py:488
  280.8 18.4 %convolution_convert_fusion = bf16[2048,2816]{1,0:T(8,128)(2,1)} fusion(bf16[512,2816]{1,0:T(8,128)(2,1)} %copy-done.31, bf16[512,2816]{1,0:T(8,128)(2,1)} %pad_maximum_fusion.1, bf16[512,2048]{1,0:T(8,128)(2,1)} %copy-done.35, bf16[512,2048]{1,0:T(8,128)(2,1)} %copy-done.34), kind=kOutput, calls=%fused_computation.1 | convolution fusion | flops 11836850176 | bytes 21495808 | tf_op jit(solution)/shard_map/dot_general | solution.py:488
  302.1 8.2 %convolution_convert_fusion.8 = bf16[512,2048]{1,0:T(8,128)(2,1)} fusion(bf16[512,1408]{1,0:T(8,128)(2,1)} %get-tuple-element.1412, bf16[1408,2048]{1,0:T(8,128)(2,1)} %param.37), kind=kOutput, calls=%fused_computation.60 | convolution fusion | flops 2953838592 | bytes 9306112 | tf_op jit(solution)/shard_map/dot_general | solution.py:484
  310.3 4.7 convolution_convert_fusion.7
  321.3 2.9 collective-permute-start.23
  324.2 5.5 collective-permute-done.22
  341.6 10.9 %mixer_backward.4 = (bf16[1024,2176]{1,0:T(8,128)(2,1)}, f32[16,512]{1,0:T(8,128)}, f32[2,4]{1,0:T(2,128)}, f32[256,1]{1,0:T(8,128)}) custom-call(f32[512,2176]{1,0:T(8,128)} %fusion.98.pre_ref.refs_0_, f32[3,4,512]{2,1,0:T(4,128)} %refs_1_.7, f32[2,4]{1,0:T(2,128)} %pad_maximum_fusion.15.decay_ref.refs_2_, f32[1,128]{1,0:T(1,128)} %bitcast.144, ...), custom_call_target="tpu_custom_call" | custom-call | flops 10000000000 | bytes 10000000 | tf_op jit(solution)/shard_map/mixer_backward/pallas_call | solution.py:456
  353.3 3.1 collective-permute-start.25
  356.4 10.9 %mixer_backward.5 = (bf16[1024,2176]{1,0:T(8,128)(2,1)}, f32[16,512]{1,0:T(8,128)}, f32[2,4]{1,0:T(2,128)}, f32[256,1]{1,0:T(8,128)}) custom-call(f32[512,2176]{1,0:T(8,128)} %fusion.98.pre_ref.refs_0_, f32[3,4,512]{2,1,0:T(4,128)} %refs_1_.7, f32[2,4]{1,0:T(2,128)} %pad_maximum_fusion.15.decay_ref.refs_2_, ...), custom_call_target="tpu_custom_call", output_to_operand_aliasing={{0}: (10, {})} | custom-call | flops 10000000000 | bytes 10000000 | tf_op jit(solution)/shard_map/mixer_backward/pallas_call | solution.py:456
  368.7 9.4 %convolution_convert_fusion.10 = bf16[512,2048]{1,0:T(8,128)(2,1)S(1)} fusion(bf16[2048,2176]{1,0:T(8,128)(2,1)} %copy-done.65, bf16[1024,2176]{1,0:T(8,128)(2,1)} %get-tuple-element.1682.refs_10_), kind=kOutput, calls=%fused_computation.62 | convolution fusion | flops 4564451328 | bytes 13238272 | tf_op jit(solution)/shard_map/dot_general | solution.py:494
  389.6 3.1 collective-permute-start.28
  392.6 11.2 %mixer_backward.6 = (bf16[1024,2176]{1,0:T(8,128)(2,1)}, f32[16,512]{1,0:T(8,128)}, f32[2,4]{1,0:T(2,128)}, f32[256,1]{1,0:T(8,128)}) custom-call(f32[512,2176]{1,0:T(8,128)} %fusion.99.pre_ref.refs_0_, f32[3,4,512]{2,1,0:T(4,128)} %refs_1_.7, f32[2,4]{1,0:T(2,128)} %pad_maximum_fusion.15.decay_ref.refs_2_, ...), custom_call_target="tpu_custom_call", output_to_operand_aliasing={{0}: (10, {})} | custom-call | flops 10000000000 | bytes 10000000 | tf_op jit(solution)/shard_map/mixer_backward/pallas_call | solution.py:456
  403.8 11.4 %mixer_backward.7 = (bf16[1024,2176]{1,0:T(8,128)(2,1)}, f32[16,512]{1,0:T(8,128)}, f32[2,4]{1,0:T(2,128)}, f32[256,1]{1,0:T(8,128)}) custom-call(f32[512,2176]{1,0:T(8,128)} %fusion.99.pre_ref.refs_0_, f32[3,4,512]{2,1,0:T(4,128)} %refs_1_.7, f32[2,4]{1,0:T(2,128)} %pad_maximum_fusion.15.decay_ref.refs_2_, ...), custom_call_target="tpu_custom_call", output_to_operand_aliasing={{0}: (10, {})} | custom-call | flops 10000000000 | bytes 10000000 | tf_op jit(solution)/shard_map/mixer_backward/pallas_call | solution.py:456
  417.5 9.0 %convolution_convert_fusion.2 = bf16[1024,2176]{1,0:T(8,128)(2,1)} fusion(bf16[1024,1024]{1,0:T(8,128)(2,1)S(1)} %copy-done.40, bf16[1024,2176]{1,0:T(8,128)(2,1)} %get-tuple-element.1817), kind=kOutput, calls=%fused_computation.7 | convolution fusion | flops 4565630976 | bytes 11010048 | tf_op jit(solution)/shard_map/dot_general | solution.py:488
  433.1 9.3 %convolution_convert_fusion.9 = bf16[512,2048]{1,0:T(8,128)(2,1)} fusion(bf16[2048,2176]{1,0:T(8,128)(2,1)} %copy-done.65, bf16[1024,2176]{1,0:T(8,128)(2,1)} %get-tuple-element.1817), kind=kOutput, calls=%fused_computation.61 | convolution fusion | flops 4564451328 | bytes 13238272 | tf_op jit(solution)/shard_map/dot_general | solution.py:494
  447.4 8.6 %add_convert_fusion = bf16[1024,2176]{1,0:T(8,128)(2,1)S(1)} fusion(bf16[1024,2176]{1,0:T(8,128)(2,1)} %collective-permute-done.31, bf16[1024,1024]{1,0:T(8,128)(2,1)} %pad_maximum_fusion.4, bf16[1024,2176]{1,0:T(8,128)(2,1)} %get-tuple-element.1817), kind=kOutput, calls=%fused_computation.2 | convolution fusion | flops 4570087424 | bytes 15466496 | tf_op jit(solution)/shard_map/dot_general | solution.py:488
  471.2 3.8 fusion.29
  496.8 4.3 collective-permute-done.38
  516.0 5.8 %collective-permute-done.45 = bf16[512,512]{1,0:T(8,128)(2,1)S(1)} collective-permute-done((bf16[512,512]{1,0:T(8,128)(2,1)S(1)}, bf16[512,512]{1,0:T(8,128)(2,1)S(1)}, u32[]{:S(2)}, u32[]{:S(2)}) %collective-permute-start.45) | collective-permute-done | bytes 524320 | tf_op jit(solution)/shard_map/ppermute | solution.py:552
  521.8 4.1 collective-permute-done.44
  539.3 4.4 collective-permute-done.49
  (446 shorter events, 182.0 us)
Async XLA Ops:
  7.2 164.0 %all-gather.2.cloned.1.call-start = ((), (), s32[]{:S(2)}) async-start(), calls=%async_computation.3 | async-start | bytes 9437184 | tf_op jit(solution)/shard_map/all_gather | solution.py:856
  8.9 25.5 %collective-permute-start.1 = (bf16[80,2048]{1,0:T(8,128)(2,1)S(1)}, bf16[80,2048]{1,0:T(8,128)(2,1)}, u32[]{:S(2)}, u32[]{:S(2)}) collective-permute-start(bf16[80,2048]{1,0:T(8,128)(2,1)S(1)} %pad_maximum_fusion.12), channel_id=1, source_target_pairs={{0,1},{1,3},{3,2},{2,0},{4,5},{5,7},{7,6},{6,4},{8,9},{9,11},{11,1... | collective-permute-start | bytes 983048 | tf_op jit(solution)/shard_map/ppermute | solution.py:552
  13.8 20.5 %collective-permute-start = (bf16[512,512]{1,0:T(8,128)(2,1)}, bf16[512,512]{1,0:T(8,128)(2,1)}, u32[]{:S(2)}, u32[]{:S(2)}) collective-permute-start(bf16[512,512]{1,0:T(8,128)(2,1)} %slice_bitcast_fusion.1), channel_id=1, source_target_pairs={{0,1},{1,3},{3,2},{2,0},{4,5},{5,7},{7,6},{6,4},{8,9},{9,11},{11,1... | collective-permute-start | bytes 1572872 | tf_op jit(solution)/shard_map/ppermute | solution.py:552
  34.4 11.8 %collective-permute-start.3 = (bf16[80,2048]{1,0:T(8,128)(2,1)}, bf16[80,2048]{1,0:T(8,128)(2,1)S(1)}, u32[]{:S(2)}, u32[]{:S(2)}) collective-permute-start(bf16[80,2048]{1,0:T(8,128)(2,1)} %collective-permute-done.1), channel_id=1, source_target_pairs={{0,1},{1,3},{3,2},{2,0},{4,5},{5,7},{7,6},{6,4},{8,9},{9,11},{11,1... | collective-permute-start | bytes 983048 | tf_op jit(solution)/shard_map/ppermute | solution.py:552
  34.8 20.9 %collective-permute-start.2 = (bf16[512,512]{1,0:T(8,128)(2,1)}, bf16[512,512]{1,0:T(8,128)(2,1)}, u32[]{:S(2)}, u32[]{:S(2)}) collective-permute-start(bf16[512,512]{1,0:T(8,128)(2,1)} %collective-permute-done), channel_id=1, source_target_pairs={{0,1},{1,3},{3,2},{2,0},{4,5},{5,7},{7,6},{6,4},{8,9},{9,11},{11,1... | collective-permute-start | bytes 1572872 | tf_op jit(solution)/shard_map/ppermute | solution.py:552
  55.7 20.4 %collective-permute-start.4 = (bf16[512,512]{1,0:T(8,128)(2,1)}, bf16[512,512]{1,0:T(8,128)(2,1)}, u32[]{:S(2)}, u32[]{:S(2)}) collective-permute-start(bf16[512,512]{1,0:T(8,128)(2,1)} %collective-permute-done.2), channel_id=1, source_target_pairs={{0,1},{1,3},{3,2},{2,0},{4,5},{5,7},{7,6},{6,4},{8,9},{9,11},{11,1... | collective-permute-start | bytes 1572872 | tf_op jit(solution)/shard_map/ppermute | solution.py:552
  55.7 20.4 %collective-permute-start.5 = (bf16[80,2048]{1,0:T(8,128)(2,1)S(1)}, bf16[80,2048]{1,0:T(8,128)(2,1)}, u32[]{:S(2)}, u32[]{:S(2)}) collective-permute-start(bf16[80,2048]{1,0:T(8,128)(2,1)S(1)} %collective-permute-done.3), channel_id=1, source_target_pairs={{0,1},{1,3},{3,2},{2,0},{4,5},{5,7},{7,6},{6,4},{8,9},{9,11},{11,1... | collective-permute-start | bytes 983048 | tf_op jit(solution)/shard_map/ppermute | solution.py:552
  77.7 12.3 %collective-permute-start.6 = (bf16[512,512]{1,0:T(8,128)(2,1)S(1)}, bf16[512,512]{1,0:T(8,128)(2,1)}, u32[]{:S(2)}, u32[]{:S(2)}) collective-permute-start(bf16[512,512]{1,0:T(8,128)(2,1)S(1)} %slice_bitcast_fusion), channel_id=1, source_target_pairs={{0,1},{1,3},{3,2},{2,0},{4,5},{5,7},{7,6},{6,4},{8,9},{9,11},{11,1... | collective-permute-start | bytes 1572872 | tf_op jit(solution)/shard_map/ppermute | solution.py:552
  93.3 259.9 %reduce-scatter.4.cloned.1.call-start = ((), (), s32[]{:S(2)}) async-start(), calls=%async_computation.4 | async-start | bytes 6488064 | tf_op jit(solution)/shard_map/reduce_scatter | solution.py:914
  94.0 13.6 %collective-permute-start.7 = (bf16[512,512]{1,0:T(8,128)(2,1)}, bf16[512,512]{1,0:T(8,128)(2,1)}, u32[]{:S(2)}, u32[]{:S(2)}) collective-permute-start(bf16[512,512]{1,0:T(8,128)(2,1)} %collective-permute-done.6), channel_id=1, source_target_pairs={{0,1},{1,3},{3,2},{2,0},{4,5},{5,7},{7,6},{6,4},{8,9},{9,11},{11,1... | collective-permute-start | bytes 1572872 | tf_op jit(solution)/shard_map/ppermute | solution.py:552
  107.6 33.9 %collective-permute-start.9 = (bf16[512,512]{1,0:T(8,128)(2,1)}, bf16[512,512]{1,0:T(8,128)(2,1)}, u32[]{:S(2)}, u32[]{:S(2)}) collective-permute-start(bf16[512,512]{1,0:T(8,128)(2,1)} %get-tuple-element.1850), channel_id=1, source_target_pairs={{0,1},{1,3},{3,2},{2,0},{4,5},{5,7},{7,6},{6,4},{8,9},{9,11},{11,1... | collective-permute-start | bytes 1572872 | tf_op jit(solution)/shard_map/ppermute | solution.py:552
  108.2 22.2 %collective-permute-start.8 = (bf16[512,512]{1,0:T(8,128)(2,1)}, bf16[512,512]{1,0:T(8,128)(2,1)S(1)}, u32[]{:S(2)}, u32[]{:S(2)}) collective-permute-start(bf16[512,512]{1,0:T(8,128)(2,1)} %collective-permute-done.7), channel_id=1, source_target_pairs={{0,1},{1,3},{3,2},{2,0},{4,5},{5,7},{7,6},{6,4},{8,9},{9,11},{11,1... | collective-permute-start | bytes 1572872 | tf_op jit(solution)/shard_map/ppermute | solution.py:552
  141.6 13.7 %collective-permute-start.10 = (bf16[512,512]{1,0:T(8,128)(2,1)}, bf16[512,512]{1,0:T(8,128)(2,1)S(1)}, u32[]{:S(2)}, u32[]{:S(2)}) collective-permute-start(bf16[512,512]{1,0:T(8,128)(2,1)} %collective-permute-done.9), channel_id=1, source_target_pairs={{0,1},{1,3},{3,2},{2,0},{4,5},{5,7},{7,6},{6,4},{8,9},{9,11},{11,1... | collective-permute-start | bytes 1572872 | tf_op jit(solution)/shard_map/ppermute | solution.py:552
  155.3 15.9 %collective-permute-start.11 = (bf16[512,512]{1,0:T(8,128)(2,1)S(1)}, bf16[512,512]{1,0:T(8,128)(2,1)}, u32[]{:S(2)}, u32[]{:S(2)}) collective-permute-start(bf16[512,512]{1,0:T(8,128)(2,1)S(1)} %collective-permute-done.10), channel_id=1, source_target_pairs={{0,1},{1,3},{3,2},{2,0},{4,5},{5,7},{7,6},{6,4},{8,9},{9,11},{11,1... | collective-permute-start | bytes 1572872 | tf_op jit(solution)/shard_map/ppermute | solution.py:552
  158.6 21.7 %collective-permute-start.12 = (bf16[512,512]{1,0:T(8,128)(2,1)}, bf16[512,512]{1,0:T(8,128)(2,1)}, u32[]{:S(2)}, u32[]{:S(2)}) collective-permute-start(bf16[512,512]{1,0:T(8,128)(2,1)} %get-tuple-element.1851), channel_id=1, source_target_pairs={{0,1},{1,3},{3,2},{2,0},{4,5},{5,7},{7,6},{6,4},{8,9},{9,11},{11,1... | collective-permute-start | bytes 1572872 | tf_op jit(solution)/shard_map/ppermute | solution.py:552
  181.0 15.8 %collective-permute-start.13 = (bf16[512,512]{1,0:T(8,128)(2,1)}, bf16[512,512]{1,0:T(8,128)(2,1)}, u32[]{:S(2)}, u32[]{:S(2)}) collective-permute-start(bf16[512,512]{1,0:T(8,128)(2,1)} %collective-permute-done.12), channel_id=1, source_target_pairs={{0,1},{1,3},{3,2},{2,0},{4,5},{5,7},{7,6},{6,4},{8,9},{9,11},{11,1... | collective-permute-start | bytes 1572872 | tf_op jit(solution)/shard_map/ppermute | solution.py:552
  196.8 15.2 %collective-permute-start.14 = (bf16[512,512]{1,0:T(8,128)(2,1)}, bf16[512,512]{1,0:T(8,128)(2,1)}, u32[]{:S(2)}, u32[]{:S(2)}) collective-permute-start(bf16[512,512]{1,0:T(8,128)(2,1)} %collective-permute-done.13), channel_id=1, source_target_pairs={{0,1},{1,3},{3,2},{2,0},{4,5},{5,7},{7,6},{6,4},{8,9},{9,11},{11,1... | collective-permute-start | bytes 1572872 | tf_op jit(solution)/shard_map/ppermute | solution.py:552
  212.1 15.0 %collective-permute-start.15 = (bf16[512,512]{1,0:T(8,128)(2,1)S(1)}, bf16[512,512]{1,0:T(8,128)(2,1)S(1)}, u32[]{:S(2)}, u32[]{:S(2)}) collective-permute-start(bf16[512,512]{1,0:T(8,128)(2,1)S(1)} %constant_dynamic-slice_fusion.5), channel_id=1, source_target_pairs={{0,1},{1,3},{3,2},{2,0},{4,5},{5,7},{7,6},{6,4},{8,9},{9,11},{11,1... | collective-permute-start | bytes 1572872 | tf_op jit(solution)/shard_map/ppermute | solution.py:552
  227.7 13.8 %collective-permute-start.16 = (bf16[512,512]{1,0:T(8,128)(2,1)S(1)}, bf16[512,512]{1,0:T(8,128)(2,1)S(1)}, u32[]{:S(2)}, u32[]{:S(2)}) collective-permute-start(bf16[512,512]{1,0:T(8,128)(2,1)S(1)} %add_convert_fusion.16), channel_id=1, source_target_pairs={{0,1},{1,3},{3,2},{2,0},{4,5},{5,7},{7,6},{6,4},{8,9},{9,11},{11,1... | collective-permute-start | bytes 1572872 | tf_op jit(solution)/shard_map/ppermute | solution.py:552
  241.7 15.8 %collective-permute-start.17 = (bf16[512,512]{1,0:T(8,128)(2,1)S(1)}, bf16[512,512]{1,0:T(8,128)(2,1)S(1)}, u32[]{:S(2)}, u32[]{:S(2)}) collective-permute-start(bf16[512,512]{1,0:T(8,128)(2,1)S(1)} %add_convert_fusion.15), channel_id=1, source_target_pairs={{0,1},{1,3},{3,2},{2,0},{4,5},{5,7},{7,6},{6,4},{8,9},{9,11},{11,1... | collective-permute-start | bytes 1572872 | tf_op jit(solution)/shard_map/ppermute | solution.py:552
  258.5 21.9 %collective-permute-start.18 = (bf16[512,512]{1,0:T(8,128)(2,1)}, bf16[512,512]{1,0:T(8,128)(2,1)}, u32[]{:S(2)}, u32[]{:S(2)}) collective-permute-start(bf16[512,512]{1,0:T(8,128)(2,1)} %get-tuple-element.1508), channel_id=1, source_target_pairs={{0,1},{1,3},{3,2},{2,0},{4,5},{5,7},{7,6},{6,4},{8,9},{9,11},{11,1... | collective-permute-start | bytes 1572872 | tf_op jit(solution)/shard_map/ppermute | solution.py:552
  267.2 31.9 %collective-permute-start.19 = (bf16[512,512]{1,0:T(8,128)(2,1)}, bf16[512,512]{1,0:T(8,128)(2,1)}, u32[]{:S(2)}, u32[]{:S(2)}) collective-permute-start(bf16[512,512]{1,0:T(8,128)(2,1)} %constant_dynamic-slice_fusion.4), channel_id=1, source_target_pairs={{0,1},{1,3},{3,2},{2,0},{4,5},{5,7},{7,6},{6,4},{8,9},{9,11},{11,1... | collective-permute-start | bytes 1572872 | tf_op jit(solution)/shard_map/ppermute | solution.py:552
  280.5 164.8 %reduce-scatter.6.cloned.1.call-start = ((), (), s32[]{:S(2)}) async-start(), calls=%async_computation.5 | async-start | bytes 12976128 | tf_op jit(solution)/shard_map/reduce_scatter | solution.py:943
  280.5 34.5 %collective-permute-start.20 = (bf16[512,512]{1,0:T(8,128)(2,1)}, bf16[512,512]{1,0:T(8,128)(2,1)}, u32[]{:S(2)}, u32[]{:S(2)}) collective-permute-start(bf16[512,512]{1,0:T(8,128)(2,1)} %collective-permute-done.18), channel_id=1, source_target_pairs={{0,1},{1,3},{3,2},{2,0},{4,5},{5,7},{7,6},{6,4},{8,9},{9,11},{11,1... | collective-permute-start | bytes 1572872 | tf_op jit(solution)/shard_map/ppermute | solution.py:552
  300.7 19.8 %collective-permute-start.21 = (bf16[512,512]{1,0:T(8,128)(2,1)S(1)}, bf16[512,512]{1,0:T(8,128)(2,1)S(1)}, u32[]{:S(2)}, u32[]{:S(2)}) collective-permute-start(bf16[512,512]{1,0:T(8,128)(2,1)S(1)} %add_convert_fusion.14), channel_id=1, source_target_pairs={{0,1},{1,3},{3,2},{2,0},{4,5},{5,7},{7,6},{6,4},{8,9},{9,11},{11,1... | collective-permute-start | bytes 1572872 | tf_op jit(solution)/shard_map/ppermute | solution.py:552
  315.0 14.6 %collective-permute-start.22 = (bf16[512,512]{1,0:T(8,128)(2,1)}, bf16[512,512]{1,0:T(8,128)(2,1)S(1)}, u32[]{:S(2)}, u32[]{:S(2)}) collective-permute-start(bf16[512,512]{1,0:T(8,128)(2,1)} %collective-permute-done.20), channel_id=1, source_target_pairs={{0,1},{1,3},{3,2},{2,0},{4,5},{5,7},{7,6},{6,4},{8,9},{9,11},{11,1... | collective-permute-start | bytes 1572872 | tf_op jit(solution)/shard_map/ppermute | solution.py:552
  321.3 16.8 %collective-permute-start.23 = (bf16[512,512]{1,0:T(8,128)(2,1)S(1)}, bf16[512,512]{1,0:T(8,128)(2,1)S(1)}, u32[]{:S(2)}, u32[]{:S(2)}) collective-permute-start(bf16[512,512]{1,0:T(8,128)(2,1)S(1)} %add_convert_fusion.13), channel_id=1, source_target_pairs={{0,1},{1,3},{3,2},{2,0},{4,5},{5,7},{7,6},{6,4},{8,9},{9,11},{11,1... | collective-permute-start | bytes 1572872 | tf_op jit(solution)/shard_map/ppermute | solution.py:552
  339.3 14.0 %collective-permute-start.24 = (bf16[512,512]{1,0:T(8,128)(2,1)S(1)}, bf16[512,512]{1,0:T(8,128)(2,1)}, u32[]{:S(2)}, u32[]{:S(2)}) collective-permute-start(bf16[512,512]{1,0:T(8,128)(2,1)S(1)} %get-tuple-element.1665), channel_id=1, source_target_pairs={{0,1},{1,3},{3,2},{2,0},{4,5},{5,7},{7,6},{6,4},{8,9},{9,11},{11,1... | collective-permute-start | bytes 1572872 | tf_op jit(solution)/shard_map/ppermute | solution.py:552
  353.3 181.4 %reduce-scatter.8.cloned.1.call-start = ((), (), s32[]{:S(2)}) async-start(), calls=%async_computation.6 | async-start | bytes 2359296 | tf_op jit(solution)/shard_map/reduce_scatter | solution.py:992
  353.3 14.0 %collective-permute-start.25 = (bf16[512,512]{1,0:T(8,128)(2,1)}, bf16[512,512]{1,0:T(8,128)(2,1)S(1)}, u32[]{:S(2)}, u32[]{:S(2)}) collective-permute-start(bf16[512,512]{1,0:T(8,128)(2,1)} %collective-permute-done.24), channel_id=1, source_target_pairs={{0,1},{1,3},{3,2},{2,0},{4,5},{5,7},{7,6},{6,4},{8,9},{9,11},{11,1... | collective-permute-start | bytes 1572872 | tf_op jit(solution)/shard_map/ppermute | solution.py:552
  367.4 12.0 %collective-permute-start.26 = (bf16[512,512]{1,0:T(8,128)(2,1)S(1)}, bf16[512,512]{1,0:T(8,128)(2,1)S(1)}, u32[]{:S(2)}, u32[]{:S(2)}) collective-permute-start(bf16[512,512]{1,0:T(8,128)(2,1)S(1)} %collective-permute-done.25), channel_id=1, source_target_pairs={{0,1},{1,3},{3,2},{2,0},{4,5},{5,7},{7,6},{6,4},{8,9},{9,11},{11,1... | collective-permute-start | bytes 1572872 | tf_op jit(solution)/shard_map/ppermute | solution.py:552
  380.2 23.6 %collective-permute-start.27 = (bf16[512,512]{1,0:T(8,128)(2,1)}, bf16[512,512]{1,0:T(8,128)(2,1)}, u32[]{:S(2)}, u32[]{:S(2)}) collective-permute-start(bf16[512,512]{1,0:T(8,128)(2,1)} %constant_dynamic-slice_fusion.3), channel_id=1, source_target_pairs={{0,1},{1,3},{3,2},{2,0},{4,5},{5,7},{7,6},{6,4},{8,9},{9,11},{11,1... | collective-permute-start | bytes 1572872 | tf_op jit(solution)/shard_map/ppermute | solution.py:552
  389.6 25.6 %collective-permute-start.28 = (bf16[512,512]{1,0:T(8,128)(2,1)}, bf16[512,512]{1,0:T(8,128)(2,1)S(1)}, u32[]{:S(2)}, u32[]{:S(2)}) collective-permute-start(bf16[512,512]{1,0:T(8,128)(2,1)} %constant_dynamic-slice_fusion.2), channel_id=1, source_target_pairs={{0,1},{1,3},{3,2},{2,0},{4,5},{5,7},{7,6},{6,4},{8,9},{9,11},{11,1... | collective-permute-start | bytes 1572872 | tf_op jit(solution)/shard_map/ppermute | solution.py:552
  427.6 19.9 %collective-permute-start.31 = (bf16[1024,2176]{1,0:T(8,128)(2,1)}, bf16[1024,2176]{1,0:T(8,128)(2,1)}, u32[]{:S(2)}, u32[]{:S(2)}) collective-permute-start(bf16[1024,2176]{1,0:T(8,128)(2,1)} %convolution_convert_fusion.2), channel_id=1, source_target_pairs={{0,4},{4,0},{8,12},{12,8},{16,20},{20,16},{24,28},{28,24},{1,5},{5... | collective-permute-start | bytes 13369352 | tf_op jit(solution)/shard_map/ppermute | solution.py:970
  429.5 15.8 %collective-permute-start.30 = (bf16[512,512]{1,0:T(8,128)(2,1)S(1)}, bf16[512,512]{1,0:T(8,128)(2,1)}, u32[]{:S(2)}, u32[]{:S(2)}) collective-permute-start(bf16[512,512]{1,0:T(8,128)(2,1)S(1)} %add_convert_fusion.11), channel_id=1, source_target_pairs={{0,1},{1,3},{3,2},{2,0},{4,5},{5,7},{7,6},{6,4},{8,9},{9,11},{11,1... | collective-permute-start | bytes 1572872 | tf_op jit(solution)/shard_map/ppermute | solution.py:552
  432.0 24.5 %collective-permute-start.32 = (bf16[512,512]{1,0:T(8,128)(2,1)}, bf16[512,512]{1,0:T(8,128)(2,1)}, u32[]{:S(2)}, u32[]{:S(2)}) collective-permute-start(bf16[512,512]{1,0:T(8,128)(2,1)} %add_convert_fusion.10), channel_id=1, source_target_pairs={{0,1},{1,3},{3,2},{2,0},{4,5},{5,7},{7,6},{6,4},{8,9},{9,11},{11,1... | collective-permute-start | bytes 1572872 | tf_op jit(solution)/shard_map/ppermute | solution.py:552
  447.4 27.5 %collective-permute-start.33 = (bf16[512,512]{1,0:T(8,128)(2,1)}, bf16[512,512]{1,0:T(8,128)(2,1)}, u32[]{:S(2)}, u32[]{:S(2)}) collective-permute-start(bf16[512,512]{1,0:T(8,128)(2,1)} %add_convert_fusion.9), channel_id=1, source_target_pairs={{0,1},{1,3},{3,2},{2,0},{4,5},{5,7},{7,6},{6,4},{8,9},{9,11},{11,1... | collective-permute-start | bytes 1572872 | tf_op jit(solution)/shard_map/ppermute | solution.py:552
  458.4 26.9 %collective-permute-start.34 = (bf16[512,512]{1,0:T(8,128)(2,1)}, bf16[512,512]{1,0:T(8,128)(2,1)}, u32[]{:S(2)}, u32[]{:S(2)}) collective-permute-start(bf16[512,512]{1,0:T(8,128)(2,1)} %constant_dynamic-slice_fusion.1), channel_id=1, source_target_pairs={{0,1},{1,3},{3,2},{2,0},{4,5},{5,7},{7,6},{6,4},{8,9},{9,11},{11,1... | collective-permute-start | bytes 1572872 | tf_op jit(solution)/shard_map/ppermute | solution.py:552
  461.7 39.4 %collective-permute-start.35 = (bf16[512,1024]{1,0:T(8,128)(2,1)}, bf16[512,1024]{1,0:T(8,128)(2,1)}, u32[]{:S(2)}, u32[]{:S(2)}) collective-permute-start(bf16[512,1024]{1,0:T(8,128)(2,1)} %pad_maximum_fusion.10), channel_id=1, source_target_pairs={{0,8},{4,12},{8,0},{12,4},{16,24},{20,28},{24,16},{28,20},{1,9},{5... | collective-permute-start | bytes 3145736 | tf_op jit(solution)/shard_map/ppermute | solution.py:648
  465.4 35.8 %collective-permute-start.36 = (bf16[512,1152]{1,0:T(8,128)(2,1)}, bf16[512,1152]{1,0:T(8,128)(2,1)}, u32[]{:S(2)}, u32[]{:S(2)}) collective-permute-start(bf16[512,1152]{1,0:T(8,128)(2,1)} %pad_maximum_fusion.8), channel_id=1, source_target_pairs={{0,16},{4,20},{8,24},{12,28},{16,0},{20,4},{24,8},{28,12},{1,17},{... | collective-permute-start | bytes 3538952 | tf_op jit(solution)/shard_map/ppermute | solution.py:648
  480.8 15.4 %collective-permute-start.39 = (f32[3200]{0:T(1024)S(1)}, f32[3200]{0:T(1024)S(1)}, u32[]{:S(2)}, u32[]{:S(2)}) collective-permute-start(f32[3200]{0:T(1024)S(1)} %pad_maximum_fusion.13), channel_id=1, source_target_pairs={{0,2},{1,3},{2,0},{3,1},{4,6},{5,7},{6,4},{7,5},{8,10},{9,11},{10,... | collective-permute-start | bytes 38408 | tf_op jit(solution)/shard_map/ppermute | solution.py:677
  485.3 15.8 %collective-permute-start.37 = (bf16[512,512]{1,0:T(8,128)(2,1)S(1)}, bf16[512,512]{1,0:T(8,128)(2,1)}, u32[]{:S(2)}, u32[]{:S(2)}) collective-permute-start(bf16[512,512]{1,0:T(8,128)(2,1)S(1)} %constant_dynamic-slice_fusion), channel_id=1, source_target_pairs={{0,1},{1,3},{3,2},{2,0},{4,5},{5,7},{7,6},{6,4},{8,9},{9,11},{11,1... | collective-permute-start | bytes 1572872 | tf_op jit(solution)/shard_map/ppermute | solution.py:552
  496.2 14.5 %collective-permute-start.41 = (bf16[512,512]{1,0:T(8,128)(2,1)}, bf16[512,512]{1,0:T(8,128)(2,1)}, u32[]{:S(2)}, u32[]{:S(2)}) collective-permute-start(bf16[512,512]{1,0:T(8,128)(2,1)} %add_convert_fusion.7), channel_id=1, source_target_pairs={{0,1},{1,3},{3,2},{2,0},{4,5},{5,7},{7,6},{6,4},{8,9},{9,11},{11,1... | collective-permute-start | bytes 1572872 | tf_op jit(solution)/shard_map/ppermute | solution.py:552
  504.6 17.2 %collective-permute-start.45 = (bf16[512,512]{1,0:T(8,128)(2,1)S(1)}, bf16[512,512]{1,0:T(8,128)(2,1)S(1)}, u32[]{:S(2)}, u32[]{:S(2)}) collective-permute-start(bf16[512,512]{1,0:T(8,128)(2,1)S(1)} %add_convert_fusion.6), channel_id=1, source_target_pairs={{0,1},{1,3},{3,2},{2,0},{4,5},{5,7},{7,6},{6,4},{8,9},{9,11},{11,1... | collective-permute-start | bytes 1572872 | tf_op jit(solution)/shard_map/ppermute | solution.py:552
  504.7 17.2 %collective-permute-start.43 = (bf16[256,1024]{1,0:T(8,128)(2,1)S(1)}, bf16[256,1024]{1,0:T(8,128)(2,1)S(1)}, u32[]{:S(2)}, u32[]{:S(2)}) collective-permute-start(bf16[256,1024]{1,0:T(8,128)(2,1)S(1)} %broadcast_select_fusion.7), channel_id=1, source_target_pairs={{0,16},{4,20},{8,24},{12,28},{16,0},{20,4},{24,8},{28,12},{1,17},{... | collective-permute-start | bytes 1572872 | tf_op jit(solution)/shard_map/ppermute | solution.py:648
  508.0 17.9 %collective-permute-start.44 = (bf16[256,1152]{1,0:T(8,128)(2,1)S(1)}, bf16[256,1152]{1,0:T(8,128)(2,1)S(1)}, u32[]{:S(2)}, u32[]{:S(2)}) collective-permute-start(bf16[256,1152]{1,0:T(8,128)(2,1)S(1)} %broadcast_select_fusion.2), channel_id=1, source_target_pairs={{0,8},{4,12},{8,0},{12,4},{16,24},{20,28},{24,16},{28,20},{1,9},{5... | collective-permute-start | bytes 1769480 | tf_op jit(solution)/shard_map/ppermute | solution.py:648
  512.9 21.8 %collective-permute-start.46 = (bf16[512,512]{1,0:T(8,128)(2,1)}, bf16[512,512]{1,0:T(8,128)(2,1)}, u32[]{:S(2)}, u32[]{:S(2)}) collective-permute-start(bf16[512,512]{1,0:T(8,128)(2,1)} %add_convert_fusion.5), channel_id=1, source_target_pairs={{0,1},{1,3},{3,2},{2,0},{4,5},{5,7},{7,6},{6,4},{8,9},{9,11},{11,1... | collective-permute-start | bytes 1572872 | tf_op jit(solution)/shard_map/ppermute | solution.py:552
  530.6 13.1 %collective-permute-start.49 = (bf16[512,512]{1,0:T(8,128)(2,1)}, bf16[512,512]{1,0:T(8,128)(2,1)}, u32[]{:S(2)}, u32[]{:S(2)}) collective-permute-start(bf16[512,512]{1,0:T(8,128)(2,1)} %add_convert_fusion.3), channel_id=1, source_target_pairs={{0,1},{1,3},{3,2},{2,0},{4,5},{5,7},{7,6},{6,4},{8,9},{9,11},{11,1... | collective-permute-start | bytes 1572872 | tf_op jit(solution)/shard_map/ppermute | solution.py:552
  (105 other events, 1025.5 us)
Sparse Core Ops, SparseCore 0:
  93.5 54.1 all-gather.1
  280.6 57.2 reduce-scatter.3
  353.4 87.3 reduce-scatter.5
  481.1 46.0 reduce-scatter.7

commit v4 on v3

--- a/solution.py
+++ b/solution.py
@@ -818,43 +818,38 @@
 
     in_a = ring.gather(block_input[0])
     slice_rows = w_out.shape[0] // groups_count
-    gain_rows = jnp.pad(jnp.stack([attn_gain, mlp_gain]), ((0, 14), (0, features - width)))
+    gains = ring.gather(jnp.stack([attn_gain, mlp_gain]))
     shares = ring.gather(
-        jnp.concatenate(
-            [
-                lax.dynamic_slice_in_dim(w_out, lax.axis_index(DP) * slice_rows, slice_rows, axis=0),
-                gain_rows,
-            ],
-            axis=0,
-        )
+        lax.dynamic_slice_in_dim(w_out, lax.axis_index(DP) * slice_rows, slice_rows, axis=0)
     )
     every.blocks = block_input
+    gains.hop()
     in_a.hop()
     shares.hop()
     pad = jnp.zeros((features, CH - 2 * heads), bf16)
     last = lax.optimization_barrier(jnp.concatenate([w_alpha, w_beta, pad], axis=1))
     every.w_in = jnp.concatenate([w_query, w_key, w_value, w_gate, last], axis=1)
-    ring.tick(in_a, shares)
+    ring.tick(in_a, shares, gains)
     in_b = ring.gather(every.blocks[1])
     del every.blocks
+    gains.hop()
     in_a.hop()
     shares.hop()
     for m in micros:
         m.grad_product = matmul_back(grad_output(m), w_down, bf16)
-    ring.tick(in_a, shares)
+    ring.tick(in_a, shares, gains)
+    gains.hop()
     in_a.hop()
+    ring.tick(in_a, gains)
+    in_b.hop()
     shares.hop()
-    ring.tick(in_a, shares)
-    in_b.hop()
-    every.gains = jnp.concatenate(
-        [block[slice_rows : slice_rows + 2, :width] for block in shares.blocks()], axis=1
-    ).astype(f32)
+    every.gains = gains.take().astype(f32)
     normalise(a, in_a.take())
     project(a)
-    ring.tick(in_b)
+    ring.tick(in_b, shares)
     in_b.hop()
     w_out_full = lax.all_gather(
-        jnp.stack([block[:slice_rows] for block in shares.take_blocks()]), DP, axis=1, tiled=True
+        jnp.stack(shares.take_blocks()), DP, axis=1, tiled=True
     ).reshape(-1, features)
     mix(a)
     every.w_ups = [w_mlp_gate, w_mlp_up]

time: 565 us -> 558 us (0.988)
    ppermute x39 -> x42, waiting for transfers between devices: 114 us -> 110 us  [send(): return lax.ppermute(block, HEAD, self.pairs)]
    ppermute x39 -> x42, starting transfers between devices: 47.6 us -> 45.7 us  [send(): return lax.ppermute(block, HEAD, self.pairs)]
    unnamed x209 -> x213, local copies, waits for them, and re-layouts: 20.9 us -> 21.8 us
  transfers between devices with their start and end apart: 54 -> 57, of which waited for: 23 -> 22; matrix products, arithmetic and copies ran while one was open for 46% -> 47% of each run, Pallas kernels for 13% -> 13%
where the time goes in v4:
time: 558 us; the launch traced here: 550 us
  matrix products  147 us (26%)
  waiting for transfers between devices  122 us (22%)
  other arithmetic  98.1 us (18%)
  Pallas kernels  69.7 us (12%)
  starting transfers between devices  57.7 us (10%)
  local copies, waits for them, and re-layouts  40.8 us (7%)
  between operations  15.8 us (3%)
    ppermute x42, waiting for transfers between devices, send(): return lax.ppermute(block, HEAD, self.pairs)  110 us
    dot_general x8, matrix products, matmul(): return jnp.dot(former, latter, preferred_element_type=f32).astype(kind)  52.6 us
    dot_general x5, matrix products, matmul_rows(): lax.dot_general(former, latter, (((0,), (0,)), ((), ())), preferred_eleme...  49.6 us
    ppermute x42, starting transfers between devices, send(): return lax.ppermute(block, HEAD, self.pairs)  45.7 us
    dot_general x8, matrix products, matmul_back(): lax.dot_general(former, latter, (((1,), (1,)), ((), ())), preferred_eleme...  44.7 us
    pallas_call x4, Pallas kernels, mixer_backward(): pl.pallas_call(kernel, grid=(1,), in_specs=in_specs, out_specs=[pl.BlockS...  44.1 us
    pallas_call x2, Pallas kernels, mixer_forward(): pl.pallas_call(forward_kernel, grid=(rows // SEQ,), in_specs=[row_spec(pr...  25.6 us
    unnamed x213, local copies, waits for them, and re-layouts  21.8 us
  transfers between devices with their start and end apart: 57, of which 22 were waited for; matrix products, arithmetic and copies ran while one was open for 47% of the time, Pallas kernels for 13%

profile of v4, /device:TPU:0, one launch (start us, length us, event | category | flops | bytes accessed | tf_op | source)
XLA Modules:
  0.0 550.5 jit_solution(3722949437550177123)
XLA Ops:
  8.8 3.1 collective-permute-start.1
  24.2 3.5 copy-done.88
  27.7 4.5 convolution_convert_fusion.6
  36.8 4.5 convolution_convert_fusion.5
  44.0 10.5 %collective-permute-done.4 = bf16[2,512]{1,0:T(2,128)(2,1)S(1)} collective-permute-done((bf16[2,512]{1,0:T(2,128)(2,1)S(1)}, bf16[2,512]{1,0:T(2,128)(2,1)S(1)}, u32[]{:S(2)}, u32[]{:S(2)}) %collective-permute-start.4) | collective-permute-done | bytes 2080 | tf_op jit(solution)/shard_map/ppermute | solution.py:552
  57.1 11.0 %collective-permute-done.7 = bf16[2,512]{1,0:T(2,128)(2,1)S(1)} collective-permute-done((bf16[2,512]{1,0:T(2,128)(2,1)S(1)}, bf16[2,512]{1,0:T(2,128)(2,1)S(1)}, u32[]{:S(2)}, u32[]{:S(2)}) %collective-permute-start.7) | collective-permute-done | bytes 2080 | tf_op jit(solution)/shard_map/ppermute | solution.py:552
  74.8 6.6 %fusion.92.pre_ref.refs_0_ = f32[512,2176]{1,0:T(8,128)} fusion(bf16[512,2048]{1,0:T(8,128)(2,1)S(1)} %fusion.5, bf16[2048,2176]{1,0:T(8,128)(2,1)S(1)} %copy-done.66), kind=kOutput, calls=%fused_computation.271 | convolution fusion | flops 4563402752 | bytes 15466496 | tf_op jit(solution)/shard_map/dot_general | solution.py:484
  81.4 4.6 collective-permute-done.9
  89.4 12.9 %mixer_forward.2 = (bf16[512,512]{1,0:T(8,128)(2,1)}, f32[512,512]{1,0:T(8,128)}, f32[512,512]{1,0:T(8,128)}, f32[512,512]{1,0:T(8,128)}) custom-call(f32[512,2176]{1,0:T(8,128)} %fusion.92.pre_ref.refs_0_, f32[3,4,512]{2,1,0:T(4,128)} %refs_1_.7, f32[2,4]{1,0:T(2,128)} %pad_maximum_fusion.15.decay_ref.refs_2_, f32[1,128]{1,0:T(1,128)} %bitcast.142), custom_call_target="tpu_custom_call" | custom-call | flops 10000000000 | bytes 10000000 | tf_op jit(solution)/shard_map/mixer_forward/pallas_call | solution.py:421
  104.3 9.8 %pad_maximum_fusion = bf16[2048,2816]{1,0:T(8,128)(2,1)} fusion(bf16[2048,1408]{1,0:T(8,128)(2,1)S(1)} %bitcast.103, bf16[2048,1408]{1,0:T(8,128)(2,1)} %param.35), kind=kLoop, calls=%fused_computation | loop fusion | flops 23068672 | bytes 23068672 | tf_op jit(solution)/shard_map/concatenate | solution.py:860
  114.1 10.7 %collective-permute-done.11 = bf16[512,512]{1,0:T(8,128)(2,1)S(1)} collective-permute-done((bf16[512,512]{1,0:T(8,128)(2,1)}, bf16[512,512]{1,0:T(8,128)(2,1)S(1)}, u32[]{:S(2)}, u32[]{:S(2)}) %collective-permute-start.11) | collective-permute-done | bytes 524320 | tf_op jit(solution)/shard_map/ppermute | solution.py:552
  129.2 6.6 %fusion.93.pre_ref.refs_0_ = f32[512,2176]{1,0:T(8,128)} fusion(bf16[512,2048]{1,0:T(8,128)(2,1)S(1)} %fusion.8, bf16[2048,2176]{1,0:T(8,128)(2,1)S(1)} %bitcast.108), kind=kOutput, calls=%fused_computation.272 | convolution fusion | flops 4563402752 | bytes 15466496 | tf_op jit(solution)/shard_map/dot_general | solution.py:484
  136.8 12.7 %mixer_forward.3 = (bf16[512,512]{1,0:T(8,128)(2,1)}, f32[512,512]{1,0:T(8,128)}, f32[512,512]{1,0:T(8,128)}, f32[512,512]{1,0:T(8,128)}) custom-call(f32[512,2176]{1,0:T(8,128)} %fusion.93.pre_ref.refs_0_, f32[3,4,512]{2,1,0:T(4,128)} %refs_1_.7, f32[2,4]{1,0:T(2,128)} %pad_maximum_fusion.15.decay_ref.refs_2_, f32[1,128]{1,0:T(1,128)} %bitcast.143), custom_call_target="tpu_custom_call" | custom-call | flops 10000000000 | bytes 10000000 | tf_op jit(solution)/shard_map/mixer_forward/pallas_call | solution.py:421
  152.6 12.3 %collective-permute-done.14 = bf16[512,512]{1,0:T(8,128)(2,1)} collective-permute-done((bf16[512,512]{1,0:T(8,128)(2,1)S(1)}, bf16[512,512]{1,0:T(8,128)(2,1)}, u32[]{:S(2)}, u32[]{:S(2)}) %collective-permute-start.14) | collective-permute-done | bytes 524320 | tf_op jit(solution)/shard_map/ppermute | solution.py:552
  166.8 7.2 %convert_add_fusion.1 = f32[512,2048]{1,0:T(8,128)S(1)} fusion(bf16[512,2048]{1,0:T(8,128)(2,1)S(1)} %copy-done.6, bf16[2048,2048]{1,0:T(8,128)(2,1)} %bitcast.138, bf16[512,512]{1,0:T(8,128)(2,1)S(1)} %get-tuple-element.2113, bf16[512,512]{1,0:T(8,128)(2,1)S(1)} %get-tuple-element.2114, bf16[512,512]{1,0:T(8,128)(2,1)S(1)} %get-tuple-element.2115, ...), kind=kOutput, calls=%fused_computation.49 | convolution fusion | flops 4305453056 | bytes 16777216 | tf_op jit(solution)/shard_map/dot_general | solution.py:484
  176.0 6.2 %fusion.94 = f32[512,2816]{1,0:T(8,128)S(1)} fusion(bf16[512,2048]{1,0:T(8,128)(2,1)S(1)} %multiply_convert_fusion.1, bf16[2048,2816]{1,0:T(8,128)(2,1)S(1)} %bitcast.101), kind=kOutput, calls=%fused_computation.273 | convolution fusion | flops 5905580032 | bytes 19398656 | tf_op jit(solution)/shard_map/dot_general | solution.py:484
  182.2 8.8 %collective-permute-done.16 = bf16[512,512]{1,0:T(8,128)(2,1)} collective-permute-done((bf16[512,512]{1,0:T(8,128)(2,1)}, bf16[512,512]{1,0:T(8,128)(2,1)}, u32[]{:S(2)}, u32[]{:S(2)}) %collective-permute-start.16) | collective-permute-done | bytes 524320 | tf_op jit(solution)/shard_map/ppermute | solution.py:552
  193.8 6.4 %convolution_convert_fusion.4 = bf16[512,2048]{1,0:T(8,128)(2,1)S(1)} fusion(bf16[2048,2816]{1,0:T(8,128)(2,1)S(1)} %bitcast.101, bf16[512,1408]{1,0:T(8,128)(2,1)S(1)} %get-tuple-element.2079, bf16[512,1408]{1,0:T(8,128)(2,1)S(1)} %get-tuple-element.2078), kind=kOutput, calls=%fused_computation.56 | convolution fusion | flops 5912395776 | bytes 16515072 | tf_op jit(solution)/shard_map/dot_general | solution.py:494
  201.9 4.0 collective-permute-done.17
  207.7 7.0 %convert_add_fusion = f32[512,2048]{1,0:T(8,128)S(1)} fusion(bf16[512,2048]{1,0:T(8,128)(2,1)S(1)} %copy-done.9, bf16[2048,2048]{1,0:T(8,128)(2,1)} %bitcast.139, bf16[512,512]{1,0:T(8,128)(2,1)S(1)} %get-tuple-element.2109, bf16[512,512]{1,0:T(8,128)(2,1)S(1)} %get-tuple-element.2110, bf16[512,512]{1,0:T(8,128)(2,1)S(1)} %get-tuple-element.2111, ...), kind=kOutput, calls=%fused_computation.46 | convolution fusion | flops 4305453056 | bytes 16777216 | tf_op jit(solution)/shard_map/dot_general | solution.py:484
  214.7 6.1 %collective-permute-done.18 = bf16[512,512]{1,0:T(8,128)(2,1)S(1)} collective-permute-done((bf16[512,512]{1,0:T(8,128)(2,1)S(1)}, bf16[512,512]{1,0:T(8,128)(2,1)S(1)}, u32[]{:S(2)}, u32[]{:S(2)}) %collective-permute-start.18) | collective-permute-done | bytes 524320 | tf_op jit(solution)/shard_map/ppermute | solution.py:552
  222.3 6.2 %fusion.95 = f32[512,2816]{1,0:T(8,128)S(1)} fusion(bf16[512,2048]{1,0:T(8,128)(2,1)S(1)} %multiply_convert_fusion, bf16[2048,2816]{1,0:T(8,128)(2,1)S(1)} %bitcast.101), kind=kOutput, calls=%fused_computation.274 | convolution fusion | flops 5905580032 | bytes 19398656 | tf_op jit(solution)/shard_map/dot_general | solution.py:484
  228.5 6.5 %collective-permute-done.19 = bf16[512,512]{1,0:T(8,128)(2,1)S(1)} collective-permute-done((bf16[512,512]{1,0:T(8,128)(2,1)S(1)}, bf16[512,512]{1,0:T(8,128)(2,1)S(1)}, u32[]{:S(2)}, u32[]{:S(2)}) %collective-permute-start.19) | collective-permute-done | bytes 524320 | tf_op jit(solution)/shard_map/ppermute | solution.py:552
  235.2 2.9 fusion.38
  238.3 12.7 %collective-permute-done.20 = bf16[512,512]{1,0:T(8,128)(2,1)S(1)} collective-permute-done((bf16[512,512]{1,0:T(8,128)(2,1)S(1)}, bf16[512,512]{1,0:T(8,128)(2,1)S(1)}, u32[]{:S(2)}, u32[]{:S(2)}) %collective-permute-start.20) | collective-permute-done | bytes 524320 | tf_op jit(solution)/shard_map/ppermute | solution.py:552
  252.0 6.4 %convolution_convert_fusion.3 = bf16[512,2048]{1,0:T(8,128)(2,1)S(1)} fusion(bf16[512,2816]{1,0:T(8,128)(2,1)S(1)} %pad_maximum_fusion.2, bf16[2048,2816]{1,0:T(8,128)(2,1)S(1)} %bitcast.101), kind=kOutput, calls=%fused_computation.55 | convolution fusion | flops 5906628608 | bytes 16515072 | tf_op jit(solution)/shard_map/dot_general | solution.py:494
  260.5 3.0 collective-permute-start.22
  263.5 9.8 %convolution_convert_fusion.1 = bf16[1408,2048]{1,0:T(8,128)(2,1)} fusion(bf16[512,2048]{1,0:T(8,128)(2,1)S(1)} %copy-done.12, bf16[512,2048]{1,0:T(8,128)(2,1)S(1)} %copy-done.15, bf16[512,1408]{1,0:T(8,128)(2,1)} %get-tuple-element.1439, bf16[512,1408]{1,0:T(8,128)(2,1)} %get-tuple-element.1428), kind=kOutput, calls=%fused_computation.3 | convolution fusion | flops 5922619392 | bytes 12845056 | tf_op jit(solution)/shard_map/dot_general | solution.py:488
  273.6 18.4 %convolution_convert_fusion = bf16[2048,2816]{1,0:T(8,128)(2,1)} fusion(bf16[512,2816]{1,0:T(8,128)(2,1)} %copy-done.31, bf16[512,2816]{1,0:T(8,128)(2,1)} %pad_maximum_fusion.1, bf16[512,2048]{1,0:T(8,128)(2,1)} %copy-done.35, bf16[512,2048]{1,0:T(8,128)(2,1)} %copy-done.34), kind=kOutput, calls=%fused_computation.1 | convolution fusion | flops 11836850176 | bytes 21495808 | tf_op jit(solution)/shard_map/dot_general | solution.py:488
  295.5 8.3 %convolution_convert_fusion.8 = bf16[512,2048]{1,0:T(8,128)(2,1)} fusion(bf16[512,1408]{1,0:T(8,128)(2,1)} %get-tuple-element.1428, bf16[1408,2048]{1,0:T(8,128)(2,1)} %param.37), kind=kOutput, calls=%fused_computation.60 | convolution fusion | flops 2953838592 | bytes 9306112 | tf_op jit(solution)/shard_map/dot_general | solution.py:484
  303.8 4.6 convolution_convert_fusion.7
  317.0 6.7 %collective-permute-done.25 = bf16[512,512]{1,0:T(8,128)(2,1)S(1)} collective-permute-done((bf16[512,512]{1,0:T(8,128)(2,1)}, bf16[512,512]{1,0:T(8,128)(2,1)S(1)}, u32[]{:S(2)}, u32[]{:S(2)}) %collective-permute-start.25) | collective-permute-done | bytes 524320 | tf_op jit(solution)/shard_map/ppermute | solution.py:552
  335.1 10.9 %mixer_backward.4 = (bf16[1024,2176]{1,0:T(8,128)(2,1)}, f32[16,512]{1,0:T(8,128)}, f32[2,4]{1,0:T(2,128)}, f32[256,1]{1,0:T(8,128)}) custom-call(f32[512,2176]{1,0:T(8,128)} %fusion.92.pre_ref.refs_0_, f32[3,4,512]{2,1,0:T(4,128)} %refs_1_.7, f32[2,4]{1,0:T(2,128)} %pad_maximum_fusion.15.decay_ref.refs_2_, f32[1,128]{1,0:T(1,128)} %bitcast.144, ...), custom_call_target="tpu_custom_call" | custom-call | flops 10000000000 | bytes 10000000 | tf_op jit(solution)/shard_map/mixer_backward/pallas_call | solution.py:456
  347.1 2.8 collective-permute-start.28
  349.9 10.9 %mixer_backward.5 = (bf16[1024,2176]{1,0:T(8,128)(2,1)}, f32[16,512]{1,0:T(8,128)}, f32[2,4]{1,0:T(2,128)}, f32[256,1]{1,0:T(8,128)}) custom-call(f32[512,2176]{1,0:T(8,128)} %fusion.92.pre_ref.refs_0_, f32[3,4,512]{2,1,0:T(4,128)} %refs_1_.7, f32[2,4]{1,0:T(2,128)} %pad_maximum_fusion.15.decay_ref.refs_2_, ...), custom_call_target="tpu_custom_call", output_to_operand_aliasing={{0}: (10, {})} | custom-call | flops 10000000000 | bytes 10000000 | tf_op jit(solution)/shard_map/mixer_backward/pallas_call | solution.py:456
  362.4 9.2 %convolution_convert_fusion.10 = bf16[512,2048]{1,0:T(8,128)(2,1)S(1)} fusion(bf16[2048,2176]{1,0:T(8,128)(2,1)} %copy-done.65, bf16[1024,2176]{1,0:T(8,128)(2,1)} %get-tuple-element.1698.refs_10_), kind=kOutput, calls=%fused_computation.62 | convolution fusion | flops 4564451328 | bytes 13238272 | tf_op jit(solution)/shard_map/dot_general | solution.py:494
  383.3 3.4 collective-permute-start.31
  386.7 10.9 %mixer_backward.6 = (bf16[1024,2176]{1,0:T(8,128)(2,1)}, f32[16,512]{1,0:T(8,128)}, f32[2,4]{1,0:T(2,128)}, f32[256,1]{1,0:T(8,128)}) custom-call(f32[512,2176]{1,0:T(8,128)} %fusion.93.pre_ref.refs_0_, f32[3,4,512]{2,1,0:T(4,128)} %refs_1_.7, f32[2,4]{1,0:T(2,128)} %pad_maximum_fusion.15.decay_ref.refs_2_, ...), custom_call_target="tpu_custom_call", output_to_operand_aliasing={{0}: (10, {})} | custom-call | flops 10000000000 | bytes 10000000 | tf_op jit(solution)/shard_map/mixer_backward/pallas_call | solution.py:456
  397.6 11.3 %mixer_backward.7 = (bf16[1024,2176]{1,0:T(8,128)(2,1)}, f32[16,512]{1,0:T(8,128)}, f32[2,4]{1,0:T(2,128)}, f32[256,1]{1,0:T(8,128)}) custom-call(f32[512,2176]{1,0:T(8,128)} %fusion.93.pre_ref.refs_0_, f32[3,4,512]{2,1,0:T(4,128)} %refs_1_.7, f32[2,4]{1,0:T(2,128)} %pad_maximum_fusion.15.decay_ref.refs_2_, ...), custom_call_target="tpu_custom_call", output_to_operand_aliasing={{0}: (10, {})} | custom-call | flops 10000000000 | bytes 10000000 | tf_op jit(solution)/shard_map/mixer_backward/pallas_call | solution.py:456
  411.2 9.0 %convolution_convert_fusion.2 = bf16[1024,2176]{1,0:T(8,128)(2,1)} fusion(bf16[1024,1024]{1,0:T(8,128)(2,1)S(1)} %copy-done.40, bf16[1024,2176]{1,0:T(8,128)(2,1)} %get-tuple-element.1833), kind=kOutput, calls=%fused_computation.7 | convolution fusion | flops 4565630976 | bytes 11010048 | tf_op jit(solution)/shard_map/dot_general | solution.py:488
  426.2 9.3 %convolution_convert_fusion.9 = bf16[512,2048]{1,0:T(8,128)(2,1)} fusion(bf16[2048,2176]{1,0:T(8,128)(2,1)} %copy-done.65, bf16[1024,2176]{1,0:T(8,128)(2,1)} %get-tuple-element.1833), kind=kOutput, calls=%fused_computation.61 | convolution fusion | flops 4564451328 | bytes 13238272 | tf_op jit(solution)/shard_map/dot_general | solution.py:494
  435.5 3.5 collective-permute-done.33
  441.2 8.6 %add_convert_fusion = bf16[1024,2176]{1,0:T(8,128)(2,1)S(1)} fusion(bf16[1024,2176]{1,0:T(8,128)(2,1)} %collective-permute-done.34, bf16[1024,1024]{1,0:T(8,128)(2,1)} %pad_maximum_fusion.4, bf16[1024,2176]{1,0:T(8,128)(2,1)} %get-tuple-element.1833), kind=kOutput, calls=%fused_computation.2 | convolution fusion | flops 4570087424 | bytes 15466496 | tf_op jit(solution)/shard_map/dot_general | solution.py:488
  463.9 3.8 fusion.29
  489.9 4.6 collective-permute-done.41
  509.3 5.1 collective-permute-done.48
  514.5 5.2 collective-permute-done.47
  532.9 4.7 collective-permute-done.52
  (453 shorter events, 177.2 us)
Async XLA Ops:
  7.2 157.7 %all-gather.2.cloned.1.call-start = ((), (), s32[]{:S(2)}) async-start(), calls=%async_computation.3 | async-start | bytes 9437184 | tf_op jit(solution)/shard_map/all_gather | solution.py:851
  8.8 26.0 %collective-permute-start.1 = (bf16[2,512]{1,0:T(2,128)(2,1)S(1)}, bf16[2,512]{1,0:T(2,128)(2,1)S(1)}, u32[]{:S(2)}, u32[]{:S(2)}) collective-permute-start(bf16[2,512]{1,0:T(2,128)(2,1)S(1)} %pad_maximum_fusion.14), channel_id=1, source_target_pairs={{0,1},{1,3},{3,2},{2,0},{4,5},{5,7},{7,6},{6,4},{8,9},{9,11},{11,1... | collective-permute-start | bytes 6152 | tf_op jit(solution)/shard_map/ppermute | solution.py:552
  11.9 22.9 %collective-permute-start.2 = (bf16[64,2048]{1,0:T(8,128)(2,1)S(1)}, bf16[64,2048]{1,0:T(8,128)(2,1)}, u32[]{:S(2)}, u32[]{:S(2)}) collective-permute-start(bf16[64,2048]{1,0:T(8,128)(2,1)S(1)} %constant_dynamic-slice_fusion.6), channel_id=1, source_target_pairs={{0,1},{1,3},{3,2},{2,0},{4,5},{5,7},{7,6},{6,4},{8,9},{9,11},{11,1... | collective-permute-start | bytes 786440 | tf_op jit(solution)/shard_map/ppermute | solution.py:552
  16.4 18.4 %collective-permute-start = (bf16[512,512]{1,0:T(8,128)(2,1)}, bf16[512,512]{1,0:T(8,128)(2,1)}, u32[]{:S(2)}, u32[]{:S(2)}) collective-permute-start(bf16[512,512]{1,0:T(8,128)(2,1)} %slice_bitcast_fusion.1), channel_id=1, source_target_pairs={{0,1},{1,3},{3,2},{2,0},{4,5},{5,7},{7,6},{6,4},{8,9},{9,11},{11,1... | collective-permute-start | bytes 1572872 | tf_op jit(solution)/shard_map/ppermute | solution.py:552
  34.8 19.6 %collective-permute-start.5 = (bf16[64,2048]{1,0:T(8,128)(2,1)}, bf16[64,2048]{1,0:T(8,128)(2,1)S(1)}, u32[]{:S(2)}, u32[]{:S(2)}) collective-permute-start(bf16[64,2048]{1,0:T(8,128)(2,1)} %collective-permute-done.2), channel_id=1, source_target_pairs={{0,1},{1,3},{3,2},{2,0},{4,5},{5,7},{7,6},{6,4},{8,9},{9,11},{11,1... | collective-permute-start | bytes 786440 | tf_op jit(solution)/shard_map/ppermute | solution.py:552
  34.9 19.6 %collective-permute-start.3 = (bf16[512,512]{1,0:T(8,128)(2,1)}, bf16[512,512]{1,0:T(8,128)(2,1)S(1)}, u32[]{:S(2)}, u32[]{:S(2)}) collective-permute-start(bf16[512,512]{1,0:T(8,128)(2,1)} %collective-permute-done), channel_id=1, source_target_pairs={{0,1},{1,3},{3,2},{2,0},{4,5},{5,7},{7,6},{6,4},{8,9},{9,11},{11,1... | collective-permute-start | bytes 1572872 | tf_op jit(solution)/shard_map/ppermute | solution.py:552
  41.3 13.1 %collective-permute-start.4 = (bf16[2,512]{1,0:T(2,128)(2,1)S(1)}, bf16[2,512]{1,0:T(2,128)(2,1)S(1)}, u32[]{:S(2)}, u32[]{:S(2)}) collective-permute-start(bf16[2,512]{1,0:T(2,128)(2,1)S(1)} %collective-permute-done.1), channel_id=1, source_target_pairs={{0,1},{1,3},{3,2},{2,0},{4,5},{5,7},{7,6},{6,4},{8,9},{9,11},{11,1... | collective-permute-start | bytes 6152 | tf_op jit(solution)/shard_map/ppermute | solution.py:552
  68.1 13.2 %collective-permute-start.8 = (bf16[64,2048]{1,0:T(8,128)(2,1)}, bf16[64,2048]{1,0:T(8,128)(2,1)S(1)}, u32[]{:S(2)}, u32[]{:S(2)}) collective-permute-start(bf16[64,2048]{1,0:T(8,128)(2,1)} %copy-done.67), channel_id=1, source_target_pairs={{0,1},{1,3},{3,2},{2,0},{4,5},{5,7},{7,6},{6,4},{8,9},{9,11},{11,1... | collective-permute-start | bytes 786440 | tf_op jit(solution)/shard_map/ppermute | solution.py:552
  68.2 17.8 %collective-permute-start.9 = (bf16[512,512]{1,0:T(8,128)(2,1)S(1)}, bf16[512,512]{1,0:T(8,128)(2,1)}, u32[]{:S(2)}, u32[]{:S(2)}) collective-permute-start(bf16[512,512]{1,0:T(8,128)(2,1)S(1)} %slice_bitcast_fusion), channel_id=1, source_target_pairs={{0,1},{1,3},{3,2},{2,0},{4,5},{5,7},{7,6},{6,4},{8,9},{9,11},{11,1... | collective-permute-start | bytes 1572872 | tf_op jit(solution)/shard_map/ppermute | solution.py:552
  88.2 258.8 %reduce-scatter.4.cloned.1.call-start = ((), (), s32[]{:S(2)}) async-start(), calls=%async_computation.4 | async-start | bytes 6488064 | tf_op jit(solution)/shard_map/reduce_scatter | solution.py:909
  88.9 13.4 %collective-permute-start.10 = (bf16[512,512]{1,0:T(8,128)(2,1)}, bf16[512,512]{1,0:T(8,128)(2,1)}, u32[]{:S(2)}, u32[]{:S(2)}) collective-permute-start(bf16[512,512]{1,0:T(8,128)(2,1)} %collective-permute-done.9), channel_id=1, source_target_pairs={{0,1},{1,3},{3,2},{2,0},{4,5},{5,7},{7,6},{6,4},{8,9},{9,11},{11,1... | collective-permute-start | bytes 1572872 | tf_op jit(solution)/shard_map/ppermute | solution.py:552
  102.2 33.6 %collective-permute-start.12 = (bf16[512,512]{1,0:T(8,128)(2,1)}, bf16[512,512]{1,0:T(8,128)(2,1)}, u32[]{:S(2)}, u32[]{:S(2)}) collective-permute-start(bf16[512,512]{1,0:T(8,128)(2,1)} %get-tuple-element.1866), channel_id=1, source_target_pairs={{0,1},{1,3},{3,2},{2,0},{4,5},{5,7},{7,6},{6,4},{8,9},{9,11},{11,1... | collective-permute-start | bytes 1572872 | tf_op jit(solution)/shard_map/ppermute | solution.py:552
  104.2 20.6 %collective-permute-start.11 = (bf16[512,512]{1,0:T(8,128)(2,1)}, bf16[512,512]{1,0:T(8,128)(2,1)S(1)}, u32[]{:S(2)}, u32[]{:S(2)}) collective-permute-start(bf16[512,512]{1,0:T(8,128)(2,1)} %collective-permute-done.10), channel_id=1, source_target_pairs={{0,1},{1,3},{3,2},{2,0},{4,5},{5,7},{7,6},{6,4},{8,9},{9,11},{11,1... | collective-permute-start | bytes 1572872 | tf_op jit(solution)/shard_map/ppermute | solution.py:552
  135.8 13.6 %collective-permute-start.13 = (bf16[512,512]{1,0:T(8,128)(2,1)}, bf16[512,512]{1,0:T(8,128)(2,1)S(1)}, u32[]{:S(2)}, u32[]{:S(2)}) collective-permute-start(bf16[512,512]{1,0:T(8,128)(2,1)} %collective-permute-done.12), channel_id=1, source_target_pairs={{0,1},{1,3},{3,2},{2,0},{4,5},{5,7},{7,6},{6,4},{8,9},{9,11},{11,1... | collective-permute-start | bytes 1572872 | tf_op jit(solution)/shard_map/ppermute | solution.py:552
  149.5 15.4 %collective-permute-start.14 = (bf16[512,512]{1,0:T(8,128)(2,1)S(1)}, bf16[512,512]{1,0:T(8,128)(2,1)}, u32[]{:S(2)}, u32[]{:S(2)}) collective-permute-start(bf16[512,512]{1,0:T(8,128)(2,1)S(1)} %collective-permute-done.13), channel_id=1, source_target_pairs={{0,1},{1,3},{3,2},{2,0},{4,5},{5,7},{7,6},{6,4},{8,9},{9,11},{11,1... | collective-permute-start | bytes 1572872 | tf_op jit(solution)/shard_map/ppermute | solution.py:552
  150.7 23.2 %collective-permute-start.15 = (bf16[512,512]{1,0:T(8,128)(2,1)}, bf16[512,512]{1,0:T(8,128)(2,1)}, u32[]{:S(2)}, u32[]{:S(2)}) collective-permute-start(bf16[512,512]{1,0:T(8,128)(2,1)} %get-tuple-element.1867), channel_id=1, source_target_pairs={{0,1},{1,3},{3,2},{2,0},{4,5},{5,7},{7,6},{6,4},{8,9},{9,11},{11,1... | collective-permute-start | bytes 1572872 | tf_op jit(solution)/shard_map/ppermute | solution.py:552
  174.7 16.2 %collective-permute-start.16 = (bf16[512,512]{1,0:T(8,128)(2,1)}, bf16[512,512]{1,0:T(8,128)(2,1)}, u32[]{:S(2)}, u32[]{:S(2)}) collective-permute-start(bf16[512,512]{1,0:T(8,128)(2,1)} %collective-permute-done.15), channel_id=1, source_target_pairs={{0,1},{1,3},{3,2},{2,0},{4,5},{5,7},{7,6},{6,4},{8,9},{9,11},{11,1... | collective-permute-start | bytes 1572872 | tf_op jit(solution)/shard_map/ppermute | solution.py:552
  191.0 15.0 %collective-permute-start.17 = (bf16[512,512]{1,0:T(8,128)(2,1)}, bf16[512,512]{1,0:T(8,128)(2,1)}, u32[]{:S(2)}, u32[]{:S(2)}) collective-permute-start(bf16[512,512]{1,0:T(8,128)(2,1)} %collective-permute-done.16), channel_id=1, source_target_pairs={{0,1},{1,3},{3,2},{2,0},{4,5},{5,7},{7,6},{6,4},{8,9},{9,11},{11,1... | collective-permute-start | bytes 1572872 | tf_op jit(solution)/shard_map/ppermute | solution.py:552
  206.0 14.8 %collective-permute-start.18 = (bf16[512,512]{1,0:T(8,128)(2,1)S(1)}, bf16[512,512]{1,0:T(8,128)(2,1)S(1)}, u32[]{:S(2)}, u32[]{:S(2)}) collective-permute-start(bf16[512,512]{1,0:T(8,128)(2,1)S(1)} %constant_dynamic-slice_fusion.5), channel_id=1, source_target_pairs={{0,1},{1,3},{3,2},{2,0},{4,5},{5,7},{7,6},{6,4},{8,9},{9,11},{11,1... | collective-permute-start | bytes 1572872 | tf_op jit(solution)/shard_map/ppermute | solution.py:552
  221.4 13.6 %collective-permute-start.19 = (bf16[512,512]{1,0:T(8,128)(2,1)S(1)}, bf16[512,512]{1,0:T(8,128)(2,1)S(1)}, u32[]{:S(2)}, u32[]{:S(2)}) collective-permute-start(bf16[512,512]{1,0:T(8,128)(2,1)S(1)} %add_convert_fusion.16), channel_id=1, source_target_pairs={{0,1},{1,3},{3,2},{2,0},{4,5},{5,7},{7,6},{6,4},{8,9},{9,11},{11,1... | collective-permute-start | bytes 1572872 | tf_op jit(solution)/shard_map/ppermute | solution.py:552
  235.1 15.8 %collective-permute-start.20 = (bf16[512,512]{1,0:T(8,128)(2,1)S(1)}, bf16[512,512]{1,0:T(8,128)(2,1)S(1)}, u32[]{:S(2)}, u32[]{:S(2)}) collective-permute-start(bf16[512,512]{1,0:T(8,128)(2,1)S(1)} %add_convert_fusion.15), channel_id=1, source_target_pairs={{0,1},{1,3},{3,2},{2,0},{4,5},{5,7},{7,6},{6,4},{8,9},{9,11},{11,1... | collective-permute-start | bytes 1572872 | tf_op jit(solution)/shard_map/ppermute | solution.py:552
  251.9 21.4 %collective-permute-start.21 = (bf16[512,512]{1,0:T(8,128)(2,1)}, bf16[512,512]{1,0:T(8,128)(2,1)}, u32[]{:S(2)}, u32[]{:S(2)}) collective-permute-start(bf16[512,512]{1,0:T(8,128)(2,1)} %get-tuple-element.1524), channel_id=1, source_target_pairs={{0,1},{1,3},{3,2},{2,0},{4,5},{5,7},{7,6},{6,4},{8,9},{9,11},{11,1... | collective-permute-start | bytes 1572872 | tf_op jit(solution)/shard_map/ppermute | solution.py:552
  260.5 31.5 %collective-permute-start.22 = (bf16[512,512]{1,0:T(8,128)(2,1)}, bf16[512,512]{1,0:T(8,128)(2,1)}, u32[]{:S(2)}, u32[]{:S(2)}) collective-permute-start(bf16[512,512]{1,0:T(8,128)(2,1)} %constant_dynamic-slice_fusion.4), channel_id=1, source_target_pairs={{0,1},{1,3},{3,2},{2,0},{4,5},{5,7},{7,6},{6,4},{8,9},{9,11},{11,1... | collective-permute-start | bytes 1572872 | tf_op jit(solution)/shard_map/ppermute | solution.py:552
  273.3 165.7 %reduce-scatter.6.cloned.1.call-start = ((), (), s32[]{:S(2)}) async-start(), calls=%async_computation.5 | async-start | bytes 12976128 | tf_op jit(solution)/shard_map/reduce_scatter | solution.py:938
  273.4 35.1 %collective-permute-start.23 = (bf16[512,512]{1,0:T(8,128)(2,1)}, bf16[512,512]{1,0:T(8,128)(2,1)}, u32[]{:S(2)}, u32[]{:S(2)}) collective-permute-start(bf16[512,512]{1,0:T(8,128)(2,1)} %collective-permute-done.21), channel_id=1, source_target_pairs={{0,1},{1,3},{3,2},{2,0},{4,5},{5,7},{7,6},{6,4},{8,9},{9,11},{11,1... | collective-permute-start | bytes 1572872 | tf_op jit(solution)/shard_map/ppermute | solution.py:552
  293.5 20.3 %collective-permute-start.24 = (bf16[512,512]{1,0:T(8,128)(2,1)S(1)}, bf16[512,512]{1,0:T(8,128)(2,1)S(1)}, u32[]{:S(2)}, u32[]{:S(2)}) collective-permute-start(bf16[512,512]{1,0:T(8,128)(2,1)S(1)} %add_convert_fusion.14), channel_id=1, source_target_pairs={{0,1},{1,3},{3,2},{2,0},{4,5},{5,7},{7,6},{6,4},{8,9},{9,11},{11,1... | collective-permute-start | bytes 1572872 | tf_op jit(solution)/shard_map/ppermute | solution.py:552
  308.5 15.2 %collective-permute-start.25 = (bf16[512,512]{1,0:T(8,128)(2,1)}, bf16[512,512]{1,0:T(8,128)(2,1)S(1)}, u32[]{:S(2)}, u32[]{:S(2)}) collective-permute-start(bf16[512,512]{1,0:T(8,128)(2,1)} %collective-permute-done.23), channel_id=1, source_target_pairs={{0,1},{1,3},{3,2},{2,0},{4,5},{5,7},{7,6},{6,4},{8,9},{9,11},{11,1... | collective-permute-start | bytes 1572872 | tf_op jit(solution)/shard_map/ppermute | solution.py:552
  314.7 17.5 %collective-permute-start.26 = (bf16[512,512]{1,0:T(8,128)(2,1)S(1)}, bf16[512,512]{1,0:T(8,128)(2,1)S(1)}, u32[]{:S(2)}, u32[]{:S(2)}) collective-permute-start(bf16[512,512]{1,0:T(8,128)(2,1)S(1)} %add_convert_fusion.13), channel_id=1, source_target_pairs={{0,1},{1,3},{3,2},{2,0},{4,5},{5,7},{7,6},{6,4},{8,9},{9,11},{11,1... | collective-permute-start | bytes 1572872 | tf_op jit(solution)/shard_map/ppermute | solution.py:552
  333.3 13.7 %collective-permute-start.27 = (bf16[512,512]{1,0:T(8,128)(2,1)S(1)}, bf16[512,512]{1,0:T(8,128)(2,1)}, u32[]{:S(2)}, u32[]{:S(2)}) collective-permute-start(bf16[512,512]{1,0:T(8,128)(2,1)S(1)} %get-tuple-element.1681), channel_id=1, source_target_pairs={{0,1},{1,3},{3,2},{2,0},{4,5},{5,7},{7,6},{6,4},{8,9},{9,11},{11,1... | collective-permute-start | bytes 1572872 | tf_op jit(solution)/shard_map/ppermute | solution.py:552
  347.1 181.2 %reduce-scatter.8.cloned.1.call-start = ((), (), s32[]{:S(2)}) async-start(), calls=%async_computation.6 | async-start | bytes 2359296 | tf_op jit(solution)/shard_map/reduce_scatter | solution.py:987
  347.1 13.8 %collective-permute-start.28 = (bf16[512,512]{1,0:T(8,128)(2,1)}, bf16[512,512]{1,0:T(8,128)(2,1)S(1)}, u32[]{:S(2)}, u32[]{:S(2)}) collective-permute-start(bf16[512,512]{1,0:T(8,128)(2,1)} %collective-permute-done.27), channel_id=1, source_target_pairs={{0,1},{1,3},{3,2},{2,0},{4,5},{5,7},{7,6},{6,4},{8,9},{9,11},{11,1... | collective-permute-start | bytes 1572872 | tf_op jit(solution)/shard_map/ppermute | solution.py:552
  372.9 24.7 %collective-permute-start.30 = (bf16[512,512]{1,0:T(8,128)(2,1)}, bf16[512,512]{1,0:T(8,128)(2,1)}, u32[]{:S(2)}, u32[]{:S(2)}) collective-permute-start(bf16[512,512]{1,0:T(8,128)(2,1)} %constant_dynamic-slice_fusion.3), channel_id=1, source_target_pairs={{0,1},{1,3},{3,2},{2,0},{4,5},{5,7},{7,6},{6,4},{8,9},{9,11},{11,1... | collective-permute-start | bytes 1572872 | tf_op jit(solution)/shard_map/ppermute | solution.py:552
  383.3 25.6 %collective-permute-start.31 = (bf16[512,512]{1,0:T(8,128)(2,1)}, bf16[512,512]{1,0:T(8,128)(2,1)S(1)}, u32[]{:S(2)}, u32[]{:S(2)}) collective-permute-start(bf16[512,512]{1,0:T(8,128)(2,1)} %constant_dynamic-slice_fusion.2), channel_id=1, source_target_pairs={{0,1},{1,3},{3,2},{2,0},{4,5},{5,7},{7,6},{6,4},{8,9},{9,11},{11,1... | collective-permute-start | bytes 1572872 | tf_op jit(solution)/shard_map/ppermute | solution.py:552
  421.3 19.9 %collective-permute-start.34 = (bf16[1024,2176]{1,0:T(8,128)(2,1)}, bf16[1024,2176]{1,0:T(8,128)(2,1)}, u32[]{:S(2)}, u32[]{:S(2)}) collective-permute-start(bf16[1024,2176]{1,0:T(8,128)(2,1)} %convolution_convert_fusion.2), channel_id=1, source_target_pairs={{0,4},{4,0},{8,12},{12,8},{16,20},{20,16},{24,28},{28,24},{1,5},{5... | collective-permute-start | bytes 13369352 | tf_op jit(solution)/shard_map/ppermute | solution.py:965
  423.3 15.8 %collective-permute-start.33 = (bf16[512,512]{1,0:T(8,128)(2,1)S(1)}, bf16[512,512]{1,0:T(8,128)(2,1)}, u32[]{:S(2)}, u32[]{:S(2)}) collective-permute-start(bf16[512,512]{1,0:T(8,128)(2,1)S(1)} %add_convert_fusion.11), channel_id=1, source_target_pairs={{0,1},{1,3},{3,2},{2,0},{4,5},{5,7},{7,6},{6,4},{8,9},{9,11},{11,1... | collective-permute-start | bytes 1572872 | tf_op jit(solution)/shard_map/ppermute | solution.py:552
  425.5 24.8 %collective-permute-start.35 = (bf16[512,512]{1,0:T(8,128)(2,1)}, bf16[512,512]{1,0:T(8,128)(2,1)}, u32[]{:S(2)}, u32[]{:S(2)}) collective-permute-start(bf16[512,512]{1,0:T(8,128)(2,1)} %add_convert_fusion.10), channel_id=1, source_target_pairs={{0,1},{1,3},{3,2},{2,0},{4,5},{5,7},{7,6},{6,4},{8,9},{9,11},{11,1... | collective-permute-start | bytes 1572872 | tf_op jit(solution)/shard_map/ppermute | solution.py:552
  441.2 26.5 %collective-permute-start.36 = (bf16[512,512]{1,0:T(8,128)(2,1)}, bf16[512,512]{1,0:T(8,128)(2,1)}, u32[]{:S(2)}, u32[]{:S(2)}) collective-permute-start(bf16[512,512]{1,0:T(8,128)(2,1)} %add_convert_fusion.9), channel_id=1, source_target_pairs={{0,1},{1,3},{3,2},{2,0},{4,5},{5,7},{7,6},{6,4},{8,9},{9,11},{11,1... | collective-permute-start | bytes 1572872 | tf_op jit(solution)/shard_map/ppermute | solution.py:552
  452.1 26.3 %collective-permute-start.37 = (bf16[512,512]{1,0:T(8,128)(2,1)}, bf16[512,512]{1,0:T(8,128)(2,1)}, u32[]{:S(2)}, u32[]{:S(2)}) collective-permute-start(bf16[512,512]{1,0:T(8,128)(2,1)} %constant_dynamic-slice_fusion.1), channel_id=1, source_target_pairs={{0,1},{1,3},{3,2},{2,0},{4,5},{5,7},{7,6},{6,4},{8,9},{9,11},{11,1... | collective-permute-start | bytes 1572872 | tf_op jit(solution)/shard_map/ppermute | solution.py:552
  454.8 39.7 %collective-permute-start.38 = (bf16[512,1024]{1,0:T(8,128)(2,1)}, bf16[512,1024]{1,0:T(8,128)(2,1)}, u32[]{:S(2)}, u32[]{:S(2)}) collective-permute-start(bf16[512,1024]{1,0:T(8,128)(2,1)} %pad_maximum_fusion.10), channel_id=1, source_target_pairs={{0,8},{4,12},{8,0},{12,4},{16,24},{20,28},{24,16},{28,20},{1,9},{5... | collective-permute-start | bytes 3145736 | tf_op jit(solution)/shard_map/ppermute | solution.py:648
  458.6 35.9 %collective-permute-start.39 = (bf16[512,1152]{1,0:T(8,128)(2,1)}, bf16[512,1152]{1,0:T(8,128)(2,1)}, u32[]{:S(2)}, u32[]{:S(2)}) collective-permute-start(bf16[512,1152]{1,0:T(8,128)(2,1)} %pad_maximum_fusion.8), channel_id=1, source_target_pairs={{0,16},{4,20},{8,24},{12,28},{16,0},{20,4},{24,8},{28,12},{1,17},{... | collective-permute-start | bytes 3538952 | tf_op jit(solution)/shard_map/ppermute | solution.py:648
  474.0 15.0 %collective-permute-start.42 = (f32[3200]{0:T(1024)S(1)}, f32[3200]{0:T(1024)S(1)}, u32[]{:S(2)}, u32[]{:S(2)}) collective-permute-start(f32[3200]{0:T(1024)S(1)} %pad_maximum_fusion.12), channel_id=1, source_target_pairs={{0,2},{1,3},{2,0},{3,1},{4,6},{5,7},{6,4},{7,5},{8,10},{9,11},{10,... | collective-permute-start | bytes 38408 | tf_op jit(solution)/shard_map/ppermute | solution.py:677
  478.4 16.1 %collective-permute-start.40 = (bf16[512,512]{1,0:T(8,128)(2,1)S(1)}, bf16[512,512]{1,0:T(8,128)(2,1)}, u32[]{:S(2)}, u32[]{:S(2)}) collective-permute-start(bf16[512,512]{1,0:T(8,128)(2,1)S(1)} %constant_dynamic-slice_fusion), channel_id=1, source_target_pairs={{0,1},{1,3},{3,2},{2,0},{4,5},{5,7},{7,6},{6,4},{8,9},{9,11},{11,1... | collective-permute-start | bytes 1572872 | tf_op jit(solution)/shard_map/ppermute | solution.py:552
  489.0 14.3 %collective-permute-start.44 = (bf16[512,512]{1,0:T(8,128)(2,1)}, bf16[512,512]{1,0:T(8,128)(2,1)}, u32[]{:S(2)}, u32[]{:S(2)}) collective-permute-start(bf16[512,512]{1,0:T(8,128)(2,1)} %add_convert_fusion.7), channel_id=1, source_target_pairs={{0,1},{1,3},{3,2},{2,0},{4,5},{5,7},{7,6},{6,4},{8,9},{9,11},{11,1... | collective-permute-start | bytes 1572872 | tf_op jit(solution)/shard_map/ppermute | solution.py:552
  498.1 16.4 %collective-permute-start.48 = (bf16[512,512]{1,0:T(8,128)(2,1)S(1)}, bf16[512,512]{1,0:T(8,128)(2,1)S(1)}, u32[]{:S(2)}, u32[]{:S(2)}) collective-permute-start(bf16[512,512]{1,0:T(8,128)(2,1)S(1)} %add_convert_fusion.6), channel_id=1, source_target_pairs={{0,1},{1,3},{3,2},{2,0},{4,5},{5,7},{7,6},{6,4},{8,9},{9,11},{11,1... | collective-permute-start | bytes 1572872 | tf_op jit(solution)/shard_map/ppermute | solution.py:552
  498.1 16.3 %collective-permute-start.46 = (bf16[256,1024]{1,0:T(8,128)(2,1)S(1)}, bf16[256,1024]{1,0:T(8,128)(2,1)S(1)}, u32[]{:S(2)}, u32[]{:S(2)}) collective-permute-start(bf16[256,1024]{1,0:T(8,128)(2,1)S(1)} %broadcast_select_fusion.7), channel_id=1, source_target_pairs={{0,16},{4,20},{8,24},{12,28},{16,0},{20,4},{24,8},{28,12},{1,17},{... | collective-permute-start | bytes 1572872 | tf_op jit(solution)/shard_map/ppermute | solution.py:648
  501.7 18.0 %collective-permute-start.47 = (bf16[256,1152]{1,0:T(8,128)(2,1)S(1)}, bf16[256,1152]{1,0:T(8,128)(2,1)S(1)}, u32[]{:S(2)}, u32[]{:S(2)}) collective-permute-start(bf16[256,1152]{1,0:T(8,128)(2,1)S(1)} %broadcast_select_fusion.2), channel_id=1, source_target_pairs={{0,8},{4,12},{8,0},{12,4},{16,24},{20,28},{24,16},{28,20},{1,9},{5... | collective-permute-start | bytes 1769480 | tf_op jit(solution)/shard_map/ppermute | solution.py:648
  505.5 22.8 %collective-permute-start.49 = (bf16[512,512]{1,0:T(8,128)(2,1)}, bf16[512,512]{1,0:T(8,128)(2,1)}, u32[]{:S(2)}, u32[]{:S(2)}) collective-permute-start(bf16[512,512]{1,0:T(8,128)(2,1)} %add_convert_fusion.5), channel_id=1, source_target_pairs={{0,1},{1,3},{3,2},{2,0},{4,5},{5,7},{7,6},{6,4},{8,9},{9,11},{11,1... | collective-permute-start | bytes 1572872 | tf_op jit(solution)/shard_map/ppermute | solution.py:552
  524.2 13.4 %collective-permute-start.52 = (bf16[512,512]{1,0:T(8,128)(2,1)}, bf16[512,512]{1,0:T(8,128)(2,1)}, u32[]{:S(2)}, u32[]{:S(2)}) collective-permute-start(bf16[512,512]{1,0:T(8,128)(2,1)} %add_convert_fusion.3), channel_id=1, source_target_pairs={{0,1},{1,3},{3,2},{2,0},{4,5},{5,7},{7,6},{6,4},{8,9},{9,11},{11,1... | collective-permute-start | bytes 1572872 | tf_op jit(solution)/shard_map/ppermute | solution.py:552
  (110 other events, 1054.2 us)
Sparse Core Ops, SparseCore 0:
  88.4 53.3 all-gather.1
  273.5 58.0 reduce-scatter.3
  347.2 86.8 reduce-scatter.5
  474.2 46.3 reduce-scatter.7
